TPU v7x, 256 devices: a whole 4x4x8 slice. The times are simulated.
256 devices in a mesh: wide: 32 (over y, x, core), narrow: 8 (over z).
Axes of the slice: x: 4, y: 4, z: 8, core: 2. Of those that a mesh axis runs over, the one named last changes fastest.
Arguments:
- leaf_rhs: bfloat16 [131072, 256], P(('wide', 'narrow')), may hold values from -6 to 6
- leaf_inv: bfloat16 [1024, 128, 128], P(('wide', 'narrow')), may hold values from -0.5 to 0.5
- leaf_coupling: bfloat16 [1024, 2, 128, 128], P(('wide', 'narrow')), may hold values from -0.25 to 0.25
- leaf_parent: int32 [1024, 2], P(('wide', 'narrow')), may hold values from 0 to 15, all different within a row
- sep_rhs: bfloat16 [65536, 256], P(('wide', 'narrow')), may hold values from -6 to 6
- sep_inv: bfloat16 [65536, 2048], P(('wide', 'narrow')), may hold values from -0.125 to 0.125
- sep_link: bfloat16 [4096, 128], P('wide'), may hold values from -2 to 2
- row_owner: int32 [32, 8], P('wide'), may hold values from 0 to 7, each once within a row
Outputs:
- leaf_adjoint: float32 [131072, 256], P(('wide', 'narrow'))
- sep_adjoint: float32 [65536, 256], P(('wide', 'narrow'))
Inputs may be any that keep to these rules, and one draw needn't show every extreme that they name: `leaf_parent`: each row names 2 different block rows of the leaf's own separator. `row_owner`: each row is a permutation of the narrow indices.
All inputs are finite; a program needn't handle non-finite values.
Results may differ from a plain program's by a relative error of at most 0.015.
Values may be sent and summed in bfloat16 or wider, within the bound.
No kernel may reach another device: no remote copies, remote signals or barrier semaphores. Data moves between devices by JAX's collectives and lax.ppermute only.
A program may use at most 64 MiB of HBM per device.

v0:
```python
import jax
import jax.numpy as jnp
from jax import lax
from jax.sharding import PartitionSpec as P

highest = lax.Precision.HIGHEST


def spread(block, axis, owner):
    block = jnp.where(lax.axis_index(axis) == owner, block, jnp.zeros_like(block))
    return lax.psum(block, axis)


def passed_along(value, axis, by):
    length = lax.axis_size(axis)
    pairs = [(i, i + by) for i in range(length) if 0 <= i + by < length]
    return lax.ppermute(value, axis, pairs)


def per_device(
    leaf_rhs, leaf_inv, leaf_coupling, leaf_parent, sep_rhs, sep_inv, sep_link, row_owner
):
    block_rows = leaf_inv.shape[1]
    leaf_count = leaf_inv.shape[0]
    sketch = leaf_rhs.shape[1]
    group_rows = sep_inv.shape[0]
    groups = lax.axis_size("narrow")
    chain_len = lax.axis_size("wide")
    blocks_sep = sep_inv.shape[1] // block_rows
    my_index = lax.axis_index("narrow")
    owners = row_owner[0]
    device_ids = jnp.arange(groups, dtype=jnp.int32)
    inverse = jnp.sum(
        device_ids[:, None] * (owners[:, None] == device_ids[None, :]).astype(jnp.int32), axis=0
    )
    my_group = inverse[my_index]
    holds_last = owners[groups - 1] == my_index
    rhs_blocks = leaf_rhs.reshape(leaf_count, block_rows, sketch)
    forward_leaf = jnp.einsum(
        "iab,ibk->iak", leaf_inv, rhs_blocks, preferred_element_type=jnp.float32
    ).astype(jnp.bfloat16)
    pushed = jnp.einsum(
        "icab,ibk->icak", leaf_coupling, forward_leaf, preferred_element_type=jnp.float32
    )
    selector = (
        leaf_parent[:, :, None] == jnp.arange(blocks_sep, dtype=jnp.int32)[None, None, :]
    ).astype(jnp.float32)
    gathered_push = jnp.einsum("icn,icak->nak", selector, pushed, precision=highest)
    empty_rows = jnp.zeros((blocks_sep * block_rows, sketch), jnp.float32)
    placed = lax.dynamic_update_slice_in_dim(
        empty_rows, sep_rhs.astype(jnp.float32), my_group * group_rows, 0
    )
    local_part = placed - gathered_push.reshape(blocks_sep * block_rows, sketch)
    coupled = lax.psum(local_part, "narrow").astype(jnp.bfloat16)
    applied = jnp.dot(sep_inv, coupled, preferred_element_type=jnp.float32)
    head_cols = sep_inv[:, :block_rows].astype(jnp.float32)
    link_matrix = sep_link.astype(jnp.float32)
    tail_rows = head_cols[group_rows - block_rows :]
    last_map = jnp.dot(tail_rows, link_matrix, precision=highest)
    packed = jnp.concatenate([last_map, applied[group_rows - block_rows :]], axis=1)
    root_index = owners[groups - 1]
    shared = spread(packed, "narrow", root_index)
    step_map = -shared[:, :block_rows]
    step_add = shared[:, block_rows:]
    zero_state = jnp.zeros((block_rows, sketch), jnp.float32)

    def forward_turn(turn_index, chain_state):
        outgoing = chain_state[0]
        received = passed_along(outgoing, "wide", 1)
        outgoing = step_add + jnp.dot(step_map, received, precision=highest)
        return (outgoing, received)

    final_state = lax.fori_loop(0, chain_len, forward_turn, (zero_state, zero_state))
    before = final_state[1]
    correction = jnp.dot(
        head_cols, jnp.dot(link_matrix, before, precision=highest), precision=highest
    )
    forward_bf = (applied - correction).astype(jnp.bfloat16)
    head_part = jnp.einsum(
        "ab,ak->bk", sep_inv[:, :block_rows], forward_bf, preferred_element_type=jnp.float32
    )
    tail_mask = jnp.where(holds_last, tail_rows, 0.0)
    first_cols, tail_block = (
        lax.psum(head_part.astype(jnp.bfloat16), "narrow").astype(jnp.float32),
        lax.psum(tail_mask.astype(jnp.bfloat16), "narrow").astype(jnp.float32),
    )
    back_map = -jnp.dot(link_matrix.T, tail_block.T, precision=highest)
    back_add = jnp.dot(link_matrix.T, first_cols, precision=highest)

    def backward_turn(turn_index, chain_state):
        outgoing = chain_state[0]
        received = passed_along(outgoing, "wide", -1)
        outgoing = back_add + jnp.dot(back_map, received, precision=highest)
        return (outgoing, received)

    final_back = lax.fori_loop(0, chain_len, backward_turn, (zero_state, zero_state))
    from_above = final_back[1]
    last_fix = jnp.where(holds_last, from_above, 0.0)
    tail_fix = jnp.pad(last_fix, ((group_rows - block_rows, 0), (0, 0)))
    adjusted = (forward_bf.astype(jnp.float32) - tail_fix).astype(jnp.bfloat16)
    column_groups = sep_inv.reshape(group_rows, groups, group_rows)
    picked = jnp.take(column_groups, inverse, axis=1)
    term_block = jnp.einsum("aqb,ak->qbk", picked, adjusted, preferred_element_type=jnp.float32)
    adjoint_sep = lax.psum_scatter(
        term_block.reshape(group_rows * lax.axis_size("narrow"), sketch),
        "narrow",
        scatter_dimension=0,
        tiled=True,
    )
    sep_bf = adjoint_sep.astype(jnp.bfloat16)
    all_groups = lax.all_gather(sep_bf, "narrow", axis=0, tiled=True)
    natural = jnp.take(all_groups.reshape(groups, group_rows, sketch), owners, axis=0).reshape(
        blocks_sep, block_rows, sketch
    )
    chosen = jnp.take(natural, leaf_parent, axis=0)
    pulled_back = jnp.einsum(
        "icab,icak->ibk", leaf_coupling, chosen, preferred_element_type=jnp.float32
    )
    leaf_middle = (forward_leaf.astype(jnp.float32) - pulled_back).astype(jnp.bfloat16)
    adjoint_leaf = jnp.einsum(
        "iab,iak->ibk", leaf_inv, leaf_middle, preferred_element_type=jnp.float32
    )
    return (adjoint_leaf.reshape(leaf_count * block_rows, sketch), adjoint_sep)


def solution(mesh):
    placed = (
        P(("wide", "narrow"), None),
        P(("wide", "narrow"), None, None),
        P(("wide", "narrow"), None, None, None),
        P(("wide", "narrow"), None),
        P(("wide", "narrow"), None),
        P(("wide", "narrow"), None),
        P("wide", None),
        P("wide", None),
    )
    return jax.shard_map(
        per_device,
        mesh=mesh,
        in_specs=placed,
        out_specs=(P(("wide", "narrow"), None), P(("wide", "narrow"), None)),
        check_vma=False,
    )
```

profile of v0, /device:TPU:1, one launch (start us, length us, event | category | flops | bytes accessed | tf_op | source)
XLA Modules:
  0.0 938.9 jit_solution(18356873346091859647)
XLA Ops:
  18.6 61.0 %all-reduce.8 = bf16[2048,256]{1,0:T(8,128)(2,1)S(1)} all-reduce(f32[2048,256]{1,0:T(8,128)} %bitcast_subtract_fusion), channel_id=1, replica_groups=mesh['wide'=32,'narrow'=8] {'narrow'}, use_global_device_ids=true, to_apply=%region_1.0 | all-reduce | flops 524288 | bytes 3145728 | tf_op jit(solution)/shard_map/psum | solution.py:54
  83.6 21.7 %psum.30 = bf16[128,128]{1,0:T(8,128)(2,1)S(1)} all-reduce(bf16[128,128]{1,0:T(8,128)(2,1)S(1)} %select_convert_fusion), channel_id=1, replica_groups=mesh['wide'=32,'narrow'=8] {'narrow'}, use_global_device_ids=true, to_apply=%region_5.6 | all-reduce | flops 16384 | bytes 65536 | tf_op jit(solution)/shard_map/psum | solution.py:85
  106.7 51.1 %all-reduce.5.cloned.1.call-done = f32[128,384]{0,1:T(8,128)} async-done(((f32[128,384]{0,1:T(8,128)}), f32[128,384]{0,1:T(8,128)}) %all-reduce.5.cloned.1.call-update) | async-done | bytes 196624 | tf_op jit(solution)/shard_map/psum | solution.py:11
  160.5 302.4 %while.26 = (s32[]{:T(128)}, f32[128,256]{1,0:T(8,128)}, f32[128,256]{1,0:T(8,128)}, f32[128,128]{1,0:T(8,128)S(1)}, f32[128,256]{1,0:T(8,128)S(1)}, /*index=5*/s32[]{:T(128)}, s32[]{:T(128)}) while((s32[]{:T(128)}, f32[128,256]{1,0:T(8,128)}, f32[128,256]{1,0:T(8,128)}, f32[128,128]{1,0:T(8,128)S(1)}, f32[128,256]{1,0:T(8,128)S(1)}, ...), condition=%wide.region_4.5_spmd.clone, body=%wide.region_3.4_spmd.clone.sunk | while | flops 50397184 | bytes 1769627 | solution.py:73
  160.5 8.2 collective-permute-start
  269.8 6.0 collective-permute-start
  279.6 6.5 collective-permute-start
  289.9 6.5 collective-permute-start
  300.1 6.5 collective-permute-start
  310.3 6.5 collective-permute-start
  320.6 6.5 collective-permute-start
  330.8 6.5 collective-permute-start
  341.0 6.5 collective-permute-start
  351.3 6.5 collective-permute-start
  361.5 6.5 collective-permute-start
  371.7 6.5 collective-permute-start
  382.0 6.5 collective-permute-start
  392.2 6.5 collective-permute-start
  402.4 6.5 collective-permute-start
  412.7 6.5 collective-permute-start
  422.9 6.5 collective-permute-start
  433.1 6.5 collective-permute-start
  443.3 6.5 collective-permute-start
  453.6 6.5 collective-permute-start
  465.9 90.5 %all-reduce.7.cloned.1.call-done = bf16[128,256]{0,1:T(8,128)(2,1)} async-done(((bf16[128,256]{0,1:T(8,128)(2,1)}), bf16[128,256]{0,1:T(8,128)(2,1)}) %all-reduce.7.cloned.1.call-update) | async-done | bytes 65552 | tf_op jit(solution)/shard_map/psum | solution.py:84
  558.2 268.9 %while.27 = (s32[]{:T(128)}, f32[128,256]{1,0:T(8,128)S(1)}, f32[128,256]{1,0:T(8,128)}, f32[128,128]{1,0:T(8,128)S(1)}, f32[128,256]{1,0:T(8,128)S(1)}, /*index=5*/s32[]{:T(128)}, s32[]{:T(128)}) while((s32[]{:T(128)}, f32[128,256]{1,0:T(8,128)S(1)}, f32[128,256]{1,0:T(8,128)}, f32[128,128]{1,0:T(8,128)S(1)}, ...), condition=%wide.region_8.9_spmd.clone, body=%wide.region_7.8_spmd.clone.sunk | while | flops 50397184 | bytes 1769627 | solution.py:96
  558.2 7.5 collective-permute-start.1
  656.8 6.5 collective-permute-done.1
  665.8 6.5 collective-permute-done.1
  674.9 6.5 collective-permute-done.1
  684.0 6.5 collective-permute-done.1
  693.0 6.5 collective-permute-done.1
  702.1 6.5 collective-permute-done.1
  711.2 6.5 collective-permute-done.1
  720.2 6.5 collective-permute-done.1
  729.3 6.5 collective-permute-done.1
  738.4 6.5 collective-permute-done.1
  747.5 6.5 collective-permute-done.1
  756.5 6.5 collective-permute-done.1
  765.6 6.5 collective-permute-done.1
  774.7 6.5 collective-permute-done.1
  783.7 6.5 collective-permute-done.1
  792.8 6.5 collective-permute-done.1
  801.9 6.5 collective-permute-done.1
  810.9 6.5 collective-permute-done.1
  820.0 6.5 collective-permute-done.1
  830.2 59.6 %reduce-scatter.2.cloned.1.call-done = f32[256,256]{1,0:T(8,128)} async-done(((f32[2048,256]{1,0:T(8,128)}), f32[256,256]{1,0:T(8,128)}) %reduce-scatter.2.cloned.1.call-update) | async-done | bytes 262160 | tf_op jit(solution)/shard_map/reduce_scatter | solution.py:104
  891.9 36.2 %all-gather.2.cloned.1.call-done = bf16[2048,256]{1,0:T(8,128)(2,1)} async-done(((bf16[256,256]{1,0:T(8,128)(2,1)}), bf16[2048,256]{1,0:T(8,128)(2,1)}) %all-gather.2.cloned.1.call-update) | async-done | bytes 1048592 | tf_op jit(solution)/shard_map/all_gather | solution.py:111
  (437 shorter events, 340.9 us)
Async XLA Ops:
  7.2 150.6 %all-reduce.5.cloned.1.call-start = ((), (), s32[]{:S(2)}) async-start(), calls=%async_computation.1 | async-start | bytes 393216 | tf_op jit(solution)/shard_map/psum | solution.py:11
  82.3 474.1 %all-reduce.7.cloned.1.call-start = ((), (), s32[]{:S(2)}) async-start(), calls=%async_computation.2 | async-start | bytes 131072 | tf_op jit(solution)/shard_map/psum | solution.py:84
  160.5 10.1 %collective-permute-start = (f32[128,256]{1,0:T(8,128)S(1)}, f32[128,256]{1,0:T(8,128)S(1)}, u32[]{:S(2)}, u32[]{:S(2)}) collective-permute-start(f32[128,256]{1,0:T(8,128)S(1)} %broadcast_select_fusion.6), channel_id=1, source_target_pairs={{0,8},{8,16},{16,24},{24,32},{32,40},{40,48},{48,56},{56,64},{64,7... | collective-permute-start | bytes 393224 | tf_op jit(solution)/shard_map/while/body/eval_jaxpr/ppermute | solution.py:17
  269.8 8.0 collective-permute-start
  279.6 8.4 collective-permute-start
  289.9 8.4 collective-permute-start
  300.1 8.4 collective-permute-start
  310.3 8.4 collective-permute-start
  320.6 8.4 collective-permute-start
  330.8 8.4 collective-permute-start
  341.0 8.4 collective-permute-start
  351.3 8.4 collective-permute-start
  361.5 8.4 collective-permute-start
  371.7 8.4 collective-permute-start
  382.0 8.4 collective-permute-start
  392.2 8.4 collective-permute-start
  402.4 8.4 collective-permute-start
  412.7 8.4 collective-permute-start
  422.9 8.4 collective-permute-start
  433.1 8.4 collective-permute-start
  443.3 8.4 collective-permute-start
  453.6 8.4 collective-permute-start
  465.2 424.5 %reduce-scatter.2.cloned.1.call-start = ((), (), s32[]{:S(2)}) async-start(), calls=%async_computation.3 | async-start | bytes 2359296 | tf_op jit(solution)/shard_map/reduce_scatter | solution.py:104
  558.2 11.2 %collective-permute-start.1 = (f32[128,256]{1,0:T(8,128)S(1)}, f32[128,256]{1,0:T(8,128)S(1)}, u32[]{:S(2)}, u32[]{:S(2)}) collective-permute-start(f32[128,256]{1,0:T(8,128)S(1)} %broadcast_select_fusion.7), channel_id=1, source_target_pairs={{8,0},{16,8},{24,16},{32,24},{40,32},{48,40},{56,48},{64,56},{72,6... | collective-permute-start | bytes 393224 | tf_op jit(solution)/shard_map/while/body/eval_jaxpr/ppermute | solution.py:17
  570.1 6.3 collective-permute-start.1
  577.0 6.3 collective-permute-start.1
  584.0 6.3 collective-permute-start.1
  646.6 7.6 collective-permute-start.1
  654.8 8.4 collective-permute-start.1
  663.9 8.4 collective-permute-start.1
  673.0 8.4 collective-permute-start.1
  682.1 8.4 collective-permute-start.1
  691.1 8.4 collective-permute-start.1
  700.2 8.4 collective-permute-start.1
  709.3 8.4 collective-permute-start.1
  718.3 8.4 collective-permute-start.1
  727.4 8.4 collective-permute-start.1
  736.5 8.4 collective-permute-start.1
  745.5 8.4 collective-permute-start.1
  754.6 8.4 collective-permute-start.1
  763.7 8.4 collective-permute-start.1
  772.7 8.4 collective-permute-start.1
  781.8 8.4 collective-permute-start.1
  790.9 8.4 collective-permute-start.1
  799.9 8.4 collective-permute-start.1
  809.0 8.4 collective-permute-start.1
  818.1 8.4 collective-permute-start.1
  830.2 98.0 %all-gather.2.cloned.1.call-start = ((), (), s32[]{:S(2)}) async-start(), calls=%async_computation.4 | async-start | bytes 1179648 | tf_op jit(solution)/shard_map/all_gather | solution.py:111
  (98 other events, 1040.8 us)
Sparse Core Ops, SparseCore 0:
  82.5 75.2 all-reduce.4
  465.4 91.0 all-reduce.6
  830.3 59.4 reduce-scatter.1
  891.5 36.5 all-gather.1
where the time goes:
time: 946 us; the launch traced here: 939 us
  waiting for transfers between devices  479 us (51%)
  starting transfers between devices  250 us (26%)
  blocking collectives  82.7 us (9%)
  matrix products  47.8 us (5%)
  other arithmetic  34.7 us (4%)
  local copies, waits for them, and re-layouts  27.5 us (3%)
  between operations  16 us (2%)
    ppermute x64, starting transfers between devices, passed_along(): return lax.ppermute(value, axis, pairs)  250 us
    ppermute x64, waiting for transfers between devices, passed_along(): return lax.ppermute(value, axis, pairs)  242 us
    psum x1, waiting for transfers between devices, per_device(): lax.psum(head_part.astype(jnp.bfloat16), 'narrow').astype(jnp.float32)  90.5 us
    psum x1, blocking collectives, per_device(): coupled = lax.psum(local_part, 'narrow').astype(jnp.bfloat16)  61 us
    reduce_scatter x1, waiting for transfers between devices, per_device(): lax.psum_scatter(term_block.reshape(group_rows * lax.axis_size('narrow'),...  59.6 us
    psum x1, waiting for transfers between devices, spread(): return lax.psum(block, axis)  51.1 us
    all_gather x1, waiting for transfers between devices, per_device(): all_groups = lax.all_gather(sep_bf, 'narrow', axis=0, tiled=True)  36.2 us
    dot_general x32, matrix products, forward_turn(): outgoing = step_add + jnp.dot(step_map, received, precision=highest)  29.2 us
  transfers between devices with their start and end apart: 68, of which 68 were waited for; matrix products, arithmetic and copies ran while one was open for 0% of the time, Pallas kernels for 0%

commit v1 on v0

v1 whole, which is shorter than its diff:
```python
import jax
import jax.numpy as jnp
from jax import lax
from jax.experimental import pallas as pl
from jax.experimental.pallas import tpu as pltpu
from jax.sharding import PartitionSpec as P

BF = jnp.bfloat16
F32 = jnp.float32
VMEM = pl.BlockSpec(memory_space=pltpu.VMEM)
SMEM = pl.BlockSpec(memory_space=pltpu.SMEM)
LIMIT = 56 * 1024 * 1024

NN = (((1,), (0,)), ((), ()))
NT = (((1,), (1,)), ((), ()))
TN = (((0,), (0,)), ((), ()))


def mm(a, b, dims):
    return lax.dot_general(a, b, dims, preferred_element_type=F32)


def halves(v):
    hi = v.astype(BF)
    return hi, (v - hi.astype(F32)).astype(BF)


def mm3(a, b, dims):
    ah, al = halves(a)
    bh, bl = halves(b)
    return mm(ah, bh, dims) + (mm(al, bh, dims) + mm(ah, bl, dims))


def mm2(a, b_exact, dims):
    ah = a.astype(BF)
    rest = a - ah.astype(F32)
    al = rest.astype(BF)
    ax = (rest - al.astype(F32)).astype(BF)
    return mm(ah, b_exact, dims) + (mm(al, b_exact, dims) + mm(ax, b_exact, dims))


def call(kernel, name, outs, n_smem, n_vmem, scratch=(), flops=0, moved=0):
    return pl.pallas_call(
        kernel,
        name=name,
        out_shape=outs,
        in_specs=[SMEM] * n_smem + [VMEM] * n_vmem,
        out_specs=jax.tree.map(lambda _: VMEM, outs),
        scratch_shapes=list(scratch),
        compiler_params=pltpu.CompilerParams(vmem_limit_bytes=LIMIT),
        cost_estimate=pl.CostEstimate(flops=flops, bytes_accessed=moved, transcendentals=0),
    )


def leaf_forward_kernel(parent, group, rhs, inv, cpl, sep_rhs, fl, local, acc):
    b = inv.shape[1]
    rows = sep_rhs.shape[0]
    acc[...] = jnp.zeros_like(acc)
    start = pl.multiple_of(group[0] * rows, rows)
    acc[pl.ds(start, rows), :] = sep_rhs[...].astype(F32)
    for i in range(inv.shape[0]):
        f = mm(inv[i], rhs[i * b : (i + 1) * b, :], NN).astype(BF)
        fl[i * b : (i + 1) * b, :] = f
        for k in range(cpl.shape[1]):
            at = pl.ds(pl.multiple_of(parent[i, k] * b, b), b)
            acc[at, :] -= mm(cpl[i, k], f, NN)
    local[...] = acc[...].astype(BF)


def sum_spread_kernel(parts, spread):
    total = parts[0].astype(F32)
    for j in range(1, parts.shape[0]):
        total += parts[j].astype(F32)
    total = total.astype(BF)
    for j in range(parts.shape[0]):
        spread[j] = total


def sum_keep_spread_kernel(parts, kept, spread):
    total = parts[0].astype(F32)
    for j in range(1, parts.shape[0]):
        total += parts[j].astype(F32)
    kept[...] = total
    total = total.astype(BF)
    for j in range(parts.shape[0]):
        spread[j] = total


def middle_kernel(owners, last, inv, coupled, ag, terms):
    rows = inv.shape[0]
    b = rows // 2
    applied = mm(inv[...], coupled[...], NN)
    app = applied.astype(BF)
    ag[:, :b] = jnp.where(last[0] == 1, applied[rows - b :, :].T, 0.0)
    ag[:, b:] = mm(app, inv[:, :b], TN)
    for g in range(terms.shape[0]):
        terms[owners[g]] = mm(inv[:, g * rows : (g + 1) * rows], app, TN).astype(BF)


def small_sum_kernel(parts, link, spread):
    b = link.shape[0]
    total = parts[0]
    for j in range(1, parts.shape[0]):
        total += parts[j]
    moved = mm2(total[:, b:], link[...], NN)
    for j in range(spread.shape[0]):
        spread[j, :, :b] = total[:, :b]
        spread[j, :, b:] = moved


def maps_kernel(x, link, out):
    b = link.shape[0]
    corner = x[:, :b]
    tail = x[:, b:].astype(BF)
    out[:b, :] = mm(link[...], tail, (((0,), (1,)), ((), ())))
    out[b : 2 * b, :] = mm(tail, link[...], NN)
    inner = mm2(corner, link[...], NN)
    out[2 * b :, :] = mm2(inner, link[...], TN)


def chain_kernel(core, me, ag_own, ag_other, maps, link, out, ag, states, incoming):
    b = link.shape[0]
    length = maps.shape[0]
    here = core[0]
    pairs = length // 2
    ag[here] = ag_own[...]
    ag[1 - here] = ag_other[...]
    state = jnp.zeros((ag_own.shape[1], b), F32)
    for w in range(length):
        states[w] = state
        if w + 1 < length:
            state = ag[w % 2, w // 2, :, :b] - mm3(state, maps[w, :b, :], NN)
    back = jnp.zeros_like(state)
    for w in range(length - 1, -1, -1):
        incoming[w] = back
        if w > 0:
            local = ag[w % 2, w // 2, :, b:] - mm3(states[w], maps[w, 2 * b :, :], NN)
            back = local - mm3(back, maps[w, b : 2 * b, :], NN)
    mine = mm2(states[me[0]], link[...], NT)
    for j in range(out.shape[0]):
        out[j, :, :b] = mine
        out[j, :, b:] = incoming[me[0]]


def final_kernel(
    parent, owners, group, kept, gathered, shared, z, cpl, inv, fl, leaf_out, sep_out, zs
):
    b = inv.shape[1]
    rows = kept.shape[0]
    zh, zl = halves(z[...])
    zs[0] = zh
    zs[1] = zl

    def fix(start, count):
        part = shared[pl.ds(start, count), :]
        ph, pw = halves(part)
        return mm(ph, zs[0], NT) + (mm(pw, zs[0], NT) + mm(ph, zs[1], NT))

    at = pl.multiple_of(group[0] * rows, rows)
    sep_out[...] = kept[...] - fix(at, rows)
    for i in range(inv.shape[0]):
        acc = fl[i * b : (i + 1) * b, :].astype(F32)
        for k in range(cpl.shape[1]):
            p = parent[i, k]
            half = lax.rem(p, 2)
            stored = pl.multiple_of(owners[lax.div(p, 2)] * rows + half * b, b)
            block = gathered[pl.ds(stored, b), :].astype(F32)
            block = (block - fix(pl.multiple_of(p * b, b), b)).astype(BF)
            acc -= mm(cpl[i, k], block, TN)
        leaf_out[i * b : (i + 1) * b, :] = mm(inv[i], acc.astype(BF), TN)


def swap(value, axis, by):
    n = lax.axis_size(axis)
    return lax.ppermute(value, axis, [(i, i ^ by) for i in range(n)])


def per_device(
    leaf_rhs, leaf_inv, leaf_coupling, leaf_parent, sep_rhs, sep_inv, sep_link, row_owner
):
    b = leaf_inv.shape[1]
    leaf_count = leaf_inv.shape[0]
    sketch = leaf_rhs.shape[1]
    rows = sep_inv.shape[0]
    n = lax.axis_size("narrow")
    chain_len = lax.axis_size("wide")
    all_rows = sep_inv.shape[1]
    cols = sketch // n
    narrow = lax.axis_index("narrow")
    wide = lax.axis_index("wide")
    owners = row_owner[0]
    ids = jnp.arange(n, dtype=jnp.int32)
    group = jnp.sum(jnp.where(owners == narrow, ids, 0)).reshape(1)
    last = (owners[n - 1] == narrow).astype(jnp.int32).reshape(1)
    is_last = last[0] == 1
    shape = jax.ShapeDtypeStruct

    head = sep_inv[:, :b]
    corner = mm(head, head, TN)
    tail = jnp.where(is_last, head[rows - b :], jnp.zeros((), BF)).astype(F32)
    x = jnp.concatenate([corner, tail], axis=1)
    for by in (1, 2, 4):
        x = x + swap(x, "narrow", by)
    maps = call(maps_kernel, "maps", shape((3 * b, b), F32), 0, 2, flops=2 * 9 * b**3)(x, sep_link)
    maps = lax.all_gather(maps, "wide", axis=0, tiled=False)
    rows_at = lax.broadcasted_iota(jnp.int32, (rows, b), 0)
    cols_at = lax.broadcasted_iota(jnp.int32, (rows, b), 1)
    pick = jnp.where(is_last & (rows_at == cols_at + (rows - b)), 1.0, 0.0).astype(BF)
    shared = lax.psum(mm(sep_inv, jnp.concatenate([head, pick], axis=1), TN), "narrow")

    fl, local = call(
        leaf_forward_kernel,
        "leaf_forward",
        (shape((leaf_count * b, sketch), BF), shape((all_rows, sketch), BF)),
        2,
        4,
        [pltpu.VMEM((all_rows, sketch), F32)],
        flops=2 * 12 * b * b * sketch,
        moved=4 << 20,
    )(leaf_parent, group, leaf_rhs, leaf_inv, leaf_coupling, sep_rhs)
    parts = lax.all_to_all(local.reshape(n, rows, sketch), "narrow", 0, 0, tiled=True)
    spread = call(
        sum_spread_kernel, "sum_spread", shape((n, rows, sketch), BF), 0, 1, moved=2 << 20
    )(parts)
    coupled = lax.all_to_all(spread, "narrow", 0, 0, tiled=True).reshape(all_rows, sketch)
    ag, terms = call(
        middle_kernel,
        "middle",
        (shape((sketch, 2 * b), F32), shape((n, rows, sketch), BF)),
        2,
        2,
        flops=4 * rows * all_rows * sketch,
        moved=4 << 20,
    )(owners, last, sep_inv, coupled)

    ag = lax.all_to_all(ag.reshape(n, cols, 2 * b), "narrow", 0, 0, tiled=True)
    quad = 4
    ag = call(
        small_sum_kernel, "small_sum", shape((quad, cols, 2 * b), F32), 0, 2, moved=1 << 19
    )(ag, sep_link)
    x_groups = [[y * 8 + i * 2 + c for i in range(4)] for y in range(4) for c in range(2)]
    y_groups = [[i * 8 + xx * 2 + c for i in range(4)] for xx in range(4) for c in range(2)]
    ag = lax.all_to_all(ag, "wide", 0, 0, tiled=True, axis_index_groups=x_groups)
    ag = jnp.broadcast_to(ag[None], (quad,) + ag.shape)
    ag = lax.all_to_all(ag, "wide", 0, 0, tiled=True, axis_index_groups=y_groups)
    ag = ag.reshape(quad * quad, cols, 2 * b)
    other = swap(ag, "wide", 1)
    core = lax.rem(wide, 2).astype(jnp.int32).reshape(1)
    z = call(
        chain_kernel,
        "chain",
        shape((n, cols, 2 * b), F32),
        2,
        4,
        [
            pltpu.VMEM((2, chain_len // 2, cols, 2 * b), F32),
            pltpu.VMEM((chain_len, cols, b), F32),
            pltpu.VMEM((chain_len, cols, b), F32),
        ],
        flops=2 * 9 * chain_len * cols * b * b * 40,
        moved=8 << 20,
    )(core, wide.astype(jnp.int32).reshape(1), ag, other, maps, sep_link)
    z = lax.all_to_all(z, "narrow", 0, 0, tiled=True).reshape(sketch, 2 * b)

    terms = lax.all_to_all(terms, "narrow", 0, 0, tiled=True)
    kept, spread = call(
        sum_keep_spread_kernel,
        "sum_keep_spread",
        (shape((rows, sketch), F32), shape((n, rows, sketch), BF)),
        0,
        1,
        moved=2 << 20,
    )(terms)
    gathered = lax.all_to_all(spread, "narrow", 0, 0, tiled=True).reshape(all_rows, sketch)

    leaf_out, sep_out = call(
        final_kernel,
        "final",
        (shape((leaf_count * b, sketch), F32), shape((rows, sketch), F32)),
        3,
        7,
        [pltpu.VMEM((2, sketch, 2 * b), BF)],
        flops=2 * 40 * b * b * sketch,
        moved=6 << 20,
    )(leaf_parent, owners, group, kept, gathered, shared, z, leaf_coupling, leaf_inv, fl)
    return leaf_out, sep_out


def solution(mesh):
    both = ("wide", "narrow")
    placed = (
        P(both, None),
        P(both, None, None),
        P(both, None, None, None),
        P(both, None),
        P(both, None),
        P(both, None),
        P("wide", None),
        P("wide", None),
    )
    return jax.shard_map(
        per_device,
        mesh=mesh,
        in_specs=placed,
        out_specs=(P(both, None), P(both, None)),
        check_vma=False,
    )
```

time: 946 us -> 288 us (0.30)
  waiting for transfers between devices: 479 us -> 90.4 us
  starting transfers between devices: 250 us -> 35.7 us
  matrix products: 47.8 us -> 3.06 us
  Pallas kernels: 0 us -> 36.9 us
  other arithmetic: 34.7 us -> 2.22 us
  local copies, waits for them, and re-layouts: 27.5 us -> 4.4 us
  blocking collectives: 82.7 us -> 94.7 us
    ppermute x64 -> x4, waiting for transfers between devices: 242 us -> 10.9 us  [swap(): return lax.ppermute(value, axis, [(i, i ^ by) for i in range(n)])]
    ppermute x64 -> x4, starting transfers between devices: 250 us -> 22.3 us  [swap(): return lax.ppermute(value, axis, [(i, i ^ by) for i in range(n)])]
    all_to_all x0 -> x5, blocking collectives: none -> 94.7 us  [the longest x1 33.1 us: per_device(): lax.all_to_all(local.reshape(n, rows, sketch), 'narrow', 0, 0, tiled=True)]
    psum x2 -> x0, blocking collectives: 82.7 us -> none  [the longest x1 61 us: per_device(): coupled = lax.psum(local_part, 'narrow').astype(jnp.bfloat16)]
    psum x2 -> x1, waiting for transfers between devices: 142 us -> 69.7 us  [per_device(): lax.psum(mm(sep_inv, jnp.concatenate([head, pick], axis=1), TN), 'narrow')]
    reduce_scatter x1 -> x0, waiting for transfers between devices: 59.6 us -> none  [per_device(): lax.psum_scatter(term_block.reshape(group_rows * lax.axis_size('narrow'),...]
    dot_general x76 -> x2, matrix products: 47.8 us -> 3.06 us  [mm(): return lax.dot_general(a, b, dims, preferred_element_type=F32)]
    pallas_call x0 -> x8, Pallas kernels: none -> 36.9 us  [the longest x1 13.2 us: per_device(): call(chain_kernel, 'chain', shape((n, cols, 2 * b), F32), 2, 4, [pltpu.VM...]
  transfers between devices with their start and end apart: 68 -> 9, of which waited for: 68 -> 6; matrix products, arithmetic and copies ran while one was open for 0% -> 1% of each run, Pallas kernels for 0% -> 10%
where the time goes in v1:
time: 288 us; the launch traced here: 284 us
  blocking collectives  94.7 us (33%)
  waiting for transfers between devices  90.4 us (31%)
  Pallas kernels  36.9 us (13%)
  starting transfers between devices  35.7 us (12%)
  between operations  16.3 us (6%)
  local copies, waits for them, and re-layouts  4.4 us (2%)
  matrix products  3.06 us (1%)
    psum x1, waiting for transfers between devices, per_device(): lax.psum(mm(sep_inv, jnp.concatenate([head, pick], axis=1), TN), 'narrow')  69.7 us
    all_to_all x1, blocking collectives, per_device(): lax.all_to_all(local.reshape(n, rows, sketch), 'narrow', 0, 0, tiled=True)  33.1 us
    all_to_all x1, blocking collectives, per_device(): lax.all_to_all(spread, 'narrow', 0, 0, tiled=True).reshape(all_rows, sketch)  28.5 us
    ppermute x4, starting transfers between devices, swap(): return lax.ppermute(value, axis, [(i, i ^ by) for i in range(n)])  22.3 us
    all_to_all x1, blocking collectives, per_device(): ag = lax.all_to_all(ag.reshape(n, cols, 2 * b), 'narrow', 0, 0, tiled=True)  13.3 us
    pallas_call x1, Pallas kernels, per_device(): call(chain_kernel, 'chain', shape((n, cols, 2 * b), F32), 2, 4, [pltpu.VM...  13.2 us
    all_to_all x1, blocking collectives, per_device(): lax.all_to_all(ag, 'wide', 0, 0, tiled=True, axis_index_groups=y_groups)  11 us
    ppermute x4, waiting for transfers between devices, swap(): return lax.ppermute(value, axis, [(i, i ^ by) for i in range(n)])  10.9 us
  transfers between devices with their start and end apart: 9, of which 6 were waited for; matrix products, arithmetic and copies ran while one was open for 1% of the time, Pallas kernels for 10%

profile of v1, /device:TPU:1, one launch (start us, length us, event | category | flops | bytes accessed | tf_op | source)
XLA Modules:
  0.0 283.7 jit_solution(14489379777651144187)
XLA Ops:
  8.0 0.0 copy-start.5
  8.0 0.0 all-gather.3.cloned.1.call-start
  8.1 1.2 slice.11
  10.0 1.1 fusion.6
  11.1 0.8 select_convert_fusion.1
  11.9 2.5 collective-permute-start.1
  14.4 2.4 collective-permute-done.1
  16.8 3.8 %collective-permute-start.2 = (f32[128,256]{1,0:T(8,128)S(1)}, f32[128,256]{1,0:T(8,128)S(1)}, u32[]{:S(2)}, u32[]{:S(2)}) collective-permute-start(f32[128,256]{1,0:T(8,128)S(1)} %fusion.8), channel_id=1, source_target_pairs={{0,2},{1,3},{2,0},{3,1},{4,6},{5,7},{6,4},{7,5},{8,10},{9,11},{10,... | collective-permute-start | bytes 393224 | tf_op jit(solution)/shard_map/ppermute | solution.py:175
  20.6 5.7 %collective-permute-done.2 = f32[128,256]{1,0:T(8,128)S(1)} collective-permute-done((f32[128,256]{1,0:T(8,128)S(1)}, f32[128,256]{1,0:T(8,128)S(1)}, u32[]{:S(2)}, u32[]{:S(2)}) %collective-permute-start.2) | collective-permute-done | bytes 131104 | tf_op jit(solution)/shard_map/ppermute | solution.py:175
  26.4 6.5 %collective-permute-start.3 = (f32[128,256]{1,0:T(8,128)S(1)}, f32[128,256]{1,0:T(8,128)S(1)}, u32[]{:S(2)}, u32[]{:S(2)}) collective-permute-start(f32[128,256]{1,0:T(8,128)S(1)} %add.21), channel_id=1, source_target_pairs={{0,4},{1,5},{2,6},{3,7},{4,0},{5,1},{6,2},{7,3},{8,12},{9,13},{10,... | collective-permute-start | bytes 393224 | tf_op jit(solution)/shard_map/ppermute | solution.py:175
  32.8 2.8 collective-permute-done.3
  35.6 0.7 add.22.x
  36.3 2.0 maps.1
  38.3 0.0 all-gather.3.cloned.1.call-update
  38.3 0.7 copy.13.parent
  39.0 0.7 fusion.4
  39.7 3.8 %leaf_forward.1 = (bf16[512,256]{1,0:T(8,128)(2,1)}, bf16[2048,256]{1,0:T(8,128)(2,1)}) custom-call(s32[4,2]{1,0:T(4,128)} %copy.13.parent, s32[1]{0:T(128)} %bitcast.1.group, bf16[512,256]{1,0:T(8,128)(2,1)} %rhs.1, bf16[4,128,128]{2,1,0:T(8,128)(2,1)} %inv.5, bf16[4,2,128,128]{3,2,1,0:T(8,128)(2,1)} %cpl.3, bf16[256,256]{1,0:T(8,128)(2,1)} %sep_rhs.1), custom_call_target="tpu_custom_call" | custom-call | flops 100663296 | bytes 4194304 | tf_op jit(solution)/shard_map/leaf_forward/pallas_call | solution.py:211
  43.4 33.1 %all_to_all.40.parts = bf16[8,256,256]{2,1,0:T(8,128)(2,1)} all-to-all(bf16[8,256,256]{2,1,0:T(8,128)(2,1)} %bitcast.20), channel_id=1, replica_groups=mesh['wide'=32,'narrow'=8] {'narrow'}, dimensions={0} | all-to-all | bytes 2097152 | tf_op jit(solution)/shard_map/all_to_all | solution.py:221
  76.6 2.6 sum_spread.1
  79.2 28.5 %all_to_all.41 = bf16[8,256,256]{2,1,0:T(8,128)(2,1)} all-to-all(bf16[8,256,256]{2,1,0:T(8,128)(2,1)} %sum_spread.1), channel_id=1, replica_groups=mesh['wide'=32,'narrow'=8] {'narrow'}, dimensions={0} | all-to-all | bytes 2097152 | tf_op jit(solution)/shard_map/all_to_all | solution.py:225
  107.7 4.0 %middle.1 = (f32[256,256]{1,0:T(8,128)}, bf16[8,256,256]{2,1,0:T(8,128)(2,1)}) custom-call(s32[8]{0:T(128)} %bitcast.24, s32[1]{0:T(128)} %bitcast.3.last, bf16[256,2048]{1,0:T(8,128)(2,1)} %inv.4, bf16[2048,256]{1,0:T(8,128)(2,1)} %bitcast.18), custom_call_target="tpu_custom_call" | custom-call | flops 536870912 | bytes 4194304 | tf_op jit(solution)/shard_map/middle/pallas_call | solution.py:226
  111.7 13.3 %all_to_all.42.parts = f32[8,32,256]{2,1,0:T(8,128)} all-to-all(f32[8,32,256]{2,1,0:T(8,128)} %bitcast.23), channel_id=1, replica_groups=mesh['wide'=32,'narrow'=8] {'narrow'}, dimensions={0} | all-to-all | bytes 524288 | tf_op jit(solution)/shard_map/all_to_all | solution.py:236
  125.0 1.8 small_sum.1
  126.8 8.8 %all_to_all.43 = f32[4,32,256]{2,1,0:T(8,128)S(1)} all-to-all(f32[4,32,256]{2,1,0:T(8,128)} %small_sum.1), channel_id=1, replica_groups={{0,16,32,48},{8,24,40,56},{64,80,96,112},{72,88,104,120},{128,144,160,1..., dimensions={0} | all-to-all | bytes 262144 | tf_op jit(solution)/shard_map/all_to_all | solution.py:243
  135.6 11.0 %all_to_all.44 = f32[4,4,32,256]{3,2,1,0:T(8,128)S(1)} all-to-all(f32[4,4,32,256]{3,2,1,0:T(8,128)S(1)} %broadcast_in_dim.25), channel_id=1, replica_groups={{0,64,128,192},{8,72,136,200},{16,80,144,208},{24,88,152,216},{32,96,16..., dimensions={0} | all-to-all | bytes 1048576 | tf_op jit(solution)/shard_map/all_to_all | solution.py:245
  146.6 3.6 %all-to-all-start.2 = ((bf16[8,256,256]{2,1,0:T(8,128)(2,1)}), bf16[8,256,256]{2,1,0:T(8,128)(2,1)S(1)}, u32[]{:S(2)}, u32[]{:S(2)}) async-start(bf16[8,256,256]{2,1,0:T(8,128)(2,1)} %get-tuple-element.9), calls=%async_computation.2 | async-start | bytes 2097152 | tf_op jit(solution)/shard_map/all_to_all | solution.py:265
  150.2 0.0 copy-start
  150.2 0.0 slice-start
  150.3 9.5 %collective-permute-start = (f32[16,32,256]{2,1,0:T(8,128)S(1)}, f32[16,32,256]{2,1,0:T(8,128)S(1)}, u32[]{:S(2)}, u32[]{:S(2)}) collective-permute-start(f32[16,32,256]{2,1,0:T(8,128)S(1)} %bitcast.21), channel_id=1, source_target_pairs={{0,8},{8,0},{16,24},{24,16},{32,40},{40,32},{48,56},{56,48},{64,72... | collective-permute-start | bytes 1572872 | tf_op jit(solution)/shard_map/ppermute | solution.py:175
  159.8 8.1 %all-to-all-done.2.parts = bf16[8,256,256]{2,1,0:T(8,128)(2,1)S(1)} async-done(((bf16[8,256,256]{2,1,0:T(8,128)(2,1)}), bf16[8,256,256]{2,1,0:T(8,128)(2,1)S(1)}, u32[]{:S(2)}, u32[]{:S(2)}) %all-to-all-start.2) | async-done | bytes 1048608 | tf_op jit(solution)/shard_map/all_to_all | solution.py:265
  167.8 1.0 copy-done.2
  168.8 2.5 sum_keep_spread.1
  171.3 0.0 copy-done.4
  171.3 4.8 %all-to-all-start.3 = ((bf16[8,256,256]{2,1,0:T(8,128)(2,1)}), bf16[8,256,256]{2,1,0:T(8,128)(2,1)S(1)}, u32[]{:S(2)}, u32[]{:S(2)}) async-start(bf16[8,256,256]{2,1,0:T(8,128)(2,1)} %get-tuple-element.11), calls=%async_computation.3 | async-start | bytes 2097152 | tf_op jit(solution)/shard_map/all_to_all | solution.py:274
  176.0 0.0 all-reduce.2.cloned.1.call-start
  176.1 0.0 copy-done
  176.1 2.0 convolution_bitcast_fusion
  178.1 0.0 all-reduce.2.cloned.1.call-update
  178.1 0.0 collective-permute-done.ag_other
  178.1 0.0 all-gather.3.cloned.1.call-done
  178.1 0.7 copy-done.7
  178.9 13.2 %chain.1 = f32[8,32,256]{2,1,0:T(8,128)} custom-call(s32[1]{0:T(128)} %bitcast.8.core, s32[1]{0:T(128)} %bitcast.9.me, f32[16,32,256]{2,1,0:T(8,128)} %bitcast.22, f32[16,32,256]{2,1,0:T(8,128)} %copy-done.7, f32[32,384,128]{2,1,0:T(8,128)} %bitcast.26, bf16[128,128]{1,0:T(8,128)(2,1)} %link.5), custom_call_target="tpu_custom_call" | custom-call | flops 12079595520 | bytes 8388608 | tf_op jit(solution)/shard_map/chain/pallas_call | solution.py:249
  192.1 1.7 all-to-all-done.3
  193.8 4.9 %all-to-all-start.7 = ((f32[8,32,256]{2,1,0:T(8,128)}), f32[8,32,256]{2,1,0:T(8,128)S(1)}, u32[]{:S(2)}, u32[]{:S(2)}) async-start(f32[8,32,256]{2,1,0:T(8,128)} %chain.1), calls=%async_computation.7 | async-start | bytes 524288 | tf_op jit(solution)/shard_map/all_to_all | solution.py:263
  198.7 69.7 %all-reduce.2.cloned.1.call-done.shared = f32[2048,256]{1,0:T(8,128)} async-done(((f32[2048,256]{1,0:T(8,128)}), f32[2048,256]{1,0:T(8,128)}) %all-reduce.2.cloned.1.call-update) | async-done | bytes 2097168 | tf_op jit(solution)/shard_map/psum | solution.py:209
  268.4 0.0 all-to-all-done.7
  268.4 0.7 copy-done.3
  269.1 7.1 %final.1 = (f32[512,256]{1,0:T(8,128)}, f32[256,256]{1,0:T(8,128)}) custom-call(s32[4,2]{1,0:T(4,128)} %copy.13.parent, s32[8]{0:T(128)} %bitcast.25, s32[1]{0:T(128)} %bitcast.1.group, f32[256,256]{1,0:T(8,128)} %get-tuple-element.10.kept, bf16[2048,256]{1,0:T(8,128)(2,1)} %bitcast.17, f32[2048,256]{1,0:T(8,128)} %all-reduce.2.cloned.1.call-done.shared, ...), custom_call_target="tpu_custom_call" | custom-call | flops 335544320 | bytes 6291456 | tf_op jit(solution)/shard_map/final/pallas_call | solution.py:276
  (16 shorter events, 0.2 us)
Async XLA Ops:
  8.0 31.0 %copy-start.5 = (s32[1,8]{1,0:T(1,128)S(1)}, s32[1,8]{1,0:T(1,128)}, u32[]{:S(2)}) copy-start(s32[1,8]{1,0:T(1,128)} %param.15) | copy-start | bytes 100
  8.0 30.3 %copy-start.6 = (s32[4,2]{0,1:T(2,128)S(1)}, s32[4,2]{0,1:T(2,128)}, u32[]{:S(2)}) copy-start(s32[4,2]{0,1:T(2,128)} %param.11) | copy-start | bytes 100
  8.0 170.1 %all-gather.3.cloned.1.call-start = ((), (), s32[]{:S(2)}) async-start(), calls=%async_computation.9 | async-start | bytes 6488064 | tf_op jit(solution)/shard_map/all_gather | solution.py:205
  11.9 4.9 %collective-permute-start.1 = (f32[128,256]{1,0:T(8,128)S(1)}, f32[128,256]{1,0:T(8,128)S(1)}, u32[]{:S(2)}, u32[]{:S(2)}) collective-permute-start(f32[128,256]{1,0:T(8,128)S(1)} %pad_maximum_fusion), channel_id=1, source_target_pairs={{0,1},{1,0},{2,3},{3,2},{4,5},{5,4},{6,7},{7,6},{8,9},{9,8},{10,11... | collective-permute-start | bytes 393224 | tf_op jit(solution)/shard_map/ppermute | solution.py:175
  16.8 9.5 %collective-permute-start.2 = (f32[128,256]{1,0:T(8,128)S(1)}, f32[128,256]{1,0:T(8,128)S(1)}, u32[]{:S(2)}, u32[]{:S(2)}) collective-permute-start(f32[128,256]{1,0:T(8,128)S(1)} %fusion.8), channel_id=1, source_target_pairs={{0,2},{1,3},{2,0},{3,1},{4,6},{5,7},{6,4},{7,5},{8,10},{9,11},{10,... | collective-permute-start | bytes 393224 | tf_op jit(solution)/shard_map/ppermute | solution.py:175
  26.4 9.2 %collective-permute-start.3 = (f32[128,256]{1,0:T(8,128)S(1)}, f32[128,256]{1,0:T(8,128)S(1)}, u32[]{:S(2)}, u32[]{:S(2)}) collective-permute-start(f32[128,256]{1,0:T(8,128)S(1)} %add.21), channel_id=1, source_target_pairs={{0,4},{1,5},{2,6},{3,7},{4,0},{5,1},{6,2},{7,3},{8,12},{9,13},{10,... | collective-permute-start | bytes 393224 | tf_op jit(solution)/shard_map/ppermute | solution.py:175
  146.6 24.6 %copy-start.4 = (f32[4,4,32,256]{3,2,1,0:T(8,128)}, f32[4,4,32,256]{3,2,1,0:T(8,128)S(1)}, u32[]{:S(2)}) copy-start(f32[4,4,32,256]{3,2,1,0:T(8,128)S(1)} %all_to_all.44) | copy-start | bytes 1572868
  146.6 21.2 %all-to-all-start.2 = ((bf16[8,256,256]{2,1,0:T(8,128)(2,1)}), bf16[8,256,256]{2,1,0:T(8,128)(2,1)S(1)}, u32[]{:S(2)}, u32[]{:S(2)}) async-start(bf16[8,256,256]{2,1,0:T(8,128)(2,1)} %get-tuple-element.9), calls=%async_computation.2 | async-start | bytes 2097152 | tf_op jit(solution)/shard_map/all_to_all | solution.py:265
  150.2 25.9 %copy-start = (bf16[256,2048]{1,0:T(8,128)(2,1)S(1)}, bf16[256,2048]{1,0:T(8,128)(2,1)}, u32[]{:S(2)}) copy-start(bf16[256,2048]{1,0:T(8,128)(2,1)} %inv.4) | copy-start | bytes 3145732
  150.2 25.9 %slice-start = ((bf16[256,2048]{1,0:T(8,128)(2,1)}), bf16[256,128]{1,0:T(8,128)(2,1)S(1)}, s32[]{:S(2)}) async-start(bf16[256,2048]{1,0:T(8,128)(2,1)} %inv.4), calls=%async_computation.10 | async-start | bytes 131072 | tf_op jit(solution)/shard_map/slice | solution.py:198
  150.3 27.8 %collective-permute-start = (f32[16,32,256]{2,1,0:T(8,128)S(1)}, f32[16,32,256]{2,1,0:T(8,128)S(1)}, u32[]{:S(2)}, u32[]{:S(2)}) collective-permute-start(f32[16,32,256]{2,1,0:T(8,128)S(1)} %bitcast.21), channel_id=1, source_target_pairs={{0,8},{8,0},{16,24},{24,16},{32,40},{40,32},{48,56},{56,48},{64,72... | collective-permute-start | bytes 1572872 | tf_op jit(solution)/shard_map/ppermute | solution.py:175
  167.8 1.0 copy-start.2
  171.3 22.5 %all-to-all-start.3 = ((bf16[8,256,256]{2,1,0:T(8,128)(2,1)}), bf16[8,256,256]{2,1,0:T(8,128)(2,1)S(1)}, u32[]{:S(2)}, u32[]{:S(2)}) async-start(bf16[8,256,256]{2,1,0:T(8,128)(2,1)} %get-tuple-element.11), calls=%async_computation.3 | async-start | bytes 2097152 | tf_op jit(solution)/shard_map/all_to_all | solution.py:274
  176.0 92.4 %all-reduce.2.cloned.1.call-start = ((), (), s32[]{:S(2)}) async-start(), calls=%async_computation.8 | async-start | bytes 4194304 | tf_op jit(solution)/shard_map/psum | solution.py:209
  178.1 0.8 copy-start.7
  193.8 74.6 %copy-start.1 = (bf16[8,256,256]{2,1,0:T(8,128)(2,1)}, bf16[8,256,256]{2,1,0:T(8,128)(2,1)S(1)}, u32[]{:S(2)}) copy-start(bf16[8,256,256]{2,1,0:T(8,128)(2,1)S(1)} %all-to-all-done.3) | copy-start | bytes 3145732
  193.8 74.6 %all-to-all-start.7 = ((f32[8,32,256]{2,1,0:T(8,128)}), f32[8,32,256]{2,1,0:T(8,128)S(1)}, u32[]{:S(2)}, u32[]{:S(2)}) async-start(f32[8,32,256]{2,1,0:T(8,128)} %chain.1), calls=%async_computation.7 | async-start | bytes 524288 | tf_op jit(solution)/shard_map/all_to_all | solution.py:263
  268.4 0.7 copy-start.3
Sparse Core Ops, SparseCore 0:
  38.4 57.4 all-gather.2
Sparse Core Ops, SparseCore 1:
  178.9 89.5 all-reduce.1

commit v2 on v1

v2 whole, which is shorter than its diff:
```python
import jax
import jax.numpy as jnp
from jax import lax
from jax.experimental import pallas as pl
from jax.experimental.pallas import tpu as pltpu
from jax.sharding import PartitionSpec as P

BF = jnp.bfloat16
F32 = jnp.float32
VMEM = pl.BlockSpec(memory_space=pltpu.VMEM)
SMEM = pl.BlockSpec(memory_space=pltpu.SMEM)
ANY = pl.BlockSpec(memory_space=pl.ANY)
LIMIT = 56 * 1024 * 1024

NN = (((1,), (0,)), ((), ()))
NT = (((1,), (1,)), ((), ()))
TN = (((0,), (0,)), ((), ()))


def mm(a, b, dims):
    return lax.dot_general(a, b, dims, preferred_element_type=F32)


def halves(v):
    hi = v.astype(BF)
    return hi, (v - hi.astype(F32)).astype(BF)


def mm3(a, b, dims):
    ah, al = halves(a)
    bh, bl = halves(b)
    return mm(ah, bh, dims) + (mm(al, bh, dims) + mm(ah, bl, dims))


def mm2(a, b_exact, dims):
    ah = a.astype(BF)
    rest = a - ah.astype(F32)
    al = rest.astype(BF)
    ax = (rest - al.astype(F32)).astype(BF)
    return mm(ah, b_exact, dims) + (mm(al, b_exact, dims) + mm(ax, b_exact, dims))


def call(kernel, name, outs, ins, scratch=(), flops=0, moved=0):
    return pl.pallas_call(
        kernel,
        name=name,
        out_shape=outs,
        in_specs=ins,
        out_specs=jax.tree.map(lambda _: VMEM, outs, is_leaf=lambda o: hasattr(o, "dtype")),
        scratch_shapes=list(scratch),
        compiler_params=pltpu.CompilerParams(vmem_limit_bytes=LIMIT),
        cost_estimate=pl.CostEstimate(flops=flops, bytes_accessed=moved, transcendentals=0),
    )


def held_group(owners):
    me = lax.axis_index("narrow")
    group = jnp.int32(0)
    for g in range(1, 8):
        group = jnp.where(owners[0, g] == me, g, group)
    return group


def leaf_forward_kernel(parent, owners, rhs, inv, cpl, sep_rhs, sep_inv, fl, *refs):
    blocks = refs[:-3]
    acc, head, sem = refs[-3:]
    fetch = pltpu.make_async_copy(sep_inv.at[:, pl.ds(0, head.shape[1])], head, sem)
    fetch.start()
    b = inv.shape[1]
    rows = sep_rhs.shape[0]
    n = len(blocks)
    me = lax.axis_index("narrow")
    acc[...] = jnp.zeros_like(acc)
    start = pl.multiple_of(held_group(owners) * rows, rows)
    acc[pl.ds(start, rows), :] = sep_rhs[...].astype(F32)
    for i in range(inv.shape[0]):
        f = mm(inv[i], rhs[i * b : (i + 1) * b, :], NN).astype(BF)
        fl[i * b : (i + 1) * b, :] = f
        for k in range(cpl.shape[1]):
            at = pl.ds(pl.multiple_of(parent[k, i] * b, b), b)
            acc[at, :] -= mm(cpl[i, k], f, NN)
    fetch.wait()
    corner_hi, corner_lo = halves(mm(head[...], head[...], TN))
    acc[n * rows : n * rows + b, :b] = corner_hi.astype(F32)
    acc[n * rows : n * rows + b, b:] = corner_lo.astype(F32)
    tail = head[rows - b :, :].astype(F32)
    acc[n * rows + b :, :b] = jnp.where(owners[0, n - 1] == me, tail, 0.0)
    step = b // n
    for j in range(n):
        g = lax.rem(me + j, n)
        blocks[j][:rows, :] = acc[pl.ds(pl.multiple_of(g * rows, rows), rows), :].astype(BF)
        corner = acc[pl.ds(pl.multiple_of(n * rows + g * step, step), step), :].astype(BF)
        tail = acc[pl.ds(pl.multiple_of(n * rows + b + g * step, step), step), :b].astype(BF)
        blocks[j][rows : rows + step, :b] = tail
        blocks[j][rows : rows + step, b:] = corner[:, :b]
        blocks[j][rows + step :, :b] = corner[:, b:]
        blocks[j][rows + step :, b:] = corner[:, b:]


def sum_own_kernel(right, left, local, out):
    rows = right.shape[1]
    b = rows // 2
    step = (right.shape[0] - rows) // 2
    total = right[...].astype(F32) + left[...].astype(F32) + local[...].astype(F32)
    corner_hi, corner_lo = halves(total[rows : rows + step, b:] + total[rows + step :, :b])
    out[:rows, :] = total[:rows].astype(BF)
    out[rows : rows + step, :b] = total[rows : rows + step, :b].astype(BF)
    out[rows : rows + step, b:] = corner_hi
    out[rows + step :, :b] = corner_lo
    out[rows + step :, b:] = corner_lo


def pack_kernel(kept, shared, *refs):
    packed = refs[-1]
    rows = kept.shape[0]
    packed[:rows, :] = kept[...]
    packed[rows:, :] = shared[...]


def middle_kernel(owners, inv, *refs):
    n = 8
    coupled = refs[:n]
    link, _, ag, terms, maps, whole, corner, tail = refs[n:]
    me = lax.axis_index("narrow")
    rows = inv.shape[0]
    b = rows // 2
    step = b // n
    for j in range(n):
        g = lax.rem(me + j, n)
        block = coupled[j]
        whole[pl.ds(pl.multiple_of(g * rows, rows), rows), :] = block[:rows, :]
        at = pl.ds(pl.multiple_of(g * step, step), step)
        tail[at, :] = block[rows : rows + step, :b]
        corner[at, :] = block[rows : rows + step, b:].astype(F32) + block[
            rows + step :, :b
        ].astype(F32)
    applied = mm(inv[...], whole[...], NN)
    app = applied.astype(BF)
    for g in range(n):
        terms[owners[0, g]] = mm(inv[:, g * rows : (g + 1) * rows], app, TN).astype(BF)
    ag[:, :b] = jnp.where(owners[0, n - 1] == me, applied[rows - b :, :], 0.0).T
    ag[:, b:] = mm(app, inv[:, :b], TN)
    maps[:b, :] = mm(tail[...], link[...], NN)
    inner = mm2(corner[...], link[...], NN)
    maps[b:, :] = mm2(inner, link[...], TN)


def small_sum_kernel(parts, link, _, spread):
    b = link.shape[0]
    total = parts[0]
    for j in range(1, parts.shape[0]):
        total += parts[j]
    moved = mm2(total[:, b:], link[...], NN)
    for j in range(spread.shape[0]):
        spread[j, :, :b] = total[:, :b]
        spread[j, :, b:] = moved


def chain_kernel(*refs):
    ag_own, ag_other = refs[:2]
    maps_own, maps_other = refs[2:6], refs[6:10]
    link, out, ag, maps, states, incoming, sems = refs[11:]
    b = link.shape[0]
    length = states.shape[0]
    wide = lax.axis_index("wide")
    here = lax.rem(wide, 2)
    x = lax.rem(lax.div(wide, 2), 4)
    y = lax.div(wide, 8)
    copies = []
    for side, ag_part, parts in ((here, ag_own, maps_own), (1 - here, ag_other, maps_other)):
        copies.append((ag_part, ag.at[side]))
        for j in range(4):
            for k in range(4):
                at = lax.rem(y + j, 4) * 4 + lax.rem(x + k, 4)
                copies.append((parts[j].at[k], maps.at[side, at]))
    copies = [pltpu.make_async_copy(p, q, sems.at[i]) for i, (p, q) in enumerate(copies)]
    for copy in copies:
        copy.start()
    for copy in copies:
        copy.wait()
    state = jnp.zeros((out.shape[1], b), F32)
    for w in range(length):
        states[w] = state
        if w + 1 < length:
            state = ag[w % 2, w // 2, :, :b] - mm3(state, maps[w % 2, w // 2, :b, :], NT)
    back = jnp.zeros_like(state)
    for w in range(length - 1, -1, -1):
        incoming[w] = back
        if w > 0:
            local = ag[w % 2, w // 2, :, b:] - mm3(states[w], maps[w % 2, w // 2, b:, :], NN)
            back = local - mm3(back, maps[w % 2, w // 2, :b, :], NN)
    mine = mm2(states[wide], link[...], NT)
    for j in range(out.shape[0]):
        out[j, :, :b] = mine
        out[j, :, b:] = incoming[wide]


def final_kernel(
    parent, owners, kept, gathered, z, cpl, inv, fl, leaf_out, sep_out, zs
):
    b = inv.shape[1]
    rows = kept.shape[0]
    zh, zl = halves(z[...])
    zs[0] = zh
    zs[1] = zl

    def fix(g, start, count):
        part = gathered[g, pl.ds(rows + start, count), :]
        return mm(part, zs[0], NT) + mm(part, zs[1], NT)

    sep_out[...] = kept[...].astype(F32) - fix(held_group(owners), 0, rows)
    for i in range(inv.shape[0]):
        acc = fl[i * b : (i + 1) * b, :].astype(F32)
        for k in range(cpl.shape[1]):
            p = parent[k, i]
            g = lax.div(p, 2)
            at = pl.multiple_of(lax.rem(p, 2) * b, b)
            block = gathered[owners[0, g], pl.ds(at, b), :].astype(F32)
            block = (block - fix(g, at, b)).astype(BF)
            acc -= mm(cpl[i, k], block, TN)
        leaf_out[i * b : (i + 1) * b, :] = mm(inv[i], acc.astype(BF), TN)


def swap(value, axis, by):
    n = lax.axis_size(axis)
    return lax.ppermute(value, axis, [(i, i ^ by) for i in range(n)])


def turned(value, by):
    n = lax.axis_size("narrow")
    return lax.ppermute(value, "narrow", [(i, (i + by) % n) for i in range(n)])


def ring_sum(blocks):
    def plus(value, block):
        return (value.astype(F32) + block.astype(F32)).astype(BF)

    right = turned(blocks[4], 1)
    left = turned(blocks[5], -1)
    right = turned(plus(right, blocks[3]), 1)
    left = turned(plus(left, blocks[6]), -1)
    right = turned(plus(right, blocks[2]), 1)
    left = turned(plus(left, blocks[7]), -1)
    right = turned(plus(right, blocks[1]), 1)
    return right, left


def ring_gather(block):
    ahead = [block]
    behind = [block]
    for _ in range(3):
        behind.append(turned(behind[-1], 1))
        ahead.append(turned(ahead[-1], -1))
    behind.append(turned(behind[-1], 1))
    return ahead + behind[:0:-1]


def turned_wide(value, along, by):
    def source(i):
        y, x, core = i // 8, (i // 2) % 4, i % 2
        y, x = (y, (x + by) % 4) if along == "x" else ((y + by) % 4, x)
        return (y * 4 + x) * 2 + core

    return lax.ppermute(value, "wide", [(source(i), i) for i in range(32)])


def per_device(
    leaf_rhs, leaf_inv, leaf_coupling, leaf_parent, sep_rhs, sep_inv, sep_link, row_owner
):
    b = leaf_inv.shape[1]
    leaf_count = leaf_inv.shape[0]
    sketch = leaf_rhs.shape[1]
    rows = sep_inv.shape[0]
    n = lax.axis_size("narrow")
    chain_len = lax.axis_size("wide")
    chips = chain_len // 2
    all_rows = sep_inv.shape[1]
    cols = sketch // n
    parent = leaf_parent.T
    shape = jax.ShapeDtypeStruct
    held = pltpu.VMEM

    extra = rows + 2 * (b // n)
    fl, *blocks = call(
        leaf_forward_kernel,
        "leaf_forward",
        (shape((leaf_count * b, sketch), BF),) + (held((extra, sketch), BF),) * n,
        [SMEM] * 2 + [VMEM] * 4 + [ANY],
        [
            pltpu.VMEM((all_rows + 2 * b, sketch), F32),
            pltpu.VMEM((rows, b), BF),
            pltpu.SemaphoreType.DMA,
        ],
        flops=2 * 12 * b * b * sketch,
        moved=4 << 20,
    )(parent, row_owner, leaf_rhs, leaf_inv, leaf_coupling, sep_rhs, sep_inv)
    right, left = ring_sum(blocks)
    own = call(sum_own_kernel, "sum_own", held((extra, sketch), BF), [VMEM] * 3, moved=1 << 18)(
        right, left, blocks[0]
    )
    coupled = ring_gather(own)

    rows_at = lax.broadcasted_iota(jnp.int32, (rows, b), 0)
    cols_at = lax.broadcasted_iota(jnp.int32, (rows, b), 1)
    last = row_owner[0, n - 1] == lax.axis_index("narrow")
    pick = jnp.where(last & (rows_at == cols_at + (rows - b)), 1.0, 0.0).astype(BF)
    shared = mm(sep_inv, jnp.concatenate([sep_inv[:, :b], pick], axis=1), TN).astype(BF)
    shared = lax.psum_scatter(shared, "narrow", scatter_dimension=0, tiled=True)

    ag, terms, maps = call(
        middle_kernel,
        "middle",
        (
            shape((sketch, 2 * b), F32),
            shape((n, rows, sketch), BF),
            shape((2 * b, b), F32),
        ),
        [SMEM] + [VMEM] * (2 + n) + [ANY],
        [
            pltpu.VMEM((all_rows, sketch), BF),
            pltpu.VMEM((b, b), F32),
            pltpu.VMEM((b, b), BF),
        ],
        flops=4 * rows * all_rows * sketch,
        moved=4 << 20,
    )(row_owner, sep_inv, *coupled, sep_link, shared)

    kept = lax.psum_scatter(
        terms.reshape(all_rows, sketch), "narrow", scatter_dimension=0, tiled=True
    )
    maps = jnp.stack([maps] + [turned_wide(maps, "x", k) for k in (1, 2, 3)])
    maps = [maps] + [turned_wide(maps, "y", k) for k in (1, 2, 3)]
    maps_other = [swap(part, "wide", 1) for part in maps]
    ag = lax.all_to_all(ag.reshape(n, cols, 2 * b), "narrow", 0, 0, tiled=True)
    ag = call(
        small_sum_kernel,
        "small_sum",
        shape((chips, cols, 2 * b), F32),
        [VMEM] * 2 + [ANY],
        moved=1 << 19,
    )(ag, sep_link, maps[0])
    same_core = [[2 * q + c for q in range(chips)] for c in range(2)]
    ag = lax.all_to_all(ag, "wide", 0, 0, tiled=True, axis_index_groups=same_core)
    other = swap(ag, "wide", 1)
    packed = call(
        pack_kernel, "pack", shape((2 * rows, sketch), BF), [VMEM] * 2 + [ANY] * 4, moved=1 << 19
    )(kept, shared, other, *maps[1:])
    gathered = lax.all_gather(packed, "narrow", axis=0, tiled=False)
    z = call(
        chain_kernel,
        "chain",
        shape((n, cols, 2 * b), F32),
        [ANY] * 11 + [VMEM],
        [
            pltpu.VMEM((2, chips, cols, 2 * b), F32),
            pltpu.VMEM((2, chips, 2 * b, b), F32),
            pltpu.VMEM((chain_len, cols, b), F32),
            pltpu.VMEM((chain_len, cols, b), F32),
            pltpu.SemaphoreType.DMA((2 + 2 * chips,)),
        ],
        flops=2 * 9 * chain_len * cols * b * b,
        moved=8 << 20,
    )(ag, other, *maps, *maps_other, packed, sep_link)
    z = lax.all_to_all(z, "narrow", 0, 0, tiled=True).reshape(sketch, 2 * b)

    leaf_out, sep_out = call(
        final_kernel,
        "final",
        (shape((leaf_count * b, sketch), F32), shape((rows, sketch), F32)),
        [SMEM] * 2 + [VMEM] * 6,
        [pltpu.VMEM((2, sketch, 2 * b), BF)],
        flops=2 * 40 * b * b * sketch,
        moved=6 << 20,
    )(parent, row_owner, kept, gathered, z, leaf_coupling, leaf_inv, fl)
    return leaf_out, sep_out


def solution(mesh):
    both = ("wide", "narrow")
    placed = (
        P(both, None),
        P(both, None, None),
        P(both, None, None, None),
        P(both, None),
        P(both, None),
        P(both, None),
        P("wide", None),
        P("wide", None),
    )
    return jax.shard_map(
        per_device,
        mesh=mesh,
        in_specs=placed,
        out_specs=(P(both, None), P(both, None)),
        check_vma=False,
    )
```

time: 288 us -> 195 us (0.68)
  blocking collectives: 94.7 us -> 20.4 us
  waiting for transfers between devices: 90.4 us -> 59 us
  starting transfers between devices: 35.7 us -> 55 us
  Pallas kernels: 36.9 us -> 32.3 us
    all_to_all x5 -> x1, blocking collectives: 94.7 us -> 20.4 us  [per_device(): z = lax.all_to_all(z, 'narrow', 0, 0, tiled=True).reshape(sketch, 2 * b)]
    psum x1 -> x0, waiting for transfers between devices: 69.7 us -> none  [per_device(): lax.psum(mm(sep_inv, jnp.concatenate([head, pick], axis=1), TN), 'narrow')]
    ppermute x0 -> x20, waiting for transfers between devices: none -> 50 us  [the longest x14 31 us: turned(): return lax.ppermute(value, 'narrow', [(i, (i + by) % n) for i in range(n)])]
    ppermute x0 -> x20, starting transfers between devices: none -> 29.3 us  [the longest x14 21.8 us: turned(): return lax.ppermute(value, 'narrow', [(i, (i + by) % n) for i in range(n)])]
    ppermute x4 -> x5, starting transfers between devices: 22.3 us -> 12.2 us  [swap(): return lax.ppermute(value, axis, [(i, i ^ by) for i in range(n)])]
    ppermute x4 -> x5, waiting for transfers between devices: 10.9 us -> 3.38 us  [swap(): return lax.ppermute(value, axis, [(i, i ^ by) for i in range(n)])]
    all_to_all x3 -> x2, waiting for transfers between devices: 9.74 us -> 5.52 us  [the longest x1 5.51 us: per_device(): lax.all_to_all(ag, 'wide', 0, 0, tiled=True, axis_index_groups=same_core)]
    pallas_call x5 -> x4, Pallas kernels: 22.1 us -> 19.4 us  [the longest x1 14.7 us: per_device(): call(chain_kernel, 'chain', shape((n, cols, 2 * b), F32), [ANY] * 11 + [V...]
  transfers between devices with their start and end apart: 9 -> 30, of which waited for: 6 -> 18; matrix products, arithmetic and copies ran while one was open for 1% -> 1% of each run, Pallas kernels for 10% -> 11%
where the time goes in v2:
time: 195 us; the launch traced here: 192 us
  waiting for transfers between devices  59 us (30%)
  starting transfers between devices  55 us (28%)
  Pallas kernels  32.3 us (17%)
  blocking collectives  20.4 us (10%)
  between operations  14.6 us (7%)
  local copies, waits for them, and re-layouts  5.88 us (3%)
  matrix products  2.79 us (1%)
  other arithmetic  1.97 us (1%)
    ppermute x14, waiting for transfers between devices, turned(): return lax.ppermute(value, 'narrow', [(i, (i + by) % n) for i in range(n)])  31 us
    ppermute x14, starting transfers between devices, turned(): return lax.ppermute(value, 'narrow', [(i, (i + by) % n) for i in range(n)])  21.8 us
    all_to_all x1, blocking collectives, per_device(): z = lax.all_to_all(z, 'narrow', 0, 0, tiled=True).reshape(sketch, 2 * b)  20.4 us
    ppermute x6, waiting for transfers between devices, turned_wide(): return lax.ppermute(value, 'wide', [(source(i), i) for i in range(32)])  19.1 us
    pallas_call x1, Pallas kernels, per_device(): call(chain_kernel, 'chain', shape((n, cols, 2 * b), F32), [ANY] * 11 + [V...  14.7 us
    ppermute x5, starting transfers between devices, swap(): return lax.ppermute(value, axis, [(i, i ^ by) for i in range(n)])  12.2 us
    all_to_all x1, starting transfers between devices, per_device(): ag = lax.all_to_all(ag.reshape(n, cols, 2 * b), 'narrow', 0, 0, tiled=True)  8.06 us
    ppermute x6, starting transfers between devices, turned_wide(): return lax.ppermute(value, 'wide', [(source(i), i) for i in range(32)])  7.54 us
  transfers between devices with their start and end apart: 30, of which 18 were waited for; matrix products, arithmetic and copies ran while one was open for 1% of the time, Pallas kernels for 11%

profile of v2, /device:TPU:1, one launch (start us, length us, event | category | flops | bytes accessed | tf_op | source)
XLA Modules:
  0.0 192.0 jit_solution(9007475426329837316)
XLA Ops:
  7.2 1.2 slice.7
  8.5 0.8 slice.6
  10.0 2.8 %fusion = bf16[2048,256]{1,0:T(8,128)(2,1)} fusion(bf16[256,2048]{1,0:T(8,128)(2,1)} %inv.4, bf16[256,128]{1,0:T(8,128)(2,1)S(1)} %select_convert_fusion, bf16[256,128]{1,0:T(8,128)(2,1)S(1)} %slice.6), kind=kOutput, calls=%fused_computation.1 | convolution fusion | flops 269221888 | bytes 2228224 | tf_op jit(solution)/shard_map/dot_general | solution.py:21
  12.9 3.6 %leaf_forward.1 = (bf16[512,256]{1,0:T(8,128)(2,1)}, bf16[288,256]{1,0:T(8,128)(2,1)S(1)}, bf16[288,256]{1,0:T(8,128)(2,1)S(1)}, bf16[288,256]{1,0:T(8,128)(2,1)...) custom-call(s32[2,4]{1,0:T(2,128)} %bitcast.21, ...), custom_call_target="tpu_custom_call" | custom-call | flops 100663296 | bytes 4194304 | tf_op jit(solution)/shard_map/leaf_forward/pallas_call | solution.py:284
  16.5 2.5 %collective-permute-start = (bf16[288,256]{1,0:T(8,128)(2,1)S(1)}, bf16[288,256]{1,0:T(8,128)(2,1)S(1)}, u32[]{:S(2)}, u32[]{:S(2)}) collective-permute-start(bf16[288,256]{1,0:T(8,128)(2,1)S(1)} %get-tuple-element.14), channel_id=1, source_target_pairs={{0,1},{1,2},{2,3},{3,4},{4,5},{5,6},{6,7},{7,0},{8,9},{9,10},{10,1... | collective-permute-start | bytes 442376 | tf_op jit(solution)/shard_map/ppermute | solution.py:231
  19.1 4.0 %collective-permute-start.4 = (bf16[288,256]{1,0:T(8,128)(2,1)S(1)}, bf16[288,256]{1,0:T(8,128)(2,1)S(1)}, u32[]{:S(2)}, u32[]{:S(2)}) collective-permute-start(bf16[288,256]{1,0:T(8,128)(2,1)S(1)} %get-tuple-element.18), channel_id=1, source_target_pairs={{0,7},{1,0},{2,1},{3,2},{4,3},{5,4},{6,5},{7,6},{8,15},{9,8},{10,9... | collective-permute-start | bytes 442376 | tf_op jit(solution)/shard_map/ppermute | solution.py:231
  23.1 3.5 %collective-permute-done = bf16[288,256]{1,0:T(8,128)(2,1)S(1)} collective-permute-done((bf16[288,256]{1,0:T(8,128)(2,1)S(1)}, bf16[288,256]{1,0:T(8,128)(2,1)S(1)}, u32[]{:S(2)}, u32[]{:S(2)}) %collective-permute-start) | collective-permute-done | bytes 147488 | tf_op jit(solution)/shard_map/ppermute | solution.py:231
  26.8 2.7 %collective-permute-start.5 = (bf16[288,256]{1,0:T(8,128)(2,1)S(1)}, bf16[288,256]{1,0:T(8,128)(2,1)S(1)}, u32[]{:S(2)}, u32[]{:S(2)}) collective-permute-start(bf16[288,256]{1,0:T(8,128)(2,1)S(1)} %add_convert_fusion.1), channel_id=1, source_target_pairs={{0,7},{1,0},{2,1},{3,2},{4,3},{5,4},{6,5},{7,6},{8,15},{9,8},{10,9... | collective-permute-start | bytes 442376 | tf_op jit(solution)/shard_map/ppermute | solution.py:231
  29.5 3.5 %collective-permute-done.1 = bf16[288,256]{1,0:T(8,128)(2,1)S(1)} collective-permute-done((bf16[288,256]{1,0:T(8,128)(2,1)S(1)}, bf16[288,256]{1,0:T(8,128)(2,1)S(1)}, u32[]{:S(2)}, u32[]{:S(2)}) %collective-permute-start.1) | collective-permute-done | bytes 147488 | tf_op jit(solution)/shard_map/ppermute | solution.py:231
  33.4 2.5 %collective-permute-start.6 = (bf16[288,256]{1,0:T(8,128)(2,1)S(1)}, bf16[288,256]{1,0:T(8,128)(2,1)S(1)}, u32[]{:S(2)}, u32[]{:S(2)}) collective-permute-start(bf16[288,256]{1,0:T(8,128)(2,1)S(1)} %add_convert_fusion), channel_id=1, source_target_pairs={{0,7},{1,0},{2,1},{3,2},{4,3},{5,4},{6,5},{7,6},{8,15},{9,8},{10,9... | collective-permute-start | bytes 442376 | tf_op jit(solution)/shard_map/ppermute | solution.py:231
  35.9 2.8 %collective-permute-done.2 = bf16[288,256]{1,0:T(8,128)(2,1)S(1)} collective-permute-done((bf16[288,256]{1,0:T(8,128)(2,1)S(1)}, bf16[288,256]{1,0:T(8,128)(2,1)S(1)}, u32[]{:S(2)}, u32[]{:S(2)}) %collective-permute-start.2) | collective-permute-done | bytes 147488 | tf_op jit(solution)/shard_map/ppermute | solution.py:231
  38.7 1.7 collective-permute-start.3
  40.4 5.1 %collective-permute-done.3.right = bf16[288,256]{1,0:T(8,128)(2,1)S(1)} collective-permute-done((bf16[288,256]{1,0:T(8,128)(2,1)S(1)}, bf16[288,256]{1,0:T(8,128)(2,1)S(1)}, u32[]{:S(2)}, u32[]{:S(2)}) %collective-permute-start.3) | collective-permute-done | bytes 147488 | tf_op jit(solution)/shard_map/ppermute | solution.py:231
  45.5 0.7 copy-done.14
  46.1 1.1 sum_own.1.refs_0_
  47.6 2.4 %collective-permute-start.7 = (bf16[288,256]{1,0:T(8,128)(2,1)S(1)}, bf16[288,256]{1,0:T(8,128)(2,1)S(1)}, u32[]{:S(2)}, u32[]{:S(2)}) collective-permute-start(bf16[288,256]{1,0:T(8,128)(2,1)S(1)} %sum_own.1.refs_0_), channel_id=1, source_target_pairs={{0,7},{1,0},{2,1},{3,2},{4,3},{5,4},{6,5},{7,6},{8,15},{9,8},{10,9... | collective-permute-start | bytes 442376 | tf_op jit(solution)/shard_map/ppermute | solution.py:231
  50.0 3.2 %collective-permute-done.10.refs_7_ = bf16[288,256]{1,0:T(8,128)(2,1)S(1)} collective-permute-done((bf16[288,256]{1,0:T(8,128)(2,1)S(1)}, bf16[288,256]{1,0:T(8,128)(2,1)S(1)}, u32[]{:S(2)}, u32[]{:S(2)}) %collective-permute-start.10) | collective-permute-done | bytes 147488 | tf_op jit(solution)/shard_map/ppermute | solution.py:231
  53.3 2.7 %collective-permute-start.8 = (bf16[288,256]{1,0:T(8,128)(2,1)S(1)}, bf16[288,256]{1,0:T(8,128)(2,1)S(1)}, u32[]{:S(2)}, u32[]{:S(2)}) collective-permute-start(bf16[288,256]{1,0:T(8,128)(2,1)S(1)} %collective-permute-done.7.refs_1_), channel_id=1, source_target_pairs={{0,7},{1,0},{2,1},{3,2},{4,3},{5,4},{6,5},{7,6},{8,15},{9,8},{10,9... | collective-permute-start | bytes 442376 | tf_op jit(solution)/shard_map/ppermute | solution.py:231
  55.9 4.2 %collective-permute-done.11.refs_6_ = bf16[288,256]{1,0:T(8,128)(2,1)S(1)} collective-permute-done((bf16[288,256]{1,0:T(8,128)(2,1)S(1)}, bf16[288,256]{1,0:T(8,128)(2,1)S(1)}, u32[]{:S(2)}, u32[]{:S(2)}) %collective-permute-start.11) | collective-permute-done | bytes 147488 | tf_op jit(solution)/shard_map/ppermute | solution.py:231
  60.2 2.7 %collective-permute-start.9 = (bf16[288,256]{1,0:T(8,128)(2,1)S(1)}, bf16[288,256]{1,0:T(8,128)(2,1)S(1)}, u32[]{:S(2)}, u32[]{:S(2)}) collective-permute-start(bf16[288,256]{1,0:T(8,128)(2,1)S(1)} %collective-permute-done.8.refs_2_), channel_id=1, source_target_pairs={{0,7},{1,0},{2,1},{3,2},{4,3},{5,4},{6,5},{7,6},{8,15},{9,8},{10,9... | collective-permute-start | bytes 442376 | tf_op jit(solution)/shard_map/ppermute | solution.py:231
  62.8 3.3 %collective-permute-done.12.refs_5_ = bf16[288,256]{1,0:T(8,128)(2,1)S(1)} collective-permute-done((bf16[288,256]{1,0:T(8,128)(2,1)S(1)}, bf16[288,256]{1,0:T(8,128)(2,1)S(1)}, u32[]{:S(2)}, u32[]{:S(2)}) %collective-permute-start.12) | collective-permute-done | bytes 147488 | tf_op jit(solution)/shard_map/ppermute | solution.py:231
  66.2 5.2 %collective-permute-done.13.refs_4_ = bf16[288,256]{1,0:T(8,128)(2,1)S(1)} collective-permute-done((bf16[288,256]{1,0:T(8,128)(2,1)S(1)}, bf16[288,256]{1,0:T(8,128)(2,1)S(1)}, u32[]{:S(2)}, u32[]{:S(2)}) %collective-permute-start.13) | collective-permute-done | bytes 147488 | tf_op jit(solution)/shard_map/ppermute | solution.py:231
  72.0 4.2 %middle.1 = (f32[256,256]{1,0:T(8,128)}, bf16[8,256,256]{2,1,0:T(8,128)(2,1)}, f32[256,128]{1,0:T(8,128)}) custom-call(s32[1,8]{1,0:T(1,128)} %owners.5, bf16[256,2048]{1,0:T(8,128)(2,1)} %inv.4, bf16[288,256]{1,0:T(8,128)(2,1)} %copy-done, bf16[288,256]{1,0:T(8,128)(2,1)} %copy-done.16, bf16[288,256]{1,0:T(8,128)(2,1)} %copy-done.18, ...), custom_call_target="tpu_custom_call" | custom-call | flops 536870912 | bytes 4194304 | tf_op jit(solution)/shard_map/middle/pallas_call | solution.py:310
  76.2 8.1 %all-to-all-start = ((f32[8,32,256]{2,1,0:T(8,128)}), f32[8,32,256]{2,1,0:T(8,128)S(1)}, u32[]{:S(2)}, u32[]{:S(2)}) async-start(f32[8,32,256]{2,1,0:T(8,128)} %bitcast.16), calls=%async_computation.2 | async-start | bytes 524288 | tf_op jit(solution)/shard_map/all_to_all | solution.py:334
  84.3 2.6 %collective-permute-start.14 = (f32[256,128]{1,0:T(8,128)}, f32[256,128]{1,0:T(8,128)S(1)}, u32[]{:S(2)}, u32[]{:S(2)}) collective-permute-start(f32[256,128]{1,0:T(8,128)} %get-tuple-element.24), channel_id=1, source_target_pairs={{16,0},{24,8},{32,16},{40,24},{48,32},{56,40},{0,48},{8,56},{80,64... | collective-permute-start | bytes 393224 | tf_op jit(solution)/shard_map/ppermute | solution.py:264
  87.2 0.8 collective-permute-start.16
  88.0 2.6 %collective-permute-done.14 = f32[256,128]{1,0:T(8,128)S(1)} collective-permute-done((f32[256,128]{1,0:T(8,128)}, f32[256,128]{1,0:T(8,128)S(1)}, u32[]{:S(2)}, u32[]{:S(2)}) %collective-permute-start.14) | collective-permute-done | bytes 131104 | tf_op jit(solution)/shard_map/ppermute | solution.py:264
  90.6 2.0 %collective-permute-done.15 = f32[256,128]{1,0:T(8,128)S(1)} collective-permute-done((f32[256,128]{1,0:T(8,128)}, f32[256,128]{1,0:T(8,128)S(1)}, u32[]{:S(2)}, u32[]{:S(2)}) %collective-permute-start.15) | collective-permute-done | bytes 131104 | tf_op jit(solution)/shard_map/ppermute | solution.py:264
  92.6 1.3 collective-permute-done.16
  93.9 1.7 pad_maximum_fusion._.refs_2_
  95.6 0.7 copy-done.8
  96.3 1.9 %small_sum.1 = f32[16,32,256]{2,1,0:T(8,128)} custom-call(f32[8,32,256]{2,1,0:T(8,128)} %copy-done.8, bf16[128,128]{1,0:T(8,128)(2,1)} %refs_11_.1, f32[4,256,128]{2,1,0:T(8,128)} %pad_maximum_fusion._.refs_2_), custom_call_target="tpu_custom_call" | custom-call | bytes 524288 | tf_op jit(solution)/shard_map/small_sum/pallas_call | solution.py:335
  98.2 5.3 %all-to-all-start.1 = ((f32[16,32,256]{2,1,0:T(8,128)}), f32[16,32,256]{2,1,0:T(8,128)S(1)}, u32[]{:S(2)}, u32[]{:S(2)}) async-start(f32[16,32,256]{2,1,0:T(8,128)} %small_sum.1), calls=%async_computation.3 | async-start | bytes 1048576 | tf_op jit(solution)/shard_map/all_to_all | solution.py:343
  103.6 2.7 %collective-permute-start.18 = (f32[4,256,128]{2,1,0:T(8,128)S(1)}, f32[4,256,128]{2,1,0:T(8,128)S(1)}, u32[]{:S(2)}, u32[]{:S(2)}) collective-permute-start(f32[4,256,128]{2,1,0:T(8,128)S(1)} %copy-done.2), channel_id=1, source_target_pairs={{64,0},{72,8},{80,16},{88,24},{96,32},{104,40},{112,48},{120,56},{... | collective-permute-start | bytes 1572872 | tf_op jit(solution)/shard_map/ppermute | solution.py:264
  107.4 5.5 %all-to-all-done.1.refs_0_ = f32[16,32,256]{2,1,0:T(8,128)S(1)} async-done(((f32[16,32,256]{2,1,0:T(8,128)}), f32[16,32,256]{2,1,0:T(8,128)S(1)}, u32[]{:S(2)}, u32[]{:S(2)}) %all-to-all-start.1) | async-done | bytes 524320 | tf_op jit(solution)/shard_map/all_to_all | solution.py:343
  112.9 9.9 %collective-permute-start.17 = (f32[16,32,256]{2,1,0:T(8,128)S(1)}, f32[16,32,256]{2,1,0:T(8,128)S(1)}, u32[]{:S(2)}, u32[]{:S(2)}) collective-permute-start(f32[16,32,256]{2,1,0:T(8,128)S(1)} %all-to-all-done.1.refs_0_), channel_id=1, source_target_pairs={{0,8},{8,0},{16,24},{24,16},{32,40},{40,32},{48,56},{56,48},{64,72... | collective-permute-start | bytes 1572872 | tf_op jit(solution)/shard_map/ppermute | solution.py:226
  122.8 13.2 %collective-permute-done.20.refs_3_.refs_5_ = f32[4,256,128]{2,1,0:T(8,128)S(1)} collective-permute-done((f32[4,256,128]{2,1,0:T(8,128)S(1)}, f32[4,256,128]{2,1,0:T(8,128)S(1)}, u32[]{:S(2)}, u32[]{:S(2)}) %collective-permute-start.20) | collective-permute-done | bytes 524320 | tf_op jit(solution)/shard_map/ppermute | solution.py:264
  136.1 0.7 copy-done.5
  137.0 1.7 pack.1.refs_10_
  138.7 1.7 collective-permute-start.21
  141.0 0.9 collective-permute-done.21.refs_6_
  142.0 1.0 collective-permute-done.22.refs_7_
  142.9 0.7 collective-permute-done.23.refs_8_
  143.7 0.7 collective-permute-done.24.refs_9_
  144.5 0.8 copy-done.12
  145.3 14.7 %chain.1 = f32[8,32,256]{2,1,0:T(8,128)} custom-call(f32[16,32,256]{2,1,0:T(8,128)} %copy-done.7, f32[16,32,256]{2,1,0:T(8,128)} %copy-done.6, f32[4,256,128]{2,1,0:T(8,128)} %pad_maximum_fusion._.refs_2_, f32[4,256,128]{2,1,0:T(8,128)} %copy-done.3, f32[4,256,128]{2,1,0:T(8,128)} %copy-done.4, f32[4,256,128]{2,1,0:T(8,128)} %copy-done.5, ...), custom_call_target="tpu_custom_call" | custom-call | flops 301989888 | bytes 8388608 | tf_op jit(solution)/shard_map/chain/pallas_call | solution.py:349
  159.9 20.4 %all_to_all.15 = f32[8,32,256]{2,1,0:T(8,128)} all-to-all(f32[8,32,256]{2,1,0:T(8,128)} %chain.1), channel_id=1, replica_groups=mesh['wide'=32,'narrow'=8] {'narrow'}, dimensions={0} | all-to-all | bytes 524288 | tf_op jit(solution)/shard_map/all_to_all | solution.py:364
  180.4 5.1 %final.1 = (f32[512,256]{1,0:T(8,128)}, f32[256,256]{1,0:T(8,128)}) custom-call(s32[2,4]{1,0:T(2,128)} %bitcast.22, s32[1,8]{1,0:T(1,128)} %owners.5, bf16[256,256]{1,0:T(8,128)(2,1)} %reduce-scatter.5.cloned.1.call-done.kept, bf16[8,512,256]{2,1,0:T(8,128)(2,1)} %bitcast.13, f32[256,256]{1,0:T(8,128)} %bitcast.14, bf16[4,2,128,128]{3,2,1,0:T(8,128)(2,1)} %cpl.3, ...), custom_call_target="tpu_custom_call" | custom-call | flops 335544320 | bytes 6291456 | tf_op jit(solution)/shard_map/final/pallas_call | solution.py:366
  (78 shorter events, 4.3 us)
Async XLA Ops:
  7.2 64.2 %reduce-scatter.3.cloned.1.call-start = ((), (), s32[]{:S(2)}) async-start(), calls=%async_computation.5 | async-start | bytes 1179648 | tf_op jit(solution)/shard_map/reduce_scatter | solution.py:308
  12.8 123.2 %reduce-scatter.5.cloned.1.call-start = ((), (), s32[]{:S(2)}) async-start(), calls=%async_computation.6 | async-start | bytes 1179648 | tf_op jit(solution)/shard_map/reduce_scatter | solution.py:328
  16.5 29.0 %copy-start.1 = (bf16[288,256]{1,0:T(8,128)(2,1)}, bf16[288,256]{1,0:T(8,128)(2,1)S(1)}, u32[]{:S(2)}) copy-start(bf16[288,256]{1,0:T(8,128)(2,1)S(1)} %get-tuple-element.21.local) | copy-start | bytes 442372
  16.5 10.0 %collective-permute-start = (bf16[288,256]{1,0:T(8,128)(2,1)S(1)}, bf16[288,256]{1,0:T(8,128)(2,1)S(1)}, u32[]{:S(2)}, u32[]{:S(2)}) collective-permute-start(bf16[288,256]{1,0:T(8,128)(2,1)S(1)} %get-tuple-element.14), channel_id=1, source_target_pairs={{0,1},{1,2},{2,3},{3,4},{4,5},{5,6},{6,7},{7,0},{8,9},{9,10},{10,1... | collective-permute-start | bytes 442376 | tf_op jit(solution)/shard_map/ppermute | solution.py:231
  19.1 7.6 %collective-permute-start.4 = (bf16[288,256]{1,0:T(8,128)(2,1)S(1)}, bf16[288,256]{1,0:T(8,128)(2,1)S(1)}, u32[]{:S(2)}, u32[]{:S(2)}) collective-permute-start(bf16[288,256]{1,0:T(8,128)(2,1)S(1)} %get-tuple-element.18), channel_id=1, source_target_pairs={{0,7},{1,0},{2,1},{3,2},{4,3},{5,4},{6,5},{7,6},{8,15},{9,8},{10,9... | collective-permute-start | bytes 442376 | tf_op jit(solution)/shard_map/ppermute | solution.py:231
  26.6 6.4 %collective-permute-start.1 = (bf16[288,256]{1,0:T(8,128)(2,1)S(1)}, bf16[288,256]{1,0:T(8,128)(2,1)S(1)}, u32[]{:S(2)}, u32[]{:S(2)}) collective-permute-start(bf16[288,256]{1,0:T(8,128)(2,1)S(1)} %add_convert_fusion.4), channel_id=1, source_target_pairs={{0,1},{1,2},{2,3},{3,4},{4,5},{5,6},{6,7},{7,0},{8,9},{9,10},{10,1... | collective-permute-start | bytes 442376 | tf_op jit(solution)/shard_map/ppermute | solution.py:231
  26.8 6.7 %collective-permute-start.5 = (bf16[288,256]{1,0:T(8,128)(2,1)S(1)}, bf16[288,256]{1,0:T(8,128)(2,1)S(1)}, u32[]{:S(2)}, u32[]{:S(2)}) collective-permute-start(bf16[288,256]{1,0:T(8,128)(2,1)S(1)} %add_convert_fusion.1), channel_id=1, source_target_pairs={{0,7},{1,0},{2,1},{3,2},{4,3},{5,4},{6,5},{7,6},{8,15},{9,8},{10,9... | collective-permute-start | bytes 442376 | tf_op jit(solution)/shard_map/ppermute | solution.py:231
  33.0 5.6 %collective-permute-start.2 = (bf16[288,256]{1,0:T(8,128)(2,1)S(1)}, bf16[288,256]{1,0:T(8,128)(2,1)S(1)}, u32[]{:S(2)}, u32[]{:S(2)}) collective-permute-start(bf16[288,256]{1,0:T(8,128)(2,1)S(1)} %add_convert_fusion.3), channel_id=1, source_target_pairs={{0,1},{1,2},{2,3},{3,4},{4,5},{5,6},{6,7},{7,0},{8,9},{9,10},{10,1... | collective-permute-start | bytes 442376 | tf_op jit(solution)/shard_map/ppermute | solution.py:231
  33.4 6.9 %collective-permute-start.6 = (bf16[288,256]{1,0:T(8,128)(2,1)S(1)}, bf16[288,256]{1,0:T(8,128)(2,1)S(1)}, u32[]{:S(2)}, u32[]{:S(2)}) collective-permute-start(bf16[288,256]{1,0:T(8,128)(2,1)S(1)} %add_convert_fusion), channel_id=1, source_target_pairs={{0,7},{1,0},{2,1},{3,2},{4,3},{5,4},{6,5},{7,6},{8,15},{9,8},{10,9... | collective-permute-start | bytes 442376 | tf_op jit(solution)/shard_map/ppermute | solution.py:231
  38.7 6.8 %collective-permute-start.3 = (bf16[288,256]{1,0:T(8,128)(2,1)S(1)}, bf16[288,256]{1,0:T(8,128)(2,1)S(1)}, u32[]{:S(2)}, u32[]{:S(2)}) collective-permute-start(bf16[288,256]{1,0:T(8,128)(2,1)S(1)} %add_convert_fusion.2), channel_id=1, source_target_pairs={{0,1},{1,2},{2,3},{3,4},{4,5},{5,6},{6,7},{7,0},{8,9},{9,10},{10,1... | collective-permute-start | bytes 442376 | tf_op jit(solution)/shard_map/ppermute | solution.py:231
  40.4 5.1 %copy-start.13 = (bf16[288,256]{1,0:T(8,128)(2,1)}, bf16[288,256]{1,0:T(8,128)(2,1)S(1)}, u32[]{:S(2)}) copy-start(bf16[288,256]{1,0:T(8,128)(2,1)S(1)} %collective-permute-done.6.left) | copy-start | bytes 442372
  47.3 24.1 %copy-start = (bf16[288,256]{1,0:T(8,128)(2,1)}, bf16[288,256]{1,0:T(8,128)(2,1)S(1)}, u32[]{:S(2)}) copy-start(bf16[288,256]{1,0:T(8,128)(2,1)S(1)} %sum_own.1.refs_0_) | copy-start | bytes 442372
  47.3 6.0 %collective-permute-start.10 = (bf16[288,256]{1,0:T(8,128)(2,1)S(1)}, bf16[288,256]{1,0:T(8,128)(2,1)S(1)}, u32[]{:S(2)}, u32[]{:S(2)}) collective-permute-start(bf16[288,256]{1,0:T(8,128)(2,1)S(1)} %sum_own.1.refs_0_), channel_id=1, source_target_pairs={{0,1},{1,2},{2,3},{3,4},{4,5},{5,6},{6,7},{7,0},{8,9},{9,10},{10,1... | collective-permute-start | bytes 442376 | tf_op jit(solution)/shard_map/ppermute | solution.py:231
  47.6 5.6 %collective-permute-start.7 = (bf16[288,256]{1,0:T(8,128)(2,1)S(1)}, bf16[288,256]{1,0:T(8,128)(2,1)S(1)}, u32[]{:S(2)}, u32[]{:S(2)}) collective-permute-start(bf16[288,256]{1,0:T(8,128)(2,1)S(1)} %sum_own.1.refs_0_), channel_id=1, source_target_pairs={{0,7},{1,0},{2,1},{3,2},{4,3},{5,4},{6,5},{7,6},{8,15},{9,8},{10,9... | collective-permute-start | bytes 442376 | tf_op jit(solution)/shard_map/ppermute | solution.py:231
  53.3 18.1 %copy-start.15 = (bf16[288,256]{1,0:T(8,128)(2,1)}, bf16[288,256]{1,0:T(8,128)(2,1)S(1)}, u32[]{:S(2)}) copy-start(bf16[288,256]{1,0:T(8,128)(2,1)S(1)} %collective-permute-done.10.refs_7_) | copy-start | bytes 442372
  53.3 6.9 %collective-permute-start.11 = (bf16[288,256]{1,0:T(8,128)(2,1)S(1)}, bf16[288,256]{1,0:T(8,128)(2,1)S(1)}, u32[]{:S(2)}, u32[]{:S(2)}) collective-permute-start(bf16[288,256]{1,0:T(8,128)(2,1)S(1)} %collective-permute-done.10.refs_7_), channel_id=1, source_target_pairs={{0,1},{1,2},{2,3},{3,4},{4,5},{5,6},{6,7},{7,0},{8,9},{9,10},{10,1... | collective-permute-start | bytes 442376 | tf_op jit(solution)/shard_map/ppermute | solution.py:231
  53.3 18.1 %copy-start.16 = (bf16[288,256]{1,0:T(8,128)(2,1)}, bf16[288,256]{1,0:T(8,128)(2,1)S(1)}, u32[]{:S(2)}) copy-start(bf16[288,256]{1,0:T(8,128)(2,1)S(1)} %collective-permute-done.7.refs_1_) | copy-start | bytes 442372
  53.3 6.9 %collective-permute-start.8 = (bf16[288,256]{1,0:T(8,128)(2,1)S(1)}, bf16[288,256]{1,0:T(8,128)(2,1)S(1)}, u32[]{:S(2)}, u32[]{:S(2)}) collective-permute-start(bf16[288,256]{1,0:T(8,128)(2,1)S(1)} %collective-permute-done.7.refs_1_), channel_id=1, source_target_pairs={{0,7},{1,0},{2,1},{3,2},{4,3},{5,4},{6,5},{7,6},{8,15},{9,8},{10,9... | collective-permute-start | bytes 442376 | tf_op jit(solution)/shard_map/ppermute | solution.py:231
  60.1 11.2 %copy-start.17 = (bf16[288,256]{1,0:T(8,128)(2,1)}, bf16[288,256]{1,0:T(8,128)(2,1)S(1)}, u32[]{:S(2)}) copy-start(bf16[288,256]{1,0:T(8,128)(2,1)S(1)} %collective-permute-done.11.refs_6_) | copy-start | bytes 442372
  60.1 6.0 %collective-permute-start.12 = (bf16[288,256]{1,0:T(8,128)(2,1)S(1)}, bf16[288,256]{1,0:T(8,128)(2,1)S(1)}, u32[]{:S(2)}, u32[]{:S(2)}) collective-permute-start(bf16[288,256]{1,0:T(8,128)(2,1)S(1)} %collective-permute-done.11.refs_6_), channel_id=1, source_target_pairs={{0,1},{1,2},{2,3},{3,4},{4,5},{5,6},{6,7},{7,0},{8,9},{9,10},{10,1... | collective-permute-start | bytes 442376 | tf_op jit(solution)/shard_map/ppermute | solution.py:231
  60.1 11.2 %copy-start.18 = (bf16[288,256]{1,0:T(8,128)(2,1)}, bf16[288,256]{1,0:T(8,128)(2,1)S(1)}, u32[]{:S(2)}) copy-start(bf16[288,256]{1,0:T(8,128)(2,1)S(1)} %collective-permute-done.8.refs_2_) | copy-start | bytes 442372
  60.2 6.0 %collective-permute-start.9 = (bf16[288,256]{1,0:T(8,128)(2,1)S(1)}, bf16[288,256]{1,0:T(8,128)(2,1)S(1)}, u32[]{:S(2)}, u32[]{:S(2)}) collective-permute-start(bf16[288,256]{1,0:T(8,128)(2,1)S(1)} %collective-permute-done.8.refs_2_), channel_id=1, source_target_pairs={{0,7},{1,0},{2,1},{3,2},{4,3},{5,4},{6,5},{7,6},{8,15},{9,8},{10,9... | collective-permute-start | bytes 442376 | tf_op jit(solution)/shard_map/ppermute | solution.py:231
  66.1 5.3 %copy-start.19 = (bf16[288,256]{1,0:T(8,128)(2,1)}, bf16[288,256]{1,0:T(8,128)(2,1)S(1)}, u32[]{:S(2)}) copy-start(bf16[288,256]{1,0:T(8,128)(2,1)S(1)} %collective-permute-done.12.refs_5_) | copy-start | bytes 442372
  66.1 5.2 %collective-permute-start.13 = (bf16[288,256]{1,0:T(8,128)(2,1)S(1)}, bf16[288,256]{1,0:T(8,128)(2,1)S(1)}, u32[]{:S(2)}, u32[]{:S(2)}) collective-permute-start(bf16[288,256]{1,0:T(8,128)(2,1)S(1)} %collective-permute-done.12.refs_5_), channel_id=1, source_target_pairs={{0,1},{1,2},{2,3},{3,4},{4,5},{5,6},{6,7},{7,0},{8,9},{9,10},{10,1... | collective-permute-start | bytes 442376 | tf_op jit(solution)/shard_map/ppermute | solution.py:231
  66.2 5.2 %copy-start.20 = (bf16[288,256]{1,0:T(8,128)(2,1)}, bf16[288,256]{1,0:T(8,128)(2,1)S(1)}, u32[]{:S(2)}) copy-start(bf16[288,256]{1,0:T(8,128)(2,1)S(1)} %collective-permute-done.9.refs_3_) | copy-start | bytes 442372
  76.2 19.4 %all-to-all-start = ((f32[8,32,256]{2,1,0:T(8,128)}), f32[8,32,256]{2,1,0:T(8,128)S(1)}, u32[]{:S(2)}, u32[]{:S(2)}) async-start(f32[8,32,256]{2,1,0:T(8,128)} %bitcast.16), calls=%async_computation.2 | async-start | bytes 524288 | tf_op jit(solution)/shard_map/all_to_all | solution.py:334
  84.3 6.3 %collective-permute-start.14 = (f32[256,128]{1,0:T(8,128)}, f32[256,128]{1,0:T(8,128)S(1)}, u32[]{:S(2)}, u32[]{:S(2)}) collective-permute-start(f32[256,128]{1,0:T(8,128)} %get-tuple-element.24), channel_id=1, source_target_pairs={{16,0},{24,8},{32,16},{40,24},{48,32},{56,40},{0,48},{8,56},{80,64... | collective-permute-start | bytes 393224 | tf_op jit(solution)/shard_map/ppermute | solution.py:264
  86.9 5.6 %collective-permute-start.15 = (f32[256,128]{1,0:T(8,128)}, f32[256,128]{1,0:T(8,128)S(1)}, u32[]{:S(2)}, u32[]{:S(2)}) collective-permute-start(f32[256,128]{1,0:T(8,128)} %get-tuple-element.24), channel_id=1, source_target_pairs={{32,0},{40,8},{48,16},{56,24},{0,32},{8,40},{16,48},{24,56},{96,64... | collective-permute-start | bytes 393224 | tf_op jit(solution)/shard_map/ppermute | solution.py:264
  87.2 6.6 %collective-permute-start.16 = (f32[256,128]{1,0:T(8,128)}, f32[256,128]{1,0:T(8,128)S(1)}, u32[]{:S(2)}, u32[]{:S(2)}) collective-permute-start(f32[256,128]{1,0:T(8,128)} %get-tuple-element.24), channel_id=1, source_target_pairs={{48,0},{56,8},{0,16},{8,24},{16,32},{24,40},{32,48},{40,56},{112,6... | collective-permute-start | bytes 393224 | tf_op jit(solution)/shard_map/ppermute | solution.py:264
  95.6 8.0 %copy-start.2 = (f32[4,256,128]{2,1,0:T(8,128)S(1)}, f32[4,256,128]{2,1,0:T(8,128)}, u32[]{:S(2)}) copy-start(f32[4,256,128]{2,1,0:T(8,128)} %pad_maximum_fusion._.refs_2_) | copy-start | bytes 1572868
  98.2 14.7 %all-to-all-start.1 = ((f32[16,32,256]{2,1,0:T(8,128)}), f32[16,32,256]{2,1,0:T(8,128)S(1)}, u32[]{:S(2)}, u32[]{:S(2)}) async-start(f32[16,32,256]{2,1,0:T(8,128)} %small_sum.1), calls=%async_computation.3 | async-start | bytes 1048576 | tf_op jit(solution)/shard_map/all_to_all | solution.py:343
  103.5 76.8 %all-gather.3.cloned.1.call-start = ((), (), s32[]{:S(2)}) async-start(), calls=%async_computation.7 | async-start | bytes 2359296 | tf_op jit(solution)/shard_map/all_gather | solution.py:348
  103.6 19.2 %collective-permute-start.18 = (f32[4,256,128]{2,1,0:T(8,128)S(1)}, f32[4,256,128]{2,1,0:T(8,128)S(1)}, u32[]{:S(2)}, u32[]{:S(2)}) collective-permute-start(f32[4,256,128]{2,1,0:T(8,128)S(1)} %copy-done.2), channel_id=1, source_target_pairs={{64,0},{72,8},{80,16},{88,24},{96,32},{104,40},{112,48},{120,56},{... | collective-permute-start | bytes 1572872 | tf_op jit(solution)/shard_map/ppermute | solution.py:264
  106.2 16.6 %collective-permute-start.19 = (f32[4,256,128]{2,1,0:T(8,128)S(1)}, f32[4,256,128]{2,1,0:T(8,128)S(1)}, u32[]{:S(2)}, u32[]{:S(2)}) collective-permute-start(f32[4,256,128]{2,1,0:T(8,128)S(1)} %copy-done.2), channel_id=1, source_target_pairs={{128,0},{136,8},{144,16},{152,24},{160,32},{168,40},{176,48},{184,... | collective-permute-start | bytes 1572872 | tf_op jit(solution)/shard_map/ppermute | solution.py:264
  106.8 29.2 %collective-permute-start.20 = (f32[4,256,128]{2,1,0:T(8,128)S(1)}, f32[4,256,128]{2,1,0:T(8,128)S(1)}, u32[]{:S(2)}, u32[]{:S(2)}) collective-permute-start(f32[4,256,128]{2,1,0:T(8,128)S(1)} %copy-done.2), channel_id=1, source_target_pairs={{192,0},{200,8},{208,16},{216,24},{224,32},{232,40},{240,48},{248,... | collective-permute-start | bytes 1572872 | tf_op jit(solution)/shard_map/ppermute | solution.py:264
  112.9 31.5 %copy-start.7 = (f32[16,32,256]{2,1,0:T(8,128)}, f32[16,32,256]{2,1,0:T(8,128)S(1)}, u32[]{:S(2)}) copy-start(f32[16,32,256]{2,1,0:T(8,128)S(1)} %all-to-all-done.1.refs_0_) | copy-start | bytes 1572868
  112.9 23.1 %collective-permute-start.17 = (f32[16,32,256]{2,1,0:T(8,128)S(1)}, f32[16,32,256]{2,1,0:T(8,128)S(1)}, u32[]{:S(2)}, u32[]{:S(2)}) collective-permute-start(f32[16,32,256]{2,1,0:T(8,128)S(1)} %all-to-all-done.1.refs_0_), channel_id=1, source_target_pairs={{0,8},{8,0},{16,24},{24,16},{32,40},{40,32},{48,56},{56,48},{64,72... | collective-permute-start | bytes 1572872 | tf_op jit(solution)/shard_map/ppermute | solution.py:226
  122.8 13.3 %copy-start.3 = (f32[4,256,128]{2,1,0:T(8,128)}, f32[4,256,128]{2,1,0:T(8,128)S(1)}, u32[]{:S(2)}) copy-start(f32[4,256,128]{2,1,0:T(8,128)S(1)} %collective-permute-done.18.refs_1_.refs_3_) | copy-start | bytes 1572868
  122.8 13.3 %copy-start.4 = (f32[4,256,128]{2,1,0:T(8,128)}, f32[4,256,128]{2,1,0:T(8,128)S(1)}, u32[]{:S(2)}) copy-start(f32[4,256,128]{2,1,0:T(8,128)S(1)} %collective-permute-done.19.refs_2_.refs_4_) | copy-start | bytes 1572868
  136.0 0.8 copy-start.5
  136.0 1.0 copy-start.6
  138.7 3.2 %collective-permute-start.21 = (f32[4,256,128]{2,1,0:T(8,128)S(1)}, f32[4,256,128]{2,1,0:T(8,128)S(1)}, u32[]{:S(2)}, u32[]{:S(2)}) collective-permute-start(f32[4,256,128]{2,1,0:T(8,128)S(1)} %copy-done.2), channel_id=1, source_target_pairs={{0,8},{8,0},{16,24},{24,16},{32,40},{40,32},{48,56},{56,48},{64,72... | collective-permute-start | bytes 1572872 | tf_op jit(solution)/shard_map/ppermute | solution.py:226
  140.4 2.5 %collective-permute-start.22 = (f32[4,256,128]{2,1,0:T(8,128)}, f32[4,256,128]{2,1,0:T(8,128)S(1)}, u32[]{:S(2)}, u32[]{:S(2)}) collective-permute-start(f32[4,256,128]{2,1,0:T(8,128)} %copy-done.3), channel_id=1, source_target_pairs={{0,8},{8,0},{16,24},{24,16},{32,40},{40,32},{48,56},{56,48},{64,72... | collective-permute-start | bytes 1572872 | tf_op jit(solution)/shard_map/ppermute | solution.py:226
  140.5 3.1 %collective-permute-start.23 = (f32[4,256,128]{2,1,0:T(8,128)}, f32[4,256,128]{2,1,0:T(8,128)S(1)}, u32[]{:S(2)}, u32[]{:S(2)}) collective-permute-start(f32[4,256,128]{2,1,0:T(8,128)} %copy-done.4), channel_id=1, source_target_pairs={{0,8},{8,0},{16,24},{24,16},{32,40},{40,32},{48,56},{56,48},{64,72... | collective-permute-start | bytes 1572872 | tf_op jit(solution)/shard_map/ppermute | solution.py:226
  140.9 3.5 %collective-permute-start.24 = (f32[4,256,128]{2,1,0:T(8,128)}, f32[4,256,128]{2,1,0:T(8,128)S(1)}, u32[]{:S(2)}, u32[]{:S(2)}) collective-permute-start(f32[4,256,128]{2,1,0:T(8,128)} %copy-done.5), channel_id=1, source_target_pairs={{0,8},{8,0},{16,24},{24,16},{32,40},{40,32},{48,56},{56,48},{64,72... | collective-permute-start | bytes 1572872 | tf_op jit(solution)/shard_map/ppermute | solution.py:226
  142.0 2.5 %copy-start.9 = (f32[4,256,128]{2,1,0:T(8,128)}, f32[4,256,128]{2,1,0:T(8,128)S(1)}, u32[]{:S(2)}) copy-start(f32[4,256,128]{2,1,0:T(8,128)S(1)} %collective-permute-done.21.refs_6_) | copy-start | bytes 1572868
  142.9 1.5 copy-start.10
  143.7 0.8 copy-start.11
  (4 other events, 2.8 us)
Sparse Core Ops, SparseCore 0:
  12.9 40.1 reduce-scatter.2
  76.3 44.3 reduce-scatter.4
  138.9 41.4 all-gather.2

commit v3 on v2

--- a/solution.py
+++ b/solution.py
@@ -61,11 +61,9 @@
     return group
 
 
-def leaf_forward_kernel(parent, owners, rhs, inv, cpl, sep_rhs, sep_inv, fl, *refs):
-    blocks = refs[:-3]
-    acc, head, sem = refs[-3:]
-    fetch = pltpu.make_async_copy(sep_inv.at[:, pl.ds(0, head.shape[1])], head, sem)
-    fetch.start()
+def leaf_forward_kernel(parent, owners, rhs, inv, cpl, sep_rhs, sep_inv, fl, shared, *refs):
+    blocks = refs[:-1]
+    acc = refs[-1]
     b = inv.shape[1]
     rows = sep_rhs.shape[0]
     n = len(blocks)
@@ -79,12 +77,19 @@
         for k in range(cpl.shape[1]):
             at = pl.ds(pl.multiple_of(parent[k, i] * b, b), b)
             acc[at, :] -= mm(cpl[i, k], f, NN)
-    fetch.wait()
-    corner_hi, corner_lo = halves(mm(head[...], head[...], TN))
+    head = sep_inv[:, :b]
+    corner_hi, corner_lo = halves(mm(head, head, TN))
     acc[n * rows : n * rows + b, :b] = corner_hi.astype(F32)
     acc[n * rows : n * rows + b, b:] = corner_lo.astype(F32)
-    tail = head[rows - b :, :].astype(F32)
-    acc[n * rows + b :, :b] = jnp.where(owners[0, n - 1] == me, tail, 0.0)
+    holds_last = owners[0, n - 1] == me
+    acc[n * rows + b :, :b] = jnp.where(holds_last, head[rows - b :, :].astype(F32), 0.0)
+    rows_at = lax.broadcasted_iota(jnp.int32, (rows, b), 0)
+    cols_at = lax.broadcasted_iota(jnp.int32, (rows, b), 1)
+    pick = jnp.where(holds_last & (rows_at == cols_at + (rows - b)), 1.0, 0.0).astype(BF)
+    ends = jnp.concatenate([head, pick], axis=1)
+    for g in range(n):
+        at = slice(g * rows, (g + 1) * rows)
+        shared[at, :] = mm(sep_inv[:, at], ends, TN).astype(BF)
     step = b // n
     for j in range(n):
         g = lax.rem(me + j, n)
@@ -110,17 +115,10 @@
     out[rows + step :, b:] = corner_lo
 
 
-def pack_kernel(kept, shared, *refs):
-    packed = refs[-1]
-    rows = kept.shape[0]
-    packed[:rows, :] = kept[...]
-    packed[rows:, :] = shared[...]
-
-
 def middle_kernel(owners, inv, *refs):
     n = 8
     coupled = refs[:n]
-    link, _, ag, terms, maps, whole, corner, tail = refs[n:]
+    link, _, terms, maps, whole, corner, tail = refs[n:]
     me = lax.axis_index("narrow")
     rows = inv.shape[0]
     b = rows // 2
@@ -136,30 +134,58 @@
         ].astype(F32)
     applied = mm(inv[...], whole[...], NN)
     app = applied.astype(BF)
+    first_hi, first_lo = halves(mm(tail[...], link[...], NN))
+    maps[:b, :] = first_hi
+    maps[b : 2 * b, :] = first_lo
+    inner = mm2(corner[...], link[...], NN)
+    maps[2 * b :, :] = mm2(inner, link[...], TN).astype(BF)
     for g in range(n):
-        terms[owners[0, g]] = mm(inv[:, g * rows : (g + 1) * rows], app, TN).astype(BF)
-    ag[:, :b] = jnp.where(owners[0, n - 1] == me, applied[rows - b :, :], 0.0).T
-    ag[:, b:] = mm(app, inv[:, :b], TN)
-    maps[:b, :] = mm(tail[...], link[...], NN)
-    inner = mm2(corner[...], link[...], NN)
-    maps[b:, :] = mm2(inner, link[...], TN)
-
-
-def small_sum_kernel(parts, link, _, spread):
+        block = mm(inv[:, g * rows : (g + 1) * rows], app, TN).astype(BF)
+        terms[owners[0, g], :rows, :] = block
+    state_hi, state_lo = halves(jnp.where(owners[0, n - 1] == me, applied[rows - b :, :], 0.0).T)
+    head_hi, head_lo = halves(mm(app, inv[:, :b], TN))
+    cols = (terms.shape[1] - rows) // 2
+    for j in range(n):
+        at = slice(j * cols, (j + 1) * cols)
+        terms[j, rows : rows + cols, :b] = state_hi[at]
+        terms[j, rows : rows + cols, b:] = head_hi[at]
+        terms[j, rows + cols :, :b] = state_lo[at]
+        terms[j, rows + cols :, b:] = head_lo[at]
+
+
+def sum_terms_kernel(parts, shared, link, *refs):
+    kept, packed, spread = refs[-3:]
+    rows = kept.shape[0]
     b = link.shape[0]
-    total = parts[0]
+    cols = spread.shape[1]
+    total = parts[0].astype(F32)
     for j in range(1, parts.shape[0]):
-        total += parts[j]
-    moved = mm2(total[:, b:], link[...], NN)
+        total += parts[j].astype(F32)
+    kept[...] = total[:rows]
+    packed[:rows, :] = total[:rows].astype(BF)
+    packed[rows:, :] = shared[...]
+    ends = total[rows : rows + cols] + total[rows + cols :]
+    head = mm2(ends[:, b:], link[...], NN)
     for j in range(spread.shape[0]):
-        spread[j, :, :b] = total[:, :b]
-        spread[j, :, b:] = moved
+        spread[j, :, :b] = ends[:, :b]
+        spread[j, :, b:] = head
+
+
+def stack_kernel(*refs):
+    out = refs[-1]
+    for j in range(out.shape[0]):
+        out[j] = refs[j][...]
+
+
+def times_map(value, hi, lo, dims):
+    vh, vl = halves(value)
+    return mm(vh, hi, dims) + (mm(vl, hi, dims) + mm(vh, lo, dims))
 
 
 def chain_kernel(*refs):
-    ag_own, ag_other = refs[:2]
-    maps_own, maps_other = refs[2:6], refs[6:10]
-    link, out, ag, maps, states, incoming, sems = refs[11:]
+    ags = refs[:2]
+    mapss = refs[2:6], refs[6:10]
+    link, out, ag, maps, states, incoming, sems = refs[10:]
     b = link.shape[0]
     length = states.shape[0]
     wide = lax.axis_index("wide")
@@ -167,12 +193,12 @@
     x = lax.rem(lax.div(wide, 2), 4)
     y = lax.div(wide, 8)
     copies = []
-    for side, ag_part, parts in ((here, ag_own, maps_own), (1 - here, ag_other, maps_other)):
+    for side, ag_part, map_parts in ((here, ags[0], mapss[0]), (1 - here, ags[1], mapss[1])):
         copies.append((ag_part, ag.at[side]))
         for j in range(4):
             for k in range(4):
                 at = lax.rem(y + j, 4) * 4 + lax.rem(x + k, 4)
-                copies.append((parts[j].at[k], maps.at[side, at]))
+                copies.append((map_parts[j].at[k], maps.at[side, at]))
     copies = [pltpu.make_async_copy(p, q, sems.at[i]) for i, (p, q) in enumerate(copies)]
     for copy in copies:
         copy.start()
@@ -182,17 +208,24 @@
     for w in range(length):
         states[w] = state
         if w + 1 < length:
-            state = ag[w % 2, w // 2, :, :b] - mm3(state, maps[w % 2, w // 2, :b, :], NT)
+            at = (w % 2, w // 2)
+            moved = times_map(state, maps[(*at, slice(0, b))], maps[(*at, slice(b, 2 * b))], NT)
+            state = ag[(*at, slice(None), slice(0, b))] - moved
     back = jnp.zeros_like(state)
     for w in range(length - 1, -1, -1):
         incoming[w] = back
         if w > 0:
-            local = ag[w % 2, w // 2, :, b:] - mm3(states[w], maps[w % 2, w // 2, b:, :], NN)
-            back = local - mm3(back, maps[w % 2, w // 2, :b, :], NN)
+            at = (w % 2, w // 2)
+            vh, vl = halves(states[w])
+            corner = maps[(*at, slice(2 * b, 3 * b))]
+            local = ag[(*at, slice(None), slice(b, 2 * b))] - (mm(vh, corner, NN) + mm(vl, corner, NN))
+            moved = times_map(back, maps[(*at, slice(0, b))], maps[(*at, slice(b, 2 * b))], NN)
+            back = local - moved
     mine = mm2(states[wide], link[...], NT)
+    last = incoming[wide]
     for j in range(out.shape[0]):
         out[j, :, :b] = mine
-        out[j, :, b:] = incoming[wide]
+        out[j, :, b:] = last
 
 
 def final_kernel(
@@ -208,7 +241,7 @@
         part = gathered[g, pl.ds(rows + start, count), :]
         return mm(part, zs[0], NT) + mm(part, zs[1], NT)
 
-    sep_out[...] = kept[...].astype(F32) - fix(held_group(owners), 0, rows)
+    sep_out[...] = kept[...] - fix(held_group(owners), 0, rows)
     for i in range(inv.shape[0]):
         acc = fl[i * b : (i + 1) * b, :].astype(F32)
         for k in range(cpl.shape[1]):
@@ -281,16 +314,13 @@
     held = pltpu.VMEM
 
     extra = rows + 2 * (b // n)
-    fl, *blocks = call(
+    fl, shared, *blocks = call(
         leaf_forward_kernel,
         "leaf_forward",
-        (shape((leaf_count * b, sketch), BF),) + (held((extra, sketch), BF),) * n,
-        [SMEM] * 2 + [VMEM] * 4 + [ANY],
-        [
-            pltpu.VMEM((all_rows + 2 * b, sketch), F32),
-            pltpu.VMEM((rows, b), BF),
-            pltpu.SemaphoreType.DMA,
-        ],
+        (shape((leaf_count * b, sketch), BF), shape((all_rows, 2 * b), BF))
+        + (held((extra, sketch), BF),) * n,
+        [SMEM] * 2 + [VMEM] * 5,
+        [pltpu.VMEM((all_rows + 2 * b, sketch), F32)],
         flops=2 * 12 * b * b * sketch,
         moved=4 << 20,
     )(parent, row_owner, leaf_rhs, leaf_inv, leaf_coupling, sep_rhs, sep_inv)
@@ -300,67 +330,54 @@
     )
     coupled = ring_gather(own)
 
-    rows_at = lax.broadcasted_iota(jnp.int32, (rows, b), 0)
-    cols_at = lax.broadcasted_iota(jnp.int32, (rows, b), 1)
-    last = row_owner[0, n - 1] == lax.axis_index("narrow")
-    pick = jnp.where(last & (rows_at == cols_at + (rows - b)), 1.0, 0.0).astype(BF)
-    shared = mm(sep_inv, jnp.concatenate([sep_inv[:, :b], pick], axis=1), TN).astype(BF)
     shared = lax.psum_scatter(shared, "narrow", scatter_dimension=0, tiled=True)
-
-    ag, terms, maps = call(
+    terms, maps = call(
         middle_kernel,
         "middle",
-        (
-            shape((sketch, 2 * b), F32),
-            shape((n, rows, sketch), BF),
-            shape((2 * b, b), F32),
-        ),
+        (shape((n, rows + 2 * cols, sketch), BF), shape((3 * b, b), BF)),
         [SMEM] + [VMEM] * (2 + n) + [ANY],
-        [
-            pltpu.VMEM((all_rows, sketch), BF),
-            pltpu.VMEM((b, b), F32),
-            pltpu.VMEM((b, b), BF),
-        ],
+        [pltpu.VMEM((all_rows, sketch), BF), pltpu.VMEM((b, b), F32), pltpu.VMEM((b, b), BF)],
         flops=4 * rows * all_rows * sketch,
         moved=4 << 20,
     )(row_owner, sep_inv, *coupled, sep_link, shared)
-
-    kept = lax.psum_scatter(
-        terms.reshape(all_rows, sketch), "narrow", scatter_dimension=0, tiled=True
+    maps = call(stack_kernel, "stack_maps", shape((4, 3 * b, b), BF), [VMEM] * 4, moved=1 << 18)(
+        maps, *[turned_wide(maps, "x", k) for k in (1, 2, 3)]
     )
-    maps = jnp.stack([maps] + [turned_wide(maps, "x", k) for k in (1, 2, 3)])
     maps = [maps] + [turned_wide(maps, "y", k) for k in (1, 2, 3)]
     maps_other = [swap(part, "wide", 1) for part in maps]
-    ag = lax.all_to_all(ag.reshape(n, cols, 2 * b), "narrow", 0, 0, tiled=True)
-    ag = call(
-        small_sum_kernel,
-        "small_sum",
-        shape((chips, cols, 2 * b), F32),
-        [VMEM] * 2 + [ANY],
-        moved=1 << 19,
-    )(ag, sep_link, maps[0])
+
+    terms = lax.all_to_all(terms, "narrow", 0, 0, tiled=True)
+    kept, packed, ag = call(
+        sum_terms_kernel,
+        "sum_terms",
+        (
+            shape((rows, sketch), F32),
+            shape((2 * rows, sketch), BF),
+            shape((chips, cols, 2 * b), F32),
+        ),
+        [VMEM] * 3 + [ANY] * 4,
+        moved=2 << 20,
+    )(terms, shared, sep_link, *maps_other)
+    gathered = lax.all_gather(packed, "narrow", axis=0, tiled=False)
+
     same_core = [[2 * q + c for q in range(chips)] for c in range(2)]
     ag = lax.all_to_all(ag, "wide", 0, 0, tiled=True, axis_index_groups=same_core)
-    other = swap(ag, "wide", 1)
-    packed = call(
-        pack_kernel, "pack", shape((2 * rows, sketch), BF), [VMEM] * 2 + [ANY] * 4, moved=1 << 19
-    )(kept, shared, other, *maps[1:])
-    gathered = lax.all_gather(packed, "narrow", axis=0, tiled=False)
+    ag_other = swap(ag, "wide", 1)
     z = call(
         chain_kernel,
         "chain",
         shape((n, cols, 2 * b), F32),
-        [ANY] * 11 + [VMEM],
+        [ANY] * 10 + [VMEM],
         [
             pltpu.VMEM((2, chips, cols, 2 * b), F32),
-            pltpu.VMEM((2, chips, 2 * b, b), F32),
+            pltpu.VMEM((2, chips, 3 * b, b), BF),
             pltpu.VMEM((chain_len, cols, b), F32),
             pltpu.VMEM((chain_len, cols, b), F32),
             pltpu.SemaphoreType.DMA((2 + 2 * chips,)),
         ],
         flops=2 * 9 * chain_len * cols * b * b,
         moved=8 << 20,
-    )(ag, other, *maps, *maps_other, packed, sep_link)
+    )(ag, ag_other, *maps, *maps_other, sep_link)
     z = lax.all_to_all(z, "narrow", 0, 0, tiled=True).reshape(sketch, 2 * b)
 
     leaf_out, sep_out = call(

time: 195 us -> 186 us (0.954); the launches traced: 192 us -> 185 us
  waiting for transfers between devices: 59 us -> 41.3 us
  blocking collectives: 20.4 us -> 32.6 us
  starting transfers between devices: 55 us -> 58.2 us
  matrix products: 2.79 us -> 0 us
    all_to_all x0 -> x1, blocking collectives: none -> 14.5 us  [per_device(): lax.all_to_all(ag, 'wide', 0, 0, tiled=True, axis_index_groups=same_core)]
    ppermute x6, waiting for transfers between devices: 19.1 us -> 4.99 us  [turned_wide(): return lax.ppermute(value, 'wide', [(source(i), i) for i in range(32)])]
    ppermute x5, starting transfers between devices: 12.2 us -> 25.5 us  [swap(): return lax.ppermute(value, axis, [(i, i ^ by) for i in range(n)])]
    all_to_all x2 -> x1, starting transfers between devices: 13.3 us -> 3.7 us  [per_device(): terms = lax.all_to_all(terms, 'narrow', 0, 0, tiled=True)]
    all_to_all x2 -> x1, waiting for transfers between devices: 5.52 us -> 0.01 us  [per_device(): terms = lax.all_to_all(terms, 'narrow', 0, 0, tiled=True)]
    dot_general x1 -> x0, matrix products: 2.79 us -> none  [mm(): return lax.dot_general(a, b, dims, preferred_element_type=F32)]
    ppermute x14, waiting for transfers between devices: 31 us -> 33.4 us  [turned(): return lax.ppermute(value, 'narrow', [(i, (i + by) % n) for i in range(n)])]
    all_to_all x1, blocking collectives: 20.4 us -> 18 us  [per_device(): z = lax.all_to_all(z, 'narrow', 0, 0, tiled=True).reshape(sketch, 2 * b)]
  transfers between devices with their start and end apart: 30 -> 28, of which waited for: 18 -> 14; matrix products, arithmetic and copies ran while one was open for 1% -> 0% of each run, Pallas kernels for 11% -> 9%
where the time goes in v3:
time: 186 us; the launch traced here: 185 us
  starting transfers between devices  58.2 us (31%)
  waiting for transfers between devices  41.3 us (22%)
  Pallas kernels  33.4 us (18%)
  blocking collectives  32.6 us (18%)
  between operations  14.3 us (8%)
  local copies, waits for them, and re-layouts  5.25 us (3%)
    ppermute x14, waiting for transfers between devices, turned(): return lax.ppermute(value, 'narrow', [(i, (i + by) % n) for i in range(n)])  33.4 us
    ppermute x5, starting transfers between devices, swap(): return lax.ppermute(value, axis, [(i, i ^ by) for i in range(n)])  25.5 us
    ppermute x14, starting transfers between devices, turned(): return lax.ppermute(value, 'narrow', [(i, (i + by) % n) for i in range(n)])  20.5 us
    all_to_all x1, blocking collectives, per_device(): z = lax.all_to_all(z, 'narrow', 0, 0, tiled=True).reshape(sketch, 2 * b)  18 us
    all_to_all x1, blocking collectives, per_device(): lax.all_to_all(ag, 'wide', 0, 0, tiled=True, axis_index_groups=same_core)  14.5 us
    pallas_call x1, Pallas kernels, per_device(): call(chain_kernel, 'chain', shape((n, cols, 2 * b), F32), [ANY] * 10 + [V...  14.4 us
    ppermute x6, starting transfers between devices, turned_wide(): return lax.ppermute(value, 'wide', [(source(i), i) for i in range(32)])  8.3 us
    unnamed x50, local copies, waits for them, and re-layouts  5.25 us
  transfers between devices with their start and end apart: 28, of which 14 were waited for; matrix products, arithmetic and copies ran while one was open for 0% of the time, Pallas kernels for 9%

profile of v3, /device:TPU:1, one launch (start us, length us, event | category | flops | bytes accessed | tf_op | source)
XLA Modules:
  0.0 185.1 jit_solution(3739249477385875841)
XLA Ops:
  7.2 4.1 %leaf_forward.1 = (bf16[512,256]{1,0:T(8,128)(2,1)}, bf16[2048,256]{1,0:T(8,128)(2,1)}, bf16[288,256]{1,0:T(8,128)(2,1)S(1)}, bf16[288,256]{1,0:T(8,128)(2,1)S(1...) custom-call(s32[2,4]{1,0:T(2,128)} %bitcast.5, ...), custom_call_target="tpu_custom_call" | custom-call | flops 100663296 | bytes 4194304 | tf_op jit(solution)/shard_map/leaf_forward/pallas_call | solution.py:317
  11.3 0.7 copy-done.1
  12.0 2.5 %collective-permute-start = (bf16[288,256]{1,0:T(8,128)(2,1)S(1)}, bf16[288,256]{1,0:T(8,128)(2,1)S(1)}, u32[]{:S(2)}, u32[]{:S(2)}) collective-permute-start(bf16[288,256]{1,0:T(8,128)(2,1)S(1)} %get-tuple-element.17), channel_id=1, source_target_pairs={{0,1},{1,2},{2,3},{3,4},{4,5},{5,6},{6,7},{7,0},{8,9},{9,10},{10,1... | collective-permute-start | bytes 442376 | tf_op jit(solution)/shard_map/ppermute | solution.py:264
  14.5 4.0 %collective-permute-start.4 = (bf16[288,256]{1,0:T(8,128)(2,1)S(1)}, bf16[288,256]{1,0:T(8,128)(2,1)S(1)}, u32[]{:S(2)}, u32[]{:S(2)}) collective-permute-start(bf16[288,256]{1,0:T(8,128)(2,1)S(1)} %get-tuple-element.21), channel_id=1, source_target_pairs={{0,7},{1,0},{2,1},{3,2},{4,3},{5,4},{6,5},{7,6},{8,15},{9,8},{10,9... | collective-permute-start | bytes 442376 | tf_op jit(solution)/shard_map/ppermute | solution.py:264
  18.6 3.5 %collective-permute-done = bf16[288,256]{1,0:T(8,128)(2,1)S(1)} collective-permute-done((bf16[288,256]{1,0:T(8,128)(2,1)S(1)}, bf16[288,256]{1,0:T(8,128)(2,1)S(1)}, u32[]{:S(2)}, u32[]{:S(2)}) %collective-permute-start) | collective-permute-done | bytes 147488 | tf_op jit(solution)/shard_map/ppermute | solution.py:264
  22.2 2.7 %collective-permute-start.5 = (bf16[288,256]{1,0:T(8,128)(2,1)S(1)}, bf16[288,256]{1,0:T(8,128)(2,1)S(1)}, u32[]{:S(2)}, u32[]{:S(2)}) collective-permute-start(bf16[288,256]{1,0:T(8,128)(2,1)S(1)} %add_convert_fusion.1), channel_id=1, source_target_pairs={{0,7},{1,0},{2,1},{3,2},{4,3},{5,4},{6,5},{7,6},{8,15},{9,8},{10,9... | collective-permute-start | bytes 442376 | tf_op jit(solution)/shard_map/ppermute | solution.py:264
  25.0 2.4 %collective-permute-done.1 = bf16[288,256]{1,0:T(8,128)(2,1)S(1)} collective-permute-done((bf16[288,256]{1,0:T(8,128)(2,1)S(1)}, bf16[288,256]{1,0:T(8,128)(2,1)S(1)}, u32[]{:S(2)}, u32[]{:S(2)}) %collective-permute-start.1) | collective-permute-done | bytes 147488 | tf_op jit(solution)/shard_map/ppermute | solution.py:264
  27.5 2.7 %collective-permute-start.6 = (bf16[288,256]{1,0:T(8,128)(2,1)S(1)}, bf16[288,256]{1,0:T(8,128)(2,1)S(1)}, u32[]{:S(2)}, u32[]{:S(2)}) collective-permute-start(bf16[288,256]{1,0:T(8,128)(2,1)S(1)} %add_convert_fusion), channel_id=1, source_target_pairs={{0,7},{1,0},{2,1},{3,2},{4,3},{5,4},{6,5},{7,6},{8,15},{9,8},{10,9... | collective-permute-start | bytes 442376 | tf_op jit(solution)/shard_map/ppermute | solution.py:264
  30.3 4.2 %collective-permute-done.2 = bf16[288,256]{1,0:T(8,128)(2,1)S(1)} collective-permute-done((bf16[288,256]{1,0:T(8,128)(2,1)S(1)}, bf16[288,256]{1,0:T(8,128)(2,1)S(1)}, u32[]{:S(2)}, u32[]{:S(2)}) %collective-permute-start.2) | collective-permute-done | bytes 147488 | tf_op jit(solution)/shard_map/ppermute | solution.py:264
  34.6 6.6 %collective-permute-done.3.right = bf16[288,256]{1,0:T(8,128)(2,1)S(1)} collective-permute-done((bf16[288,256]{1,0:T(8,128)(2,1)S(1)}, bf16[288,256]{1,0:T(8,128)(2,1)S(1)}, u32[]{:S(2)}, u32[]{:S(2)}) %collective-permute-start.3) | collective-permute-done | bytes 147488 | tf_op jit(solution)/shard_map/ppermute | solution.py:264
  41.2 0.7 copy-done.13
  41.8 1.1 sum_own.1.refs_0_
  43.1 2.7 %collective-permute-start.7 = (bf16[288,256]{1,0:T(8,128)(2,1)S(1)}, bf16[288,256]{1,0:T(8,128)(2,1)S(1)}, u32[]{:S(2)}, u32[]{:S(2)}) collective-permute-start(bf16[288,256]{1,0:T(8,128)(2,1)S(1)} %sum_own.1.refs_0_), channel_id=1, source_target_pairs={{0,7},{1,0},{2,1},{3,2},{4,3},{5,4},{6,5},{7,6},{8,15},{9,8},{10,9... | collective-permute-start | bytes 442376 | tf_op jit(solution)/shard_map/ppermute | solution.py:264
  45.7 3.5 %collective-permute-done.10.refs_7_ = bf16[288,256]{1,0:T(8,128)(2,1)S(1)} collective-permute-done((bf16[288,256]{1,0:T(8,128)(2,1)S(1)}, bf16[288,256]{1,0:T(8,128)(2,1)S(1)}, u32[]{:S(2)}, u32[]{:S(2)}) %collective-permute-start.10) | collective-permute-done | bytes 147488 | tf_op jit(solution)/shard_map/ppermute | solution.py:264
  49.2 2.8 %collective-permute-start.8 = (bf16[288,256]{1,0:T(8,128)(2,1)S(1)}, bf16[288,256]{1,0:T(8,128)(2,1)S(1)}, u32[]{:S(2)}, u32[]{:S(2)}) collective-permute-start(bf16[288,256]{1,0:T(8,128)(2,1)S(1)} %collective-permute-done.7.refs_1_), channel_id=1, source_target_pairs={{0,7},{1,0},{2,1},{3,2},{4,3},{5,4},{6,5},{7,6},{8,15},{9,8},{10,9... | collective-permute-start | bytes 442376 | tf_op jit(solution)/shard_map/ppermute | solution.py:264
  52.0 3.3 %collective-permute-done.11.refs_6_ = bf16[288,256]{1,0:T(8,128)(2,1)S(1)} collective-permute-done((bf16[288,256]{1,0:T(8,128)(2,1)S(1)}, bf16[288,256]{1,0:T(8,128)(2,1)S(1)}, u32[]{:S(2)}, u32[]{:S(2)}) %collective-permute-start.11) | collective-permute-done | bytes 147488 | tf_op jit(solution)/shard_map/ppermute | solution.py:264
  55.3 2.7 %collective-permute-start.9 = (bf16[288,256]{1,0:T(8,128)(2,1)S(1)}, bf16[288,256]{1,0:T(8,128)(2,1)S(1)}, u32[]{:S(2)}, u32[]{:S(2)}) collective-permute-start(bf16[288,256]{1,0:T(8,128)(2,1)S(1)} %collective-permute-done.8.refs_2_), channel_id=1, source_target_pairs={{0,7},{1,0},{2,1},{3,2},{4,3},{5,4},{6,5},{7,6},{8,15},{9,8},{10,9... | collective-permute-start | bytes 442376 | tf_op jit(solution)/shard_map/ppermute | solution.py:264
  58.1 3.0 %collective-permute-done.12.refs_5_ = bf16[288,256]{1,0:T(8,128)(2,1)S(1)} collective-permute-done((bf16[288,256]{1,0:T(8,128)(2,1)S(1)}, bf16[288,256]{1,0:T(8,128)(2,1)S(1)}, u32[]{:S(2)}, u32[]{:S(2)}) %collective-permute-start.12) | collective-permute-done | bytes 147488 | tf_op jit(solution)/shard_map/ppermute | solution.py:264
  61.1 0.4 collective-permute-done.9.refs_3_
  61.4 6.6 %collective-permute-done.13.refs_4_ = bf16[288,256]{1,0:T(8,128)(2,1)S(1)} collective-permute-done((bf16[288,256]{1,0:T(8,128)(2,1)S(1)}, bf16[288,256]{1,0:T(8,128)(2,1)S(1)}, u32[]{:S(2)}, u32[]{:S(2)}) %collective-permute-start.13) | collective-permute-done | bytes 147488 | tf_op jit(solution)/shard_map/ppermute | solution.py:264
  68.1 0.6 copy-done.20
  68.7 4.2 %middle.1 = (bf16[8,320,256]{2,1,0:T(8,128)(2,1)}, bf16[384,128]{1,0:T(8,128)(2,1)}) custom-call(s32[1,8]{1,0:T(1,128)} %owners.5, bf16[256,2048]{1,0:T(8,128)(2,1)} %inv.4, bf16[288,256]{1,0:T(8,128)(2,1)} %copy-done, bf16[288,256]{1,0:T(8,128)(2,1)} %copy-done.15, bf16[288,256]{1,0:T(8,128)(2,1)} %copy-done.17, bf16[288,256]{1,0:T(8,128)(2,1)} %copy-done.19, ...), custom_call_target="tpu_custom_call" | custom-call | flops 536870912 | bytes 4194304 | tf_op jit(solution)/shard_map/middle/pallas_call | solution.py:334
  72.9 3.7 %all-to-all-start = ((bf16[8,320,256]{2,1,0:T(8,128)(2,1)}), bf16[8,320,256]{2,1,0:T(8,128)(2,1)S(1)}, u32[]{:S(2)}, u32[]{:S(2)}) async-start(bf16[8,320,256]{2,1,0:T(8,128)(2,1)} %get-tuple-element.26), calls=%async_computation.1 | async-start | bytes 2621440 | tf_op jit(solution)/shard_map/all_to_all | solution.py:349
  76.7 2.5 %collective-permute-start.14 = (bf16[384,128]{1,0:T(8,128)(2,1)S(1)}, bf16[384,128]{1,0:T(8,128)(2,1)S(1)}, u32[]{:S(2)}, u32[]{:S(2)}) collective-permute-start(bf16[384,128]{1,0:T(8,128)(2,1)S(1)} %copy-done.21), channel_id=1, source_target_pairs={{16,0},{24,8},{32,16},{40,24},{48,32},{56,40},{0,48},{8,56},{80,64... | collective-permute-start | bytes 294920 | tf_op jit(solution)/shard_map/ppermute | solution.py:297
  79.1 0.2 collective-permute-start.15
  79.4 0.7 collective-permute-start.16
  80.1 1.6 collective-permute-done.14.refs_1_
  81.8 2.5 %collective-permute-done.15.refs_2_ = bf16[384,128]{1,0:T(8,128)(2,1)S(1)} collective-permute-done((bf16[384,128]{1,0:T(8,128)(2,1)S(1)}, bf16[384,128]{1,0:T(8,128)(2,1)S(1)}, u32[]{:S(2)}, u32[]{:S(2)}) %collective-permute-start.15) | collective-permute-done | bytes 98336 | tf_op jit(solution)/shard_map/ppermute | solution.py:297
  84.2 0.9 collective-permute-done.16.refs_3_
  85.1 0.6 copy-done.24
  85.8 1.8 stack_maps.1.refs_2_
  87.6 4.3 %collective-permute-start.18 = (bf16[4,384,128]{2,1,0:T(8,128)(2,1)}, bf16[4,384,128]{2,1,0:T(8,128)(2,1)S(1)}, u32[]{:S(2)}, u32[]{:S(2)}) collective-permute-start(bf16[4,384,128]{2,1,0:T(8,128)(2,1)} %stack_maps.1.refs_2_), channel_id=1, source_target_pairs={{64,0},{72,8},{80,16},{88,24},{96,32},{104,40},{112,48},{120,56},{... | collective-permute-start | bytes 1179656 | tf_op jit(solution)/shard_map/ppermute | solution.py:297
  91.8 0.6 collective-permute-start.22
  92.4 11.5 %collective-permute-start.17 = (bf16[4,384,128]{2,1,0:T(8,128)(2,1)}, bf16[4,384,128]{2,1,0:T(8,128)(2,1)S(1)}, u32[]{:S(2)}, u32[]{:S(2)}) collective-permute-start(bf16[4,384,128]{2,1,0:T(8,128)(2,1)} %stack_maps.1.refs_2_), channel_id=1, source_target_pairs={{0,8},{8,0},{16,24},{24,16},{32,40},{40,32},{48,56},{56,48},{64,72... | collective-permute-start | bytes 1179656 | tf_op jit(solution)/shard_map/ppermute | solution.py:259
  103.9 9.0 %collective-permute-start.19 = (bf16[4,384,128]{2,1,0:T(8,128)(2,1)S(1)}, bf16[4,384,128]{2,1,0:T(8,128)(2,1)S(1)}, u32[]{:S(2)}, u32[]{:S(2)}) collective-permute-start(bf16[4,384,128]{2,1,0:T(8,128)(2,1)S(1)} %collective-permute-done.18.refs_3_), channel_id=1, source_target_pairs={{0,8},{8,0},{16,24},{24,16},{32,40},{40,32},{48,56},{56,48},{64,72... | collective-permute-start | bytes 1179656 | tf_op jit(solution)/shard_map/ppermute | solution.py:259
  112.9 0.1 collective-permute-start.21
  113.0 3.5 %collective-permute-start.23 = (bf16[4,384,128]{2,1,0:T(8,128)(2,1)S(1)}, bf16[4,384,128]{2,1,0:T(8,128)(2,1)S(1)}, u32[]{:S(2)}, u32[]{:S(2)}) collective-permute-start(bf16[4,384,128]{2,1,0:T(8,128)(2,1)S(1)} %collective-permute-done.22.refs_5_), channel_id=1, source_target_pairs={{0,8},{8,0},{16,24},{24,16},{32,40},{40,32},{48,56},{56,48},{64,72... | collective-permute-start | bytes 1179656 | tf_op jit(solution)/shard_map/ppermute | solution.py:259
  116.5 1.3 collective-permute-done.23.refs_3_.refs_9_
  117.8 0.7 copy-done.7
  118.6 1.1 copy-done.2
  119.7 2.6 %sum_terms.1 = (f32[256,256]{1,0:T(8,128)}, bf16[512,256]{1,0:T(8,128)(2,1)}, f32[16,32,256]{2,1,0:T(8,128)}) custom-call(bf16[8,320,256]{2,1,0:T(8,128)(2,1)} %copy-done.2, bf16[256,256]{1,0:T(8,128)(2,1)} %reduce-scatter.2.cloned.1.call-done.refs_9_.shared, bf16[128,128]{1,0:T(8,128)(2,1)} %refs_10_.1, bf16[4,384,128]{2,1,0:T(8,128)(2,1)} %copy-done.4, ...), custom_call_target="tpu_custom_call" | custom-call | bytes 2097152 | tf_op jit(solution)/shard_map/sum_terms/pallas_call | solution.py:350
  122.3 14.5 %all_to_all.15.refs_0_ = f32[16,32,256]{2,1,0:T(8,128)S(1)} all-to-all(f32[16,32,256]{2,1,0:T(8,128)} %get-tuple-element.30), channel_id=1, replica_groups={{0,16,32,48,64,80,96,112,128,144,160,176,192,208,224,240},{8,24,40,56,7..., dimensions={0} | all-to-all | bytes 1048576 | tf_op jit(solution)/shard_map/all_to_all | solution.py:364
  136.9 1.5 collective-permute-start.24
  138.4 1.5 collective-permute-done.24.refs_1_
  139.9 0.8 copy-done.8
  140.7 14.4 %chain.1 = f32[8,32,256]{2,1,0:T(8,128)} custom-call(f32[16,32,256]{2,1,0:T(8,128)} %copy-done.3, f32[16,32,256]{2,1,0:T(8,128)} %copy-done.8, bf16[4,384,128]{2,1,0:T(8,128)(2,1)} %stack_maps.1.refs_2_, bf16[4,384,128]{2,1,0:T(8,128)(2,1)} %copy-done.9, bf16[4,384,128]{2,1,0:T(8,128)(2,1)} %copy-done.10, bf16[4,384,128]{2,1,0:T(8,128)(2,1)} %copy-done.11, ...), custom_call_target="tpu_custom_call" | custom-call | flops 301989888 | bytes 8388608 | tf_op jit(solution)/shard_map/chain/pallas_call | solution.py:366
  155.1 18.0 %all_to_all.16 = f32[8,32,256]{2,1,0:T(8,128)} all-to-all(f32[8,32,256]{2,1,0:T(8,128)} %chain.1), channel_id=1, replica_groups=mesh['wide'=32,'narrow'=8] {'narrow'}, dimensions={0} | all-to-all | bytes 524288 | tf_op jit(solution)/shard_map/all_to_all | solution.py:381
  173.1 5.1 %final.1 = (f32[512,256]{1,0:T(8,128)}, f32[256,256]{1,0:T(8,128)}) custom-call(s32[2,4]{1,0:T(2,128)} %bitcast.6, s32[1,8]{1,0:T(1,128)} %owners.5, f32[256,256]{1,0:T(8,128)} %get-tuple-element.28.kept, bf16[8,512,256]{2,1,0:T(8,128)(2,1)} %bitcast.3, f32[256,256]{1,0:T(8,128)} %bitcast.4, bf16[4,2,128,128]{3,2,1,0:T(8,128)(2,1)} %cpl.3, ...), custom_call_target="tpu_custom_call" | custom-call | flops 335544320 | bytes 6291456 | tf_op jit(solution)/shard_map/final/pallas_call | solution.py:383
  (74 shorter events, 0.8 us)
Async XLA Ops:
  7.2 60.9 %reduce-scatter.2.cloned.1.call-start = ((), (), s32[]{:S(2)}) async-start(), calls=%async_computation.4 | async-start | bytes 1179648 | tf_op jit(solution)/shard_map/reduce_scatter | solution.py:333
  12.0 10.1 %collective-permute-start = (bf16[288,256]{1,0:T(8,128)(2,1)S(1)}, bf16[288,256]{1,0:T(8,128)(2,1)S(1)}, u32[]{:S(2)}, u32[]{:S(2)}) collective-permute-start(bf16[288,256]{1,0:T(8,128)(2,1)S(1)} %get-tuple-element.17), channel_id=1, source_target_pairs={{0,1},{1,2},{2,3},{3,4},{4,5},{5,6},{6,7},{7,0},{8,9},{9,10},{10,1... | collective-permute-start | bytes 442376 | tf_op jit(solution)/shard_map/ppermute | solution.py:264
  14.5 7.6 %collective-permute-start.4 = (bf16[288,256]{1,0:T(8,128)(2,1)S(1)}, bf16[288,256]{1,0:T(8,128)(2,1)S(1)}, u32[]{:S(2)}, u32[]{:S(2)}) collective-permute-start(bf16[288,256]{1,0:T(8,128)(2,1)S(1)} %get-tuple-element.21), channel_id=1, source_target_pairs={{0,7},{1,0},{2,1},{3,2},{4,3},{5,4},{6,5},{7,6},{8,15},{9,8},{10,9... | collective-permute-start | bytes 442376 | tf_op jit(solution)/shard_map/ppermute | solution.py:264
  22.1 5.3 %collective-permute-start.1 = (bf16[288,256]{1,0:T(8,128)(2,1)S(1)}, bf16[288,256]{1,0:T(8,128)(2,1)S(1)}, u32[]{:S(2)}, u32[]{:S(2)}) collective-permute-start(bf16[288,256]{1,0:T(8,128)(2,1)S(1)} %add_convert_fusion.4), channel_id=1, source_target_pairs={{0,1},{1,2},{2,3},{3,4},{4,5},{5,6},{6,7},{7,0},{8,9},{9,10},{10,1... | collective-permute-start | bytes 442376 | tf_op jit(solution)/shard_map/ppermute | solution.py:264
  22.2 5.3 %collective-permute-start.5 = (bf16[288,256]{1,0:T(8,128)(2,1)S(1)}, bf16[288,256]{1,0:T(8,128)(2,1)S(1)}, u32[]{:S(2)}, u32[]{:S(2)}) collective-permute-start(bf16[288,256]{1,0:T(8,128)(2,1)S(1)} %add_convert_fusion.1), channel_id=1, source_target_pairs={{0,7},{1,0},{2,1},{3,2},{4,3},{5,4},{6,5},{7,6},{8,15},{9,8},{10,9... | collective-permute-start | bytes 442376 | tf_op jit(solution)/shard_map/ppermute | solution.py:264
  27.4 7.0 %collective-permute-start.2 = (bf16[288,256]{1,0:T(8,128)(2,1)S(1)}, bf16[288,256]{1,0:T(8,128)(2,1)S(1)}, u32[]{:S(2)}, u32[]{:S(2)}) collective-permute-start(bf16[288,256]{1,0:T(8,128)(2,1)S(1)} %add_convert_fusion.3), channel_id=1, source_target_pairs={{0,1},{1,2},{2,3},{3,4},{4,5},{5,6},{6,7},{7,0},{8,9},{9,10},{10,1... | collective-permute-start | bytes 442376 | tf_op jit(solution)/shard_map/ppermute | solution.py:264
  27.5 7.0 %collective-permute-start.6 = (bf16[288,256]{1,0:T(8,128)(2,1)S(1)}, bf16[288,256]{1,0:T(8,128)(2,1)S(1)}, u32[]{:S(2)}, u32[]{:S(2)}) collective-permute-start(bf16[288,256]{1,0:T(8,128)(2,1)S(1)} %add_convert_fusion), channel_id=1, source_target_pairs={{0,7},{1,0},{2,1},{3,2},{4,3},{5,4},{6,5},{7,6},{8,15},{9,8},{10,9... | collective-permute-start | bytes 442376 | tf_op jit(solution)/shard_map/ppermute | solution.py:264
  34.5 6.7 %collective-permute-start.3 = (bf16[288,256]{1,0:T(8,128)(2,1)S(1)}, bf16[288,256]{1,0:T(8,128)(2,1)S(1)}, u32[]{:S(2)}, u32[]{:S(2)}) collective-permute-start(bf16[288,256]{1,0:T(8,128)(2,1)S(1)} %add_convert_fusion.2), channel_id=1, source_target_pairs={{0,1},{1,2},{2,3},{3,4},{4,5},{5,6},{6,7},{7,0},{8,9},{9,10},{10,1... | collective-permute-start | bytes 442376 | tf_op jit(solution)/shard_map/ppermute | solution.py:264
  34.6 6.6 %copy-start.12 = (bf16[288,256]{1,0:T(8,128)(2,1)}, bf16[288,256]{1,0:T(8,128)(2,1)S(1)}, u32[]{:S(2)}) copy-start(bf16[288,256]{1,0:T(8,128)(2,1)S(1)} %collective-permute-done.6.left) | copy-start | bytes 442372
  43.0 25.1 %copy-start = (bf16[288,256]{1,0:T(8,128)(2,1)}, bf16[288,256]{1,0:T(8,128)(2,1)S(1)}, u32[]{:S(2)}) copy-start(bf16[288,256]{1,0:T(8,128)(2,1)S(1)} %sum_own.1.refs_0_) | copy-start | bytes 442372
  43.0 6.2 %collective-permute-start.10 = (bf16[288,256]{1,0:T(8,128)(2,1)S(1)}, bf16[288,256]{1,0:T(8,128)(2,1)S(1)}, u32[]{:S(2)}, u32[]{:S(2)}) collective-permute-start(bf16[288,256]{1,0:T(8,128)(2,1)S(1)} %sum_own.1.refs_0_), channel_id=1, source_target_pairs={{0,1},{1,2},{2,3},{3,4},{4,5},{5,6},{6,7},{7,0},{8,9},{9,10},{10,1... | collective-permute-start | bytes 442376 | tf_op jit(solution)/shard_map/ppermute | solution.py:264
  43.1 6.1 %collective-permute-start.7 = (bf16[288,256]{1,0:T(8,128)(2,1)S(1)}, bf16[288,256]{1,0:T(8,128)(2,1)S(1)}, u32[]{:S(2)}, u32[]{:S(2)}) collective-permute-start(bf16[288,256]{1,0:T(8,128)(2,1)S(1)} %sum_own.1.refs_0_), channel_id=1, source_target_pairs={{0,7},{1,0},{2,1},{3,2},{4,3},{5,4},{6,5},{7,6},{8,15},{9,8},{10,9... | collective-permute-start | bytes 442376 | tf_op jit(solution)/shard_map/ppermute | solution.py:264
  49.2 18.9 %copy-start.14 = (bf16[288,256]{1,0:T(8,128)(2,1)}, bf16[288,256]{1,0:T(8,128)(2,1)S(1)}, u32[]{:S(2)}) copy-start(bf16[288,256]{1,0:T(8,128)(2,1)S(1)} %collective-permute-done.10.refs_7_) | copy-start | bytes 442372
  49.2 6.1 %collective-permute-start.11 = (bf16[288,256]{1,0:T(8,128)(2,1)S(1)}, bf16[288,256]{1,0:T(8,128)(2,1)S(1)}, u32[]{:S(2)}, u32[]{:S(2)}) collective-permute-start(bf16[288,256]{1,0:T(8,128)(2,1)S(1)} %collective-permute-done.10.refs_7_), channel_id=1, source_target_pairs={{0,1},{1,2},{2,3},{3,4},{4,5},{5,6},{6,7},{7,0},{8,9},{9,10},{10,1... | collective-permute-start | bytes 442376 | tf_op jit(solution)/shard_map/ppermute | solution.py:264
  49.2 18.8 %copy-start.15 = (bf16[288,256]{1,0:T(8,128)(2,1)}, bf16[288,256]{1,0:T(8,128)(2,1)S(1)}, u32[]{:S(2)}) copy-start(bf16[288,256]{1,0:T(8,128)(2,1)S(1)} %collective-permute-done.7.refs_1_) | copy-start | bytes 442372
  49.2 6.1 %collective-permute-start.8 = (bf16[288,256]{1,0:T(8,128)(2,1)S(1)}, bf16[288,256]{1,0:T(8,128)(2,1)S(1)}, u32[]{:S(2)}, u32[]{:S(2)}) collective-permute-start(bf16[288,256]{1,0:T(8,128)(2,1)S(1)} %collective-permute-done.7.refs_1_), channel_id=1, source_target_pairs={{0,7},{1,0},{2,1},{3,2},{4,3},{5,4},{6,5},{7,6},{8,15},{9,8},{10,9... | collective-permute-start | bytes 442376 | tf_op jit(solution)/shard_map/ppermute | solution.py:264
  55.3 12.7 %copy-start.16 = (bf16[288,256]{1,0:T(8,128)(2,1)}, bf16[288,256]{1,0:T(8,128)(2,1)S(1)}, u32[]{:S(2)}) copy-start(bf16[288,256]{1,0:T(8,128)(2,1)S(1)} %collective-permute-done.11.refs_6_) | copy-start | bytes 442372
  55.3 5.8 %collective-permute-start.12 = (bf16[288,256]{1,0:T(8,128)(2,1)S(1)}, bf16[288,256]{1,0:T(8,128)(2,1)S(1)}, u32[]{:S(2)}, u32[]{:S(2)}) collective-permute-start(bf16[288,256]{1,0:T(8,128)(2,1)S(1)} %collective-permute-done.11.refs_6_), channel_id=1, source_target_pairs={{0,1},{1,2},{2,3},{3,4},{4,5},{5,6},{6,7},{7,0},{8,9},{9,10},{10,1... | collective-permute-start | bytes 442376 | tf_op jit(solution)/shard_map/ppermute | solution.py:264
  55.3 12.7 %copy-start.17 = (bf16[288,256]{1,0:T(8,128)(2,1)}, bf16[288,256]{1,0:T(8,128)(2,1)S(1)}, u32[]{:S(2)}) copy-start(bf16[288,256]{1,0:T(8,128)(2,1)S(1)} %collective-permute-done.8.refs_2_) | copy-start | bytes 442372
  55.3 6.1 %collective-permute-start.9 = (bf16[288,256]{1,0:T(8,128)(2,1)S(1)}, bf16[288,256]{1,0:T(8,128)(2,1)S(1)}, u32[]{:S(2)}, u32[]{:S(2)}) collective-permute-start(bf16[288,256]{1,0:T(8,128)(2,1)S(1)} %collective-permute-done.8.refs_2_), channel_id=1, source_target_pairs={{0,7},{1,0},{2,1},{3,2},{4,3},{5,4},{6,5},{7,6},{8,15},{9,8},{10,9... | collective-permute-start | bytes 442376 | tf_op jit(solution)/shard_map/ppermute | solution.py:264
  61.1 7.0 %copy-start.18 = (bf16[288,256]{1,0:T(8,128)(2,1)}, bf16[288,256]{1,0:T(8,128)(2,1)S(1)}, u32[]{:S(2)}) copy-start(bf16[288,256]{1,0:T(8,128)(2,1)S(1)} %collective-permute-done.12.refs_5_) | copy-start | bytes 442372
  61.1 7.0 %collective-permute-start.13 = (bf16[288,256]{1,0:T(8,128)(2,1)S(1)}, bf16[288,256]{1,0:T(8,128)(2,1)S(1)}, u32[]{:S(2)}, u32[]{:S(2)}) collective-permute-start(bf16[288,256]{1,0:T(8,128)(2,1)S(1)} %collective-permute-done.12.refs_5_), channel_id=1, source_target_pairs={{0,1},{1,2},{2,3},{3,4},{4,5},{5,6},{6,7},{7,0},{8,9},{9,10},{10,1... | collective-permute-start | bytes 442376 | tf_op jit(solution)/shard_map/ppermute | solution.py:264
  61.4 6.7 %copy-start.19 = (bf16[288,256]{1,0:T(8,128)(2,1)}, bf16[288,256]{1,0:T(8,128)(2,1)S(1)}, u32[]{:S(2)}) copy-start(bf16[288,256]{1,0:T(8,128)(2,1)S(1)} %collective-permute-done.9.refs_3_) | copy-start | bytes 442372
  72.9 3.8 %copy-start.21 = (bf16[384,128]{1,0:T(8,128)(2,1)S(1)}, bf16[384,128]{1,0:T(8,128)(2,1)}, u32[]{:S(2)}) copy-start(bf16[384,128]{1,0:T(8,128)(2,1)} %get-tuple-element.27.refs_0_) | copy-start | bytes 294916
  72.9 44.9 %all-to-all-start = ((bf16[8,320,256]{2,1,0:T(8,128)(2,1)}), bf16[8,320,256]{2,1,0:T(8,128)(2,1)S(1)}, u32[]{:S(2)}, u32[]{:S(2)}) async-start(bf16[8,320,256]{2,1,0:T(8,128)(2,1)} %get-tuple-element.26), calls=%async_computation.1 | async-start | bytes 2621440 | tf_op jit(solution)/shard_map/all_to_all | solution.py:349
  76.6 96.5 %all-gather.3.cloned.1.call-start = ((), (), s32[]{:S(2)}) async-start(), calls=%async_computation.5 | async-start | bytes 2359296 | tf_op jit(solution)/shard_map/all_gather | solution.py:361
  76.7 5.1 %collective-permute-start.14 = (bf16[384,128]{1,0:T(8,128)(2,1)S(1)}, bf16[384,128]{1,0:T(8,128)(2,1)S(1)}, u32[]{:S(2)}, u32[]{:S(2)}) collective-permute-start(bf16[384,128]{1,0:T(8,128)(2,1)S(1)} %copy-done.21), channel_id=1, source_target_pairs={{16,0},{24,8},{32,16},{40,24},{48,32},{56,40},{0,48},{8,56},{80,64... | collective-permute-start | bytes 294920 | tf_op jit(solution)/shard_map/ppermute | solution.py:297
  79.1 5.1 %collective-permute-start.15 = (bf16[384,128]{1,0:T(8,128)(2,1)S(1)}, bf16[384,128]{1,0:T(8,128)(2,1)S(1)}, u32[]{:S(2)}, u32[]{:S(2)}) collective-permute-start(bf16[384,128]{1,0:T(8,128)(2,1)S(1)} %copy-done.21), channel_id=1, source_target_pairs={{32,0},{40,8},{48,16},{56,24},{0,32},{8,40},{16,48},{24,56},{96,64... | collective-permute-start | bytes 294920 | tf_op jit(solution)/shard_map/ppermute | solution.py:297
  79.4 5.7 %collective-permute-start.16 = (bf16[384,128]{1,0:T(8,128)(2,1)S(1)}, bf16[384,128]{1,0:T(8,128)(2,1)S(1)}, u32[]{:S(2)}, u32[]{:S(2)}) collective-permute-start(bf16[384,128]{1,0:T(8,128)(2,1)S(1)} %copy-done.21), channel_id=1, source_target_pairs={{48,0},{56,8},{0,16},{8,24},{16,32},{24,40},{32,48},{40,56},{112,6... | collective-permute-start | bytes 294920 | tf_op jit(solution)/shard_map/ppermute | solution.py:297
  81.8 3.4 %copy-start.22 = (bf16[384,128]{1,0:T(8,128)(2,1)}, bf16[384,128]{1,0:T(8,128)(2,1)S(1)}, u32[]{:S(2)}) copy-start(bf16[384,128]{1,0:T(8,128)(2,1)S(1)} %collective-permute-done.14.refs_1_) | copy-start | bytes 294916
  84.2 0.9 copy-start.23
  87.6 16.3 %collective-permute-start.18 = (bf16[4,384,128]{2,1,0:T(8,128)(2,1)}, bf16[4,384,128]{2,1,0:T(8,128)(2,1)S(1)}, u32[]{:S(2)}, u32[]{:S(2)}) collective-permute-start(bf16[4,384,128]{2,1,0:T(8,128)(2,1)} %stack_maps.1.refs_2_), channel_id=1, source_target_pairs={{64,0},{72,8},{80,16},{88,24},{96,32},{104,40},{112,48},{120,56},{... | collective-permute-start | bytes 1179656 | tf_op jit(solution)/shard_map/ppermute | solution.py:297
  91.8 21.0 %collective-permute-start.20 = (bf16[4,384,128]{2,1,0:T(8,128)(2,1)}, bf16[4,384,128]{2,1,0:T(8,128)(2,1)S(1)}, u32[]{:S(2)}, u32[]{:S(2)}) collective-permute-start(bf16[4,384,128]{2,1,0:T(8,128)(2,1)} %stack_maps.1.refs_2_), channel_id=1, source_target_pairs={{128,0},{136,8},{144,16},{152,24},{160,32},{168,40},{176,48},{184,... | collective-permute-start | bytes 1179656 | tf_op jit(solution)/shard_map/ppermute | solution.py:297
  91.8 21.1 %collective-permute-start.22 = (bf16[4,384,128]{2,1,0:T(8,128)(2,1)}, bf16[4,384,128]{2,1,0:T(8,128)(2,1)S(1)}, u32[]{:S(2)}, u32[]{:S(2)}) collective-permute-start(bf16[4,384,128]{2,1,0:T(8,128)(2,1)} %stack_maps.1.refs_2_), channel_id=1, source_target_pairs={{192,0},{200,8},{208,16},{216,24},{224,32},{232,40},{240,48},{248,... | collective-permute-start | bytes 1179656 | tf_op jit(solution)/shard_map/ppermute | solution.py:297
  92.4 24.1 %collective-permute-start.17 = (bf16[4,384,128]{2,1,0:T(8,128)(2,1)}, bf16[4,384,128]{2,1,0:T(8,128)(2,1)S(1)}, u32[]{:S(2)}, u32[]{:S(2)}) collective-permute-start(bf16[4,384,128]{2,1,0:T(8,128)(2,1)} %stack_maps.1.refs_2_), channel_id=1, source_target_pairs={{0,8},{8,0},{16,24},{24,16},{32,40},{40,32},{48,56},{56,48},{64,72... | collective-permute-start | bytes 1179656 | tf_op jit(solution)/shard_map/ppermute | solution.py:259
  103.9 36.0 %copy-start.9 = (bf16[4,384,128]{2,1,0:T(8,128)(2,1)}, bf16[4,384,128]{2,1,0:T(8,128)(2,1)S(1)}, u32[]{:S(2)}) copy-start(bf16[4,384,128]{2,1,0:T(8,128)(2,1)S(1)} %collective-permute-done.18.refs_3_) | copy-start | bytes 1179652
  103.9 12.6 %collective-permute-start.19 = (bf16[4,384,128]{2,1,0:T(8,128)(2,1)S(1)}, bf16[4,384,128]{2,1,0:T(8,128)(2,1)S(1)}, u32[]{:S(2)}, u32[]{:S(2)}) collective-permute-start(bf16[4,384,128]{2,1,0:T(8,128)(2,1)S(1)} %collective-permute-done.18.refs_3_), channel_id=1, source_target_pairs={{0,8},{8,0},{16,24},{24,16},{32,40},{40,32},{48,56},{56,48},{64,72... | collective-permute-start | bytes 1179656 | tf_op jit(solution)/shard_map/ppermute | solution.py:259
  112.9 3.6 %copy-start.10 = (bf16[4,384,128]{2,1,0:T(8,128)(2,1)}, bf16[4,384,128]{2,1,0:T(8,128)(2,1)S(1)}, u32[]{:S(2)}) copy-start(bf16[4,384,128]{2,1,0:T(8,128)(2,1)S(1)} %collective-permute-done.20.refs_4_) | copy-start | bytes 1179652
  112.9 3.6 %collective-permute-start.21 = (bf16[4,384,128]{2,1,0:T(8,128)(2,1)S(1)}, bf16[4,384,128]{2,1,0:T(8,128)(2,1)S(1)}, u32[]{:S(2)}, u32[]{:S(2)}) collective-permute-start(bf16[4,384,128]{2,1,0:T(8,128)(2,1)S(1)} %collective-permute-done.20.refs_4_), channel_id=1, source_target_pairs={{0,8},{8,0},{16,24},{24,16},{32,40},{40,32},{48,56},{56,48},{64,72... | collective-permute-start | bytes 1179656 | tf_op jit(solution)/shard_map/ppermute | solution.py:259
  113.0 3.5 %copy-start.11 = (bf16[4,384,128]{2,1,0:T(8,128)(2,1)}, bf16[4,384,128]{2,1,0:T(8,128)(2,1)S(1)}, u32[]{:S(2)}) copy-start(bf16[4,384,128]{2,1,0:T(8,128)(2,1)S(1)} %collective-permute-done.22.refs_5_) | copy-start | bytes 1179652
  113.0 4.8 %collective-permute-start.23 = (bf16[4,384,128]{2,1,0:T(8,128)(2,1)S(1)}, bf16[4,384,128]{2,1,0:T(8,128)(2,1)S(1)}, u32[]{:S(2)}, u32[]{:S(2)}) collective-permute-start(bf16[4,384,128]{2,1,0:T(8,128)(2,1)S(1)} %collective-permute-done.22.refs_5_), channel_id=1, source_target_pairs={{0,8},{8,0},{16,24},{24,16},{32,40},{40,32},{48,56},{56,48},{64,72... | collective-permute-start | bytes 1179656 | tf_op jit(solution)/shard_map/ppermute | solution.py:259
  116.5 1.4 copy-start.4
  116.5 1.3 copy-start.5
  116.5 1.3 copy-start.6
  118.6 1.1 copy-start.2
  136.9 3.0 %copy-start.3 = (f32[16,32,256]{2,1,0:T(8,128)}, f32[16,32,256]{2,1,0:T(8,128)S(1)}, u32[]{:S(2)}) copy-start(f32[16,32,256]{2,1,0:T(8,128)S(1)} %all_to_all.15.refs_0_) | copy-start | bytes 1572868
  136.9 3.0 %collective-permute-start.24 = (f32[16,32,256]{2,1,0:T(8,128)S(1)}, f32[16,32,256]{2,1,0:T(8,128)S(1)}, u32[]{:S(2)}, u32[]{:S(2)}) collective-permute-start(f32[16,32,256]{2,1,0:T(8,128)S(1)} %all_to_all.15.refs_0_), channel_id=1, source_target_pairs={{0,8},{8,0},{16,24},{24,16},{32,40},{40,32},{48,56},{56,48},{64,72... | collective-permute-start | bytes 1572872 | tf_op jit(solution)/shard_map/ppermute | solution.py:259
  139.9 0.8 copy-start.8
  (5 other events, 3.4 us)
Sparse Core Ops, SparseCore 0:
  12.1 39.5 reduce-scatter.1
  122.5 35.0 all-gather.2

commit v4 on v3

--- a/solution.py
+++ b/solution.py
@@ -10,7 +10,7 @@
 VMEM = pl.BlockSpec(memory_space=pltpu.VMEM)
 SMEM = pl.BlockSpec(memory_space=pltpu.SMEM)
 ANY = pl.BlockSpec(memory_space=pl.ANY)
-LIMIT = 56 * 1024 * 1024
+MIB = 1024 * 1024
 
 NN = (((1,), (0,)), ((), ()))
 NT = (((1,), (1,)), ((), ()))
@@ -40,7 +40,7 @@
     return mm(ah, b_exact, dims) + (mm(al, b_exact, dims) + mm(ax, b_exact, dims))
 
 
-def call(kernel, name, outs, ins, scratch=(), flops=0, moved=0):
+def call(kernel, name, outs, ins, scratch=(), flops=0, moved=0, limit=20):
     return pl.pallas_call(
         kernel,
         name=name,
@@ -48,9 +48,13 @@
         in_specs=ins,
         out_specs=jax.tree.map(lambda _: VMEM, outs, is_leaf=lambda o: hasattr(o, "dtype")),
         scratch_shapes=list(scratch),
-        compiler_params=pltpu.CompilerParams(vmem_limit_bytes=LIMIT),
+        compiler_params=pltpu.CompilerParams(vmem_limit_bytes=limit * MIB),
         cost_estimate=pl.CostEstimate(flops=flops, bytes_accessed=moved, transcendentals=0),
     )
+
+
+def near(value):
+    return pltpu.with_memory_space_constraint(value, pltpu.VMEM)
 
 
 def held_group(owners):
@@ -153,22 +157,29 @@
         terms[j, rows + cols :, b:] = head_lo[at]
 
 
-def sum_terms_kernel(parts, shared, link, *refs):
-    kept, packed, spread = refs[-3:]
-    rows = kept.shape[0]
+def sum_ends_kernel(parts, link, *refs):
+    spread = refs[-1]
     b = link.shape[0]
     cols = spread.shape[1]
-    total = parts[0].astype(F32)
+    rows = parts.shape[1] - 2 * cols
+    total = parts[0, rows:, :].astype(F32)
     for j in range(1, parts.shape[0]):
-        total += parts[j].astype(F32)
-    kept[...] = total[:rows]
-    packed[:rows, :] = total[:rows].astype(BF)
-    packed[rows:, :] = shared[...]
-    ends = total[rows : rows + cols] + total[rows + cols :]
+        total += parts[j, rows:, :].astype(F32)
+    ends = total[:cols] + total[cols:]
     head = mm2(ends[:, b:], link[...], NN)
     for j in range(spread.shape[0]):
         spread[j, :, :b] = ends[:, :b]
         spread[j, :, b:] = head
+
+
+def sum_terms_kernel(parts, shared, _, kept, packed):
+    rows = kept.shape[0]
+    total = parts[0, :rows, :].astype(F32)
+    for j in range(1, parts.shape[0]):
+        total += parts[j, :rows, :].astype(F32)
+    kept[...] = total
+    packed[:rows, :] = total.astype(BF)
+    packed[rows:, :] = shared[...]
 
 
 def stack_kernel(*refs):
@@ -192,23 +203,19 @@
     here = lax.rem(wide, 2)
     x = lax.rem(lax.div(wide, 2), 4)
     y = lax.div(wide, 8)
-    copies = []
     for side, ag_part, map_parts in ((here, ags[0], mapss[0]), (1 - here, ags[1], mapss[1])):
-        copies.append((ag_part, ag.at[side]))
         for j in range(4):
             for k in range(4):
                 at = lax.rem(y + j, 4) * 4 + lax.rem(x + k, 4)
-                copies.append((map_parts[j].at[k], maps.at[side, at]))
-    copies = [pltpu.make_async_copy(p, q, sems.at[i]) for i, (p, q) in enumerate(copies)]
-    for copy in copies:
-        copy.start()
-    for copy in copies:
-        copy.wait()
+                where = maps.at[side, at]
+                pltpu.make_async_copy(map_parts[j].at[k], where, sems.at[side, at]).start()
+        ag[side] = ag_part[...]
     state = jnp.zeros((out.shape[1], b), F32)
     for w in range(length):
         states[w] = state
+        at = (w % 2, w // 2)
+        pltpu.make_async_copy(mapss[0][0].at[0], maps.at[at], sems.at[at]).wait()
         if w + 1 < length:
-            at = (w % 2, w // 2)
             moved = times_map(state, maps[(*at, slice(0, b))], maps[(*at, slice(b, 2 * b))], NT)
             state = ag[(*at, slice(None), slice(0, b))] - moved
     back = jnp.zeros_like(state)
@@ -221,37 +228,38 @@
             local = ag[(*at, slice(None), slice(b, 2 * b))] - (mm(vh, corner, NN) + mm(vl, corner, NN))
             moved = times_map(back, maps[(*at, slice(0, b))], maps[(*at, slice(b, 2 * b))], NN)
             back = local - moved
-    mine = mm2(states[wide], link[...], NT)
-    last = incoming[wide]
+    mine = mm2(states[wide], link[...], NT).astype(BF)
+    last = incoming[wide].astype(BF)
     for j in range(out.shape[0]):
         out[j, :, :b] = mine
         out[j, :, b:] = last
 
 
-def final_kernel(
-    parent, owners, kept, gathered, z, cpl, inv, fl, leaf_out, sep_out, zs
-):
-    b = inv.shape[1]
-    rows = kept.shape[0]
-    zh, zl = halves(z[...])
-    zs[0] = zh
-    zs[1] = zl
-
-    def fix(g, start, count):
-        part = gathered[g, pl.ds(rows + start, count), :]
-        return mm(part, zs[0], NT) + mm(part, zs[1], NT)
-
-    sep_out[...] = kept[...] - fix(held_group(owners), 0, rows)
-    for i in range(inv.shape[0]):
-        acc = fl[i * b : (i + 1) * b, :].astype(F32)
+def before_kernel(parent, owners, gathered, cpl, fl, base, fix, own):
+    b = cpl.shape[2]
+    rows = own.shape[0]
+    own[...] = gathered[held_group(owners), rows:, :]
+    for i in range(cpl.shape[0]):
+        at = slice(i * b, (i + 1) * b)
+        value = fl[at, :].astype(F32)
+        move = jnp.zeros((b, 2 * b), F32)
         for k in range(cpl.shape[1]):
             p = parent[k, i]
             g = lax.div(p, 2)
-            at = pl.multiple_of(lax.rem(p, 2) * b, b)
-            block = gathered[owners[0, g], pl.ds(at, b), :].astype(F32)
-            block = (block - fix(g, at, b)).astype(BF)
-            acc -= mm(cpl[i, k], block, TN)
-        leaf_out[i * b : (i + 1) * b, :] = mm(inv[i], acc.astype(BF), TN)
+            start = pl.multiple_of(lax.rem(p, 2) * b, b)
+            value -= mm(cpl[i, k], gathered[owners[0, g], pl.ds(start, b), :], TN)
+            move += mm(cpl[i, k], gathered[g, pl.ds(rows + start, b), :], TN)
+        base[at, :] = value
+        fix[at, :] = move.astype(BF)
+
+
+def final_kernel(kept, own, base, fix, z, inv, leaf_out, sep_out):
+    b = inv.shape[1]
+    sep_out[...] = kept[...] - mm(own[...], z[...], NT)
+    for i in range(inv.shape[0]):
+        at = slice(i * b, (i + 1) * b)
+        middle = (base[at, :] + mm(fix[at, :], z[...], NT)).astype(BF)
+        leaf_out[at, :] = mm(inv[i], middle, TN)
 
 
 def swap(value, axis, by):
@@ -323,72 +331,91 @@
         [pltpu.VMEM((all_rows + 2 * b, sketch), F32)],
         flops=2 * 12 * b * b * sketch,
         moved=4 << 20,
+        limit=56,
     )(parent, row_owner, leaf_rhs, leaf_inv, leaf_coupling, sep_rhs, sep_inv)
     right, left = ring_sum(blocks)
     own = call(sum_own_kernel, "sum_own", held((extra, sketch), BF), [VMEM] * 3, moved=1 << 18)(
-        right, left, blocks[0]
+        near(right), near(left), near(blocks[0])
     )
-    coupled = ring_gather(own)
+    coupled = [near(block) for block in ring_gather(own)]
 
     shared = lax.psum_scatter(shared, "narrow", scatter_dimension=0, tiled=True)
     terms, maps = call(
         middle_kernel,
         "middle",
-        (shape((n, rows + 2 * cols, sketch), BF), shape((3 * b, b), BF)),
+        (held((n, rows + 2 * cols, sketch), BF), held((3 * b, b), BF)),
         [SMEM] + [VMEM] * (2 + n) + [ANY],
         [pltpu.VMEM((all_rows, sketch), BF), pltpu.VMEM((b, b), F32), pltpu.VMEM((b, b), BF)],
         flops=4 * rows * all_rows * sketch,
         moved=4 << 20,
+        limit=56,
     )(row_owner, sep_inv, *coupled, sep_link, shared)
-    maps = call(stack_kernel, "stack_maps", shape((4, 3 * b, b), BF), [VMEM] * 4, moved=1 << 18)(
-        maps, *[turned_wide(maps, "x", k) for k in (1, 2, 3)]
+    maps = call(stack_kernel, "stack_maps", held((4, 3 * b, b), BF), [VMEM] * 4, moved=1 << 18)(
+        near(maps), *[near(turned_wide(maps, "x", k)) for k in (1, 2, 3)]
     )
     maps = [maps] + [turned_wide(maps, "y", k) for k in (1, 2, 3)]
     maps_other = [swap(part, "wide", 1) for part in maps]
 
     terms = lax.all_to_all(terms, "narrow", 0, 0, tiled=True)
-    kept, packed, ag = call(
+    terms = near(terms)
+    ag = call(
+        sum_ends_kernel,
+        "sum_ends",
+        held((chips, cols, 2 * b), F32),
+        [VMEM] * 6,
+        moved=1 << 19,
+    )(terms, sep_link, *[near(part) for part in maps_other])
+    kept, packed = call(
         sum_terms_kernel,
         "sum_terms",
-        (
-            shape((rows, sketch), F32),
-            shape((2 * rows, sketch), BF),
-            shape((chips, cols, 2 * b), F32),
-        ),
-        [VMEM] * 3 + [ANY] * 4,
+        (pltpu.HBM((rows, sketch), F32), pltpu.HBM((2 * rows, sketch), BF)),
+        [VMEM] * 2 + [ANY],
         moved=2 << 20,
-    )(terms, shared, sep_link, *maps_other)
+    )(terms, shared, near(ag))
     gathered = lax.all_gather(packed, "narrow", axis=0, tiled=False)
 
     same_core = [[2 * q + c for q in range(chips)] for c in range(2)]
     ag = lax.all_to_all(ag, "wide", 0, 0, tiled=True, axis_index_groups=same_core)
-    ag_other = swap(ag, "wide", 1)
+    ag_other = near(swap(ag, "wide", 1))
+    ag = near(ag)
     z = call(
         chain_kernel,
         "chain",
-        shape((n, cols, 2 * b), F32),
-        [ANY] * 10 + [VMEM],
+        held((n, cols, 2 * b), BF),
+        [VMEM] * 2 + [ANY] * 8 + [VMEM],
         [
             pltpu.VMEM((2, chips, cols, 2 * b), F32),
             pltpu.VMEM((2, chips, 3 * b, b), BF),
             pltpu.VMEM((chain_len, cols, b), F32),
             pltpu.VMEM((chain_len, cols, b), F32),
-            pltpu.SemaphoreType.DMA((2 + 2 * chips,)),
+            pltpu.SemaphoreType.DMA((2, chips)),
         ],
         flops=2 * 9 * chain_len * cols * b * b,
         moved=8 << 20,
+        limit=56,
     )(ag, ag_other, *maps, *maps_other, sep_link)
     z = lax.all_to_all(z, "narrow", 0, 0, tiled=True).reshape(sketch, 2 * b)
 
+    base, fix, own = call(
+        before_kernel,
+        "before",
+        (
+            held((leaf_count * b, sketch), F32),
+            held((leaf_count * b, 2 * b), BF),
+            held((rows, 2 * b), BF),
+        ),
+        [SMEM] * 2 + [VMEM] * 3,
+        flops=2 * 16 * b * b * sketch,
+        moved=4 << 20,
+    )(parent, row_owner, gathered, leaf_coupling, fl)
     leaf_out, sep_out = call(
         final_kernel,
         "final",
         (shape((leaf_count * b, sketch), F32), shape((rows, sketch), F32)),
-        [SMEM] * 2 + [VMEM] * 6,
-        [pltpu.VMEM((2, sketch, 2 * b), BF)],
-        flops=2 * 40 * b * b * sketch,
-        moved=6 << 20,
-    )(parent, row_owner, kept, gathered, z, leaf_coupling, leaf_inv, fl)
+        [VMEM] * 6,
+        flops=2 * 16 * b * b * sketch,
+        moved=2 << 20,
+    )(kept, near(own), near(base), near(fix), near(z), leaf_inv)
     return leaf_out, sep_out
 
 

time: 186 us -> 171 us (0.919)
  blocking collectives: 32.6 us -> 13.1 us
  starting transfers between devices: 58.2 us -> 66.1 us
  Pallas kernels: 33.4 us -> 26.3 us
  waiting for transfers between devices: 41.3 us -> 46.6 us
    all_to_all x1 -> x0, blocking collectives: 18 us -> none  [per_device(): z = lax.all_to_all(z, 'narrow', 0, 0, tiled=True).reshape(sketch, 2 * b)]
    all_to_all x0 -> x1, starting transfers between devices: none -> 6.83 us  [per_device(): z = lax.all_to_all(z, 'narrow', 0, 0, tiled=True).reshape(sketch, 2 * b)]
    all_to_all x0 -> x1, waiting for transfers between devices: none -> 5.69 us  [per_device(): z = lax.all_to_all(z, 'narrow', 0, 0, tiled=True).reshape(sketch, 2 * b)]
    pallas_call x1, Pallas kernels: 5.12 us -> 1.54 us  [per_device(): call(final_kernel, 'final', (shape((leaf_count * b, sketch), F32), shape(...]
    pallas_call x4 -> x6, Pallas kernels: 23 us -> 20.7 us  [the longest x1 14.7 us: per_device(): call(chain_kernel, 'chain', held((n, cols, 2 * b), BF), [VMEM] * 2 + [ANY...]
    unnamed x50 -> x36, local copies, waits for them, and re-layouts: 5.25 us -> 4.14 us
  transfers between devices with their start and end apart: 28 -> 29, of which waited for: 14 -> 13; matrix products, arithmetic and copies ran while one was open for 0% -> 0% of each run, Pallas kernels for 9% -> 9%
where the time goes in v4:
time: 171 us
  starting transfers between devices  66.1 us (39%)
  waiting for transfers between devices  46.6 us (27%)
  Pallas kernels  26.3 us (15%)
  between operations  14.3 us (8%)
  blocking collectives  13.1 us (8%)
  local copies, waits for them, and re-layouts  4.14 us (2%)
    ppermute x14, waiting for transfers between devices, turned(): return lax.ppermute(value, 'narrow', [(i, (i + by) % n) for i in range(n)])  34.1 us
    ppermute x5, starting transfers between devices, swap(): return lax.ppermute(value, axis, [(i, i ^ by) for i in range(n)])  26.3 us
    ppermute x14, starting transfers between devices, turned(): return lax.ppermute(value, 'narrow', [(i, (i + by) % n) for i in range(n)])  20.4 us
    pallas_call x1, Pallas kernels, per_device(): call(chain_kernel, 'chain', held((n, cols, 2 * b), BF), [VMEM] * 2 + [ANY...  14.7 us
    all_to_all x1, blocking collectives, per_device(): lax.all_to_all(ag, 'wide', 0, 0, tiled=True, axis_index_groups=same_core)  13.1 us
    ppermute x6, starting transfers between devices, turned_wide(): return lax.ppermute(value, 'wide', [(source(i), i) for i in range(32)])  7.87 us
    all_to_all x1, starting transfers between devices, per_device(): z = lax.all_to_all(z, 'narrow', 0, 0, tiled=True).reshape(sketch, 2 * b)  6.83 us
    all_to_all x1, waiting for transfers between devices, per_device(): z = lax.all_to_all(z, 'narrow', 0, 0, tiled=True).reshape(sketch, 2 * b)  5.69 us
  transfers between devices with their start and end apart: 29, of which 13 were waited for; matrix products, arithmetic and copies ran while one was open for 0% of the time, Pallas kernels for 9%

profile of v4, /device:TPU:1, one launch (start us, length us, event | category | flops | bytes accessed | tf_op | source)
XLA Modules:
  0.0 170.9 jit_solution(15055743549220270572)
XLA Ops:
  7.2 4.1 %leaf_forward.1 = (bf16[512,256]{1,0:T(8,128)(2,1)}, bf16[2048,256]{1,0:T(8,128)(2,1)}, bf16[288,256]{1,0:T(8,128)(2,1)S(1)}, bf16[288,256]{1,0:T(8,128)(2,1)S(1...) custom-call(s32[2,4]{1,0:T(2,128)} %bitcast.5, ...), custom_call_target="tpu_custom_call" | custom-call | flops 100663296 | bytes 4194304 | tf_op jit(solution)/shard_map/leaf_forward/pallas_call | solution.py:325
  11.3 2.5 %collective-permute-start = (bf16[288,256]{1,0:T(8,128)(2,1)S(1)}, bf16[288,256]{1,0:T(8,128)(2,1)S(1)}, u32[]{:S(2)}, u32[]{:S(2)}) collective-permute-start(bf16[288,256]{1,0:T(8,128)(2,1)S(1)} %get-tuple-element.19), channel_id=1, source_target_pairs={{0,1},{1,2},{2,3},{3,4},{4,5},{5,6},{6,7},{7,0},{8,9},{9,10},{10,1... | collective-permute-start | bytes 442376 | tf_op jit(solution)/shard_map/ppermute | solution.py:272
  13.8 4.0 %collective-permute-start.4 = (bf16[288,256]{1,0:T(8,128)(2,1)S(1)}, bf16[288,256]{1,0:T(8,128)(2,1)S(1)}, u32[]{:S(2)}, u32[]{:S(2)}) collective-permute-start(bf16[288,256]{1,0:T(8,128)(2,1)S(1)} %get-tuple-element.23), channel_id=1, source_target_pairs={{0,7},{1,0},{2,1},{3,2},{4,3},{5,4},{6,5},{7,6},{8,15},{9,8},{10,9... | collective-permute-start | bytes 442376 | tf_op jit(solution)/shard_map/ppermute | solution.py:272
  17.9 3.5 %collective-permute-done = bf16[288,256]{1,0:T(8,128)(2,1)S(1)} collective-permute-done((bf16[288,256]{1,0:T(8,128)(2,1)S(1)}, bf16[288,256]{1,0:T(8,128)(2,1)S(1)}, u32[]{:S(2)}, u32[]{:S(2)}) %collective-permute-start) | collective-permute-done | bytes 147488 | tf_op jit(solution)/shard_map/ppermute | solution.py:272
  21.4 0.1 collective-permute-start.1
  21.5 2.7 %collective-permute-start.5 = (bf16[288,256]{1,0:T(8,128)(2,1)S(1)}, bf16[288,256]{1,0:T(8,128)(2,1)S(1)}, u32[]{:S(2)}, u32[]{:S(2)}) collective-permute-start(bf16[288,256]{1,0:T(8,128)(2,1)S(1)} %add_convert_fusion.1), channel_id=1, source_target_pairs={{0,7},{1,0},{2,1},{3,2},{4,3},{5,4},{6,5},{7,6},{8,15},{9,8},{10,9... | collective-permute-start | bytes 442376 | tf_op jit(solution)/shard_map/ppermute | solution.py:272
  24.3 2.4 %collective-permute-done.1 = bf16[288,256]{1,0:T(8,128)(2,1)S(1)} collective-permute-done((bf16[288,256]{1,0:T(8,128)(2,1)S(1)}, bf16[288,256]{1,0:T(8,128)(2,1)S(1)}, u32[]{:S(2)}, u32[]{:S(2)}) %collective-permute-start.1) | collective-permute-done | bytes 147488 | tf_op jit(solution)/shard_map/ppermute | solution.py:272
  26.7 0.1 collective-permute-start.2
  26.9 2.7 %collective-permute-start.6 = (bf16[288,256]{1,0:T(8,128)(2,1)S(1)}, bf16[288,256]{1,0:T(8,128)(2,1)S(1)}, u32[]{:S(2)}, u32[]{:S(2)}) collective-permute-start(bf16[288,256]{1,0:T(8,128)(2,1)S(1)} %add_convert_fusion), channel_id=1, source_target_pairs={{0,7},{1,0},{2,1},{3,2},{4,3},{5,4},{6,5},{7,6},{8,15},{9,8},{10,9... | collective-permute-start | bytes 442376 | tf_op jit(solution)/shard_map/ppermute | solution.py:272
  29.6 4.2 %collective-permute-done.2 = bf16[288,256]{1,0:T(8,128)(2,1)S(1)} collective-permute-done((bf16[288,256]{1,0:T(8,128)(2,1)S(1)}, bf16[288,256]{1,0:T(8,128)(2,1)S(1)}, u32[]{:S(2)}, u32[]{:S(2)}) %collective-permute-start.2) | collective-permute-done | bytes 147488 | tf_op jit(solution)/shard_map/ppermute | solution.py:272
  33.8 0.1 collective-permute-start.3
  33.9 6.6 %collective-permute-done.3.right = bf16[288,256]{1,0:T(8,128)(2,1)S(1)} collective-permute-done((bf16[288,256]{1,0:T(8,128)(2,1)S(1)}, bf16[288,256]{1,0:T(8,128)(2,1)S(1)}, u32[]{:S(2)}, u32[]{:S(2)}) %collective-permute-start.3) | collective-permute-done | bytes 147488 | tf_op jit(solution)/shard_map/ppermute | solution.py:272
  40.6 2.7 %collective-permute-start.7 = (bf16[288,256]{1,0:T(8,128)(2,1)S(1)}, bf16[288,256]{1,0:T(8,128)(2,1)S(1)}, u32[]{:S(2)}, u32[]{:S(2)}) collective-permute-start(bf16[288,256]{1,0:T(8,128)(2,1)S(1)} %sum_own.1.refs_0_), channel_id=1, source_target_pairs={{0,7},{1,0},{2,1},{3,2},{4,3},{5,4},{6,5},{7,6},{8,15},{9,8},{10,9... | collective-permute-start | bytes 442376 | tf_op jit(solution)/shard_map/ppermute | solution.py:272
  43.3 4.4 %collective-permute-done.10.refs_7_ = bf16[288,256]{1,0:T(8,128)(2,1)S(1)} collective-permute-done((bf16[288,256]{1,0:T(8,128)(2,1)S(1)}, bf16[288,256]{1,0:T(8,128)(2,1)S(1)}, u32[]{:S(2)}, u32[]{:S(2)}) %collective-permute-start.10) | collective-permute-done | bytes 147488 | tf_op jit(solution)/shard_map/ppermute | solution.py:272
  47.7 2.7 %collective-permute-start.8 = (bf16[288,256]{1,0:T(8,128)(2,1)S(1)}, bf16[288,256]{1,0:T(8,128)(2,1)S(1)}, u32[]{:S(2)}, u32[]{:S(2)}) collective-permute-start(bf16[288,256]{1,0:T(8,128)(2,1)S(1)} %collective-permute-done.7.refs_1_), channel_id=1, source_target_pairs={{0,7},{1,0},{2,1},{3,2},{4,3},{5,4},{6,5},{7,6},{8,15},{9,8},{10,9... | collective-permute-start | bytes 442376 | tf_op jit(solution)/shard_map/ppermute | solution.py:272
  50.4 3.3 %collective-permute-done.11.refs_6_ = bf16[288,256]{1,0:T(8,128)(2,1)S(1)} collective-permute-done((bf16[288,256]{1,0:T(8,128)(2,1)S(1)}, bf16[288,256]{1,0:T(8,128)(2,1)S(1)}, u32[]{:S(2)}, u32[]{:S(2)}) %collective-permute-start.11) | collective-permute-done | bytes 147488 | tf_op jit(solution)/shard_map/ppermute | solution.py:272
  53.7 2.7 %collective-permute-start.9 = (bf16[288,256]{1,0:T(8,128)(2,1)S(1)}, bf16[288,256]{1,0:T(8,128)(2,1)S(1)}, u32[]{:S(2)}, u32[]{:S(2)}) collective-permute-start(bf16[288,256]{1,0:T(8,128)(2,1)S(1)} %collective-permute-done.8.refs_2_), channel_id=1, source_target_pairs={{0,7},{1,0},{2,1},{3,2},{4,3},{5,4},{6,5},{7,6},{8,15},{9,8},{10,9... | collective-permute-start | bytes 442376 | tf_op jit(solution)/shard_map/ppermute | solution.py:272
  56.4 2.9 %collective-permute-done.12.refs_5_ = bf16[288,256]{1,0:T(8,128)(2,1)S(1)} collective-permute-done((bf16[288,256]{1,0:T(8,128)(2,1)S(1)}, bf16[288,256]{1,0:T(8,128)(2,1)S(1)}, u32[]{:S(2)}, u32[]{:S(2)}) %collective-permute-start.12) | collective-permute-done | bytes 147488 | tf_op jit(solution)/shard_map/ppermute | solution.py:272
  59.2 6.9 %collective-permute-done.13.refs_4_ = bf16[288,256]{1,0:T(8,128)(2,1)S(1)} collective-permute-done((bf16[288,256]{1,0:T(8,128)(2,1)S(1)}, bf16[288,256]{1,0:T(8,128)(2,1)S(1)}, u32[]{:S(2)}, u32[]{:S(2)}) %collective-permute-start.13) | collective-permute-done | bytes 147488 | tf_op jit(solution)/shard_map/ppermute | solution.py:272
  66.1 3.8 %middle.1 = (bf16[8,320,256]{2,1,0:T(8,128)(2,1)}, bf16[384,128]{1,0:T(8,128)(2,1)S(1)}) custom-call(s32[1,8]{1,0:T(1,128)} %owners.5, bf16[256,2048]{1,0:T(8,128)(2,1)} %inv.4, bf16[288,256]{1,0:T(8,128)(2,1)S(1)} %sum_own.1.refs_0_, bf16[288,256]{1,0:T(8,128)(2,1)S(1)} %collective-permute-done.7.refs_1_, ...), custom_call_target="tpu_custom_call" | custom-call | flops 536870912 | bytes 4194304 | tf_op jit(solution)/shard_map/middle/pallas_call | solution.py:343
  69.9 4.7 %all-to-all-start = ((bf16[8,320,256]{2,1,0:T(8,128)(2,1)}), bf16[8,320,256]{2,1,0:T(8,128)(2,1)S(1)}, u32[]{:S(2)}, u32[]{:S(2)}) async-start(bf16[8,320,256]{2,1,0:T(8,128)(2,1)} %get-tuple-element.28), calls=%async_computation.1 | async-start | bytes 2621440 | tf_op jit(solution)/shard_map/all_to_all | solution.py:359
  74.6 1.7 %collective-permute-start.14 = (bf16[384,128]{1,0:T(8,128)(2,1)S(1)}, bf16[384,128]{1,0:T(8,128)(2,1)S(1)}, u32[]{:S(2)}, u32[]{:S(2)}) collective-permute-start(bf16[384,128]{1,0:T(8,128)(2,1)S(1)} %get-tuple-element.29.refs_0_), channel_id=1, source_target_pairs={{16,0},{24,8},{32,16},{40,24},{48,32},{56,40},{0,48},{8,56},{80,64... | collective-permute-start | bytes 294920 | tf_op jit(solution)/shard_map/ppermute | solution.py:305
  76.4 1.3 collective-permute-start.15
  77.6 0.8 collective-permute-start.16
  78.4 2.9 %collective-permute-done.15.refs_2_ = bf16[384,128]{1,0:T(8,128)(2,1)S(1)} collective-permute-done((bf16[384,128]{1,0:T(8,128)(2,1)S(1)}, bf16[384,128]{1,0:T(8,128)(2,1)S(1)}, u32[]{:S(2)}, u32[]{:S(2)}) %collective-permute-start.15) | collective-permute-done | bytes 98336 | tf_op jit(solution)/shard_map/ppermute | solution.py:305
  81.3 1.1 collective-permute-done.16.refs_3_
  82.4 2.9 %collective-permute-start.18 = (bf16[4,384,128]{2,1,0:T(8,128)(2,1)S(1)}, bf16[4,384,128]{2,1,0:T(8,128)(2,1)S(1)}, u32[]{:S(2)}, u32[]{:S(2)}) collective-permute-start(bf16[4,384,128]{2,1,0:T(8,128)(2,1)S(1)} %stack_maps.1.refs_2_), channel_id=1, source_target_pairs={{64,0},{72,8},{80,16},{88,24},{96,32},{104,40},{112,48},{120,56},{... | collective-permute-start | bytes 1179656 | tf_op jit(solution)/shard_map/ppermute | solution.py:305
  85.3 0.9 collective-permute-start.20
  86.2 0.3 collective-permute-start.22
  86.5 12.4 %collective-permute-start.17 = (bf16[4,384,128]{2,1,0:T(8,128)(2,1)S(1)}, bf16[4,384,128]{2,1,0:T(8,128)(2,1)S(1)}, u32[]{:S(2)}, u32[]{:S(2)}) collective-permute-start(bf16[4,384,128]{2,1,0:T(8,128)(2,1)S(1)} %stack_maps.1.refs_2_), channel_id=1, source_target_pairs={{0,8},{8,0},{16,24},{24,16},{32,40},{40,32},{48,56},{56,48},{64,72... | collective-permute-start | bytes 1179656 | tf_op jit(solution)/shard_map/ppermute | solution.py:267
  98.9 7.9 %collective-permute-start.19 = (bf16[4,384,128]{2,1,0:T(8,128)(2,1)S(1)}, bf16[4,384,128]{2,1,0:T(8,128)(2,1)S(1)}, u32[]{:S(2)}, u32[]{:S(2)}) collective-permute-start(bf16[4,384,128]{2,1,0:T(8,128)(2,1)S(1)} %collective-permute-done.18.refs_3_), channel_id=1, source_target_pairs={{0,8},{8,0},{16,24},{24,16},{32,40},{40,32},{48,56},{56,48},{64,72... | collective-permute-start | bytes 1179656 | tf_op jit(solution)/shard_map/ppermute | solution.py:267
  106.8 0.1 collective-permute-start.21
  106.9 3.9 %collective-permute-start.23 = (bf16[4,384,128]{2,1,0:T(8,128)(2,1)S(1)}, bf16[4,384,128]{2,1,0:T(8,128)(2,1)S(1)}, u32[]{:S(2)}, u32[]{:S(2)}) collective-permute-start(bf16[4,384,128]{2,1,0:T(8,128)(2,1)S(1)} %collective-permute-done.22.refs_5_), channel_id=1, source_target_pairs={{0,8},{8,0},{16,24},{24,16},{32,40},{40,32},{48,56},{56,48},{64,72... | collective-permute-start | bytes 1179656 | tf_op jit(solution)/shard_map/ppermute | solution.py:267
  110.8 1.3 collective-permute-done.23.refs_3_.refs_9_
  112.1 0.7 copy-done.5
  112.9 1.0 copy-done.6
  113.9 0.8 copy-done.10
  114.6 0.2 sum_ends.1._
  114.9 0.9 sum_terms.1
  115.8 13.1 %all_to_all.15.refs_0_ = f32[16,32,256]{2,1,0:T(8,128)S(1)} all-to-all(f32[16,32,256]{2,1,0:T(8,128)S(1)} %sum_ends.1._), channel_id=1, replica_groups={{0,16,32,48,64,80,96,112,128,144,160,176,192,208,224,240},{8,24,40,56,7..., dimensions={0} | all-to-all | bytes 1048576 | tf_op jit(solution)/shard_map/all_to_all | solution.py:378
  128.9 2.1 %collective-permute-start.24 = (f32[16,32,256]{2,1,0:T(8,128)S(1)}, f32[16,32,256]{2,1,0:T(8,128)S(1)}, u32[]{:S(2)}, u32[]{:S(2)}) collective-permute-start(f32[16,32,256]{2,1,0:T(8,128)S(1)} %all_to_all.15.refs_0_), channel_id=1, source_target_pairs={{0,8},{8,0},{16,24},{24,16},{32,40},{40,32},{48,56},{56,48},{64,72... | collective-permute-start | bytes 1572872 | tf_op jit(solution)/shard_map/ppermute | solution.py:267
  131.0 1.5 collective-permute-done.24.refs_1_
  132.6 14.7 %chain.1 = bf16[8,32,256]{2,1,0:T(8,128)(2,1)} custom-call(f32[16,32,256]{2,1,0:T(8,128)S(1)} %all_to_all.15.refs_0_, f32[16,32,256]{2,1,0:T(8,128)S(1)} %collective-permute-done.24.refs_1_, bf16[4,384,128]{2,1,0:T(8,128)(2,1)} %copy-done.1, bf16[4,384,128]{2,1,0:T(8,128)(2,1)} %copy-done.15, bf16[4,384,128]{2,1,0:T(8,128)(2,1)} %copy-done.16, ...), custom_call_target="tpu_custom_call" | custom-call | flops 301989888 | bytes 8388608 | tf_op jit(solution)/shard_map/chain/pallas_call | solution.py:381
  147.3 6.8 %all-to-all-start.2 = ((bf16[8,32,256]{2,1,0:T(8,128)(2,1)}), bf16[8,32,256]{2,1,0:T(8,128)(2,1)S(1)}, u32[]{:S(2)}, u32[]{:S(2)}) async-start(bf16[8,32,256]{2,1,0:T(8,128)(2,1)} %chain.1), calls=%async_computation.3 | async-start | bytes 262144 | tf_op jit(solution)/shard_map/all_to_all | solution.py:397
  154.2 1.6 copy-done
  155.8 1.0 before.1
  156.8 5.7 %all-to-all-done.2 = bf16[8,32,256]{2,1,0:T(8,128)(2,1)S(1)} async-done(((bf16[8,32,256]{2,1,0:T(8,128)(2,1)}), bf16[8,32,256]{2,1,0:T(8,128)(2,1)S(1)}, u32[]{:S(2)}, u32[]{:S(2)}) %all-to-all-start.2) | async-done | bytes 131104 | tf_op jit(solution)/shard_map/all_to_all | solution.py:397
  162.5 1.5 final.1
  (63 shorter events, 0.6 us)
Async XLA Ops:
  7.2 58.9 %reduce-scatter.2.cloned.1.call-start = ((), (), s32[]{:S(2)}) async-start(), calls=%async_computation.4 | async-start | bytes 1179648 | tf_op jit(solution)/shard_map/reduce_scatter | solution.py:342
  11.3 10.1 %collective-permute-start = (bf16[288,256]{1,0:T(8,128)(2,1)S(1)}, bf16[288,256]{1,0:T(8,128)(2,1)S(1)}, u32[]{:S(2)}, u32[]{:S(2)}) collective-permute-start(bf16[288,256]{1,0:T(8,128)(2,1)S(1)} %get-tuple-element.19), channel_id=1, source_target_pairs={{0,1},{1,2},{2,3},{3,4},{4,5},{5,6},{6,7},{7,0},{8,9},{9,10},{10,1... | collective-permute-start | bytes 442376 | tf_op jit(solution)/shard_map/ppermute | solution.py:272
  13.8 7.6 %collective-permute-start.4 = (bf16[288,256]{1,0:T(8,128)(2,1)S(1)}, bf16[288,256]{1,0:T(8,128)(2,1)S(1)}, u32[]{:S(2)}, u32[]{:S(2)}) collective-permute-start(bf16[288,256]{1,0:T(8,128)(2,1)S(1)} %get-tuple-element.23), channel_id=1, source_target_pairs={{0,7},{1,0},{2,1},{3,2},{4,3},{5,4},{6,5},{7,6},{8,15},{9,8},{10,9... | collective-permute-start | bytes 442376 | tf_op jit(solution)/shard_map/ppermute | solution.py:272
  21.4 5.3 %collective-permute-start.1 = (bf16[288,256]{1,0:T(8,128)(2,1)S(1)}, bf16[288,256]{1,0:T(8,128)(2,1)S(1)}, u32[]{:S(2)}, u32[]{:S(2)}) collective-permute-start(bf16[288,256]{1,0:T(8,128)(2,1)S(1)} %add_convert_fusion.4), channel_id=1, source_target_pairs={{0,1},{1,2},{2,3},{3,4},{4,5},{5,6},{6,7},{7,0},{8,9},{9,10},{10,1... | collective-permute-start | bytes 442376 | tf_op jit(solution)/shard_map/ppermute | solution.py:272
  21.5 5.3 %collective-permute-start.5 = (bf16[288,256]{1,0:T(8,128)(2,1)S(1)}, bf16[288,256]{1,0:T(8,128)(2,1)S(1)}, u32[]{:S(2)}, u32[]{:S(2)}) collective-permute-start(bf16[288,256]{1,0:T(8,128)(2,1)S(1)} %add_convert_fusion.1), channel_id=1, source_target_pairs={{0,7},{1,0},{2,1},{3,2},{4,3},{5,4},{6,5},{7,6},{8,15},{9,8},{10,9... | collective-permute-start | bytes 442376 | tf_op jit(solution)/shard_map/ppermute | solution.py:272
  26.7 7.0 %collective-permute-start.2 = (bf16[288,256]{1,0:T(8,128)(2,1)S(1)}, bf16[288,256]{1,0:T(8,128)(2,1)S(1)}, u32[]{:S(2)}, u32[]{:S(2)}) collective-permute-start(bf16[288,256]{1,0:T(8,128)(2,1)S(1)} %add_convert_fusion.3), channel_id=1, source_target_pairs={{0,1},{1,2},{2,3},{3,4},{4,5},{5,6},{6,7},{7,0},{8,9},{9,10},{10,1... | collective-permute-start | bytes 442376 | tf_op jit(solution)/shard_map/ppermute | solution.py:272
  26.9 7.0 %collective-permute-start.6 = (bf16[288,256]{1,0:T(8,128)(2,1)S(1)}, bf16[288,256]{1,0:T(8,128)(2,1)S(1)}, u32[]{:S(2)}, u32[]{:S(2)}) collective-permute-start(bf16[288,256]{1,0:T(8,128)(2,1)S(1)} %add_convert_fusion), channel_id=1, source_target_pairs={{0,7},{1,0},{2,1},{3,2},{4,3},{5,4},{6,5},{7,6},{8,15},{9,8},{10,9... | collective-permute-start | bytes 442376 | tf_op jit(solution)/shard_map/ppermute | solution.py:272
  33.8 6.7 %collective-permute-start.3 = (bf16[288,256]{1,0:T(8,128)(2,1)S(1)}, bf16[288,256]{1,0:T(8,128)(2,1)S(1)}, u32[]{:S(2)}, u32[]{:S(2)}) collective-permute-start(bf16[288,256]{1,0:T(8,128)(2,1)S(1)} %add_convert_fusion.2), channel_id=1, source_target_pairs={{0,1},{1,2},{2,3},{3,4},{4,5},{5,6},{6,7},{7,0},{8,9},{9,10},{10,1... | collective-permute-start | bytes 442376 | tf_op jit(solution)/shard_map/ppermute | solution.py:272
  40.5 7.2 %collective-permute-start.10 = (bf16[288,256]{1,0:T(8,128)(2,1)S(1)}, bf16[288,256]{1,0:T(8,128)(2,1)S(1)}, u32[]{:S(2)}, u32[]{:S(2)}) collective-permute-start(bf16[288,256]{1,0:T(8,128)(2,1)S(1)} %sum_own.1.refs_0_), channel_id=1, source_target_pairs={{0,1},{1,2},{2,3},{3,4},{4,5},{5,6},{6,7},{7,0},{8,9},{9,10},{10,1... | collective-permute-start | bytes 442376 | tf_op jit(solution)/shard_map/ppermute | solution.py:272
  40.6 7.1 %collective-permute-start.7 = (bf16[288,256]{1,0:T(8,128)(2,1)S(1)}, bf16[288,256]{1,0:T(8,128)(2,1)S(1)}, u32[]{:S(2)}, u32[]{:S(2)}) collective-permute-start(bf16[288,256]{1,0:T(8,128)(2,1)S(1)} %sum_own.1.refs_0_), channel_id=1, source_target_pairs={{0,7},{1,0},{2,1},{3,2},{4,3},{5,4},{6,5},{7,6},{8,15},{9,8},{10,9... | collective-permute-start | bytes 442376 | tf_op jit(solution)/shard_map/ppermute | solution.py:272
  47.7 6.0 %collective-permute-start.11 = (bf16[288,256]{1,0:T(8,128)(2,1)S(1)}, bf16[288,256]{1,0:T(8,128)(2,1)S(1)}, u32[]{:S(2)}, u32[]{:S(2)}) collective-permute-start(bf16[288,256]{1,0:T(8,128)(2,1)S(1)} %collective-permute-done.10.refs_7_), channel_id=1, source_target_pairs={{0,1},{1,2},{2,3},{3,4},{4,5},{5,6},{6,7},{7,0},{8,9},{9,10},{10,1... | collective-permute-start | bytes 442376 | tf_op jit(solution)/shard_map/ppermute | solution.py:272
  47.7 6.0 %collective-permute-start.8 = (bf16[288,256]{1,0:T(8,128)(2,1)S(1)}, bf16[288,256]{1,0:T(8,128)(2,1)S(1)}, u32[]{:S(2)}, u32[]{:S(2)}) collective-permute-start(bf16[288,256]{1,0:T(8,128)(2,1)S(1)} %collective-permute-done.7.refs_1_), channel_id=1, source_target_pairs={{0,7},{1,0},{2,1},{3,2},{4,3},{5,4},{6,5},{7,6},{8,15},{9,8},{10,9... | collective-permute-start | bytes 442376 | tf_op jit(solution)/shard_map/ppermute | solution.py:272
  53.7 5.6 %collective-permute-start.12 = (bf16[288,256]{1,0:T(8,128)(2,1)S(1)}, bf16[288,256]{1,0:T(8,128)(2,1)S(1)}, u32[]{:S(2)}, u32[]{:S(2)}) collective-permute-start(bf16[288,256]{1,0:T(8,128)(2,1)S(1)} %collective-permute-done.11.refs_6_), channel_id=1, source_target_pairs={{0,1},{1,2},{2,3},{3,4},{4,5},{5,6},{6,7},{7,0},{8,9},{9,10},{10,1... | collective-permute-start | bytes 442376 | tf_op jit(solution)/shard_map/ppermute | solution.py:272
  53.7 5.6 %collective-permute-start.9 = (bf16[288,256]{1,0:T(8,128)(2,1)S(1)}, bf16[288,256]{1,0:T(8,128)(2,1)S(1)}, u32[]{:S(2)}, u32[]{:S(2)}) collective-permute-start(bf16[288,256]{1,0:T(8,128)(2,1)S(1)} %collective-permute-done.8.refs_2_), channel_id=1, source_target_pairs={{0,7},{1,0},{2,1},{3,2},{4,3},{5,4},{6,5},{7,6},{8,15},{9,8},{10,9... | collective-permute-start | bytes 442376 | tf_op jit(solution)/shard_map/ppermute | solution.py:272
  59.2 6.9 %collective-permute-start.13 = (bf16[288,256]{1,0:T(8,128)(2,1)S(1)}, bf16[288,256]{1,0:T(8,128)(2,1)S(1)}, u32[]{:S(2)}, u32[]{:S(2)}) collective-permute-start(bf16[288,256]{1,0:T(8,128)(2,1)S(1)} %collective-permute-done.12.refs_5_), channel_id=1, source_target_pairs={{0,1},{1,2},{2,3},{3,4},{4,5},{5,6},{6,7},{7,0},{8,9},{9,10},{10,1... | collective-permute-start | bytes 442376 | tf_op jit(solution)/shard_map/ppermute | solution.py:272
  69.9 43.0 %all-to-all-start = ((bf16[8,320,256]{2,1,0:T(8,128)(2,1)}), bf16[8,320,256]{2,1,0:T(8,128)(2,1)S(1)}, u32[]{:S(2)}, u32[]{:S(2)}) async-start(bf16[8,320,256]{2,1,0:T(8,128)(2,1)} %get-tuple-element.28), calls=%async_computation.1 | async-start | bytes 2621440 | tf_op jit(solution)/shard_map/all_to_all | solution.py:359
  74.6 79.6 %all-gather.3.cloned.1.call-start = ((), (), s32[]{:S(2)}) async-start(), calls=%async_computation.5 | async-start | bytes 2359296 | tf_op jit(solution)/shard_map/all_gather | solution.py:375
  74.6 3.8 %collective-permute-start.14 = (bf16[384,128]{1,0:T(8,128)(2,1)S(1)}, bf16[384,128]{1,0:T(8,128)(2,1)S(1)}, u32[]{:S(2)}, u32[]{:S(2)}) collective-permute-start(bf16[384,128]{1,0:T(8,128)(2,1)S(1)} %get-tuple-element.29.refs_0_), channel_id=1, source_target_pairs={{16,0},{24,8},{32,16},{40,24},{48,32},{56,40},{0,48},{8,56},{80,64... | collective-permute-start | bytes 294920 | tf_op jit(solution)/shard_map/ppermute | solution.py:305
  76.4 5.0 %collective-permute-start.15 = (bf16[384,128]{1,0:T(8,128)(2,1)S(1)}, bf16[384,128]{1,0:T(8,128)(2,1)S(1)}, u32[]{:S(2)}, u32[]{:S(2)}) collective-permute-start(bf16[384,128]{1,0:T(8,128)(2,1)S(1)} %get-tuple-element.29.refs_0_), channel_id=1, source_target_pairs={{32,0},{40,8},{48,16},{56,24},{0,32},{8,40},{16,48},{24,56},{96,64... | collective-permute-start | bytes 294920 | tf_op jit(solution)/shard_map/ppermute | solution.py:305
  77.6 4.7 %collective-permute-start.16 = (bf16[384,128]{1,0:T(8,128)(2,1)S(1)}, bf16[384,128]{1,0:T(8,128)(2,1)S(1)}, u32[]{:S(2)}, u32[]{:S(2)}) collective-permute-start(bf16[384,128]{1,0:T(8,128)(2,1)S(1)} %get-tuple-element.29.refs_0_), channel_id=1, source_target_pairs={{48,0},{56,8},{0,16},{8,24},{16,32},{24,40},{32,48},{40,56},{112,6... | collective-permute-start | bytes 294920 | tf_op jit(solution)/shard_map/ppermute | solution.py:305
  82.4 32.5 %copy-start.9 = (bf16[256,256]{1,0:T(8,128)(2,1)S(1)}, bf16[256,256]{1,0:T(8,128)(2,1)}, u32[]{:S(2)}) copy-start(bf16[256,256]{1,0:T(8,128)(2,1)} %reduce-scatter.2.cloned.1.call-done.refs_9_.shared) | copy-start | bytes 393220
  82.4 32.4 %copy-start.1 = (bf16[4,384,128]{2,1,0:T(8,128)(2,1)}, bf16[4,384,128]{2,1,0:T(8,128)(2,1)S(1)}, u32[]{:S(2)}) copy-start(bf16[4,384,128]{2,1,0:T(8,128)(2,1)S(1)} %stack_maps.1.refs_2_) | copy-start | bytes 1179652
  82.4 16.5 %collective-permute-start.18 = (bf16[4,384,128]{2,1,0:T(8,128)(2,1)S(1)}, bf16[4,384,128]{2,1,0:T(8,128)(2,1)S(1)}, u32[]{:S(2)}, u32[]{:S(2)}) collective-permute-start(bf16[4,384,128]{2,1,0:T(8,128)(2,1)S(1)} %stack_maps.1.refs_2_), channel_id=1, source_target_pairs={{64,0},{72,8},{80,16},{88,24},{96,32},{104,40},{112,48},{120,56},{... | collective-permute-start | bytes 1179656 | tf_op jit(solution)/shard_map/ppermute | solution.py:305
  85.3 21.5 %collective-permute-start.20 = (bf16[4,384,128]{2,1,0:T(8,128)(2,1)S(1)}, bf16[4,384,128]{2,1,0:T(8,128)(2,1)S(1)}, u32[]{:S(2)}, u32[]{:S(2)}) collective-permute-start(bf16[4,384,128]{2,1,0:T(8,128)(2,1)S(1)} %stack_maps.1.refs_2_), channel_id=1, source_target_pairs={{128,0},{136,8},{144,16},{152,24},{160,32},{168,40},{176,48},{184,... | collective-permute-start | bytes 1179656 | tf_op jit(solution)/shard_map/ppermute | solution.py:305
  86.2 20.7 %collective-permute-start.22 = (bf16[4,384,128]{2,1,0:T(8,128)(2,1)S(1)}, bf16[4,384,128]{2,1,0:T(8,128)(2,1)S(1)}, u32[]{:S(2)}, u32[]{:S(2)}) collective-permute-start(bf16[4,384,128]{2,1,0:T(8,128)(2,1)S(1)} %stack_maps.1.refs_2_), channel_id=1, source_target_pairs={{192,0},{200,8},{208,16},{216,24},{224,32},{232,40},{240,48},{248,... | collective-permute-start | bytes 1179656 | tf_op jit(solution)/shard_map/ppermute | solution.py:305
  86.5 24.3 %collective-permute-start.17 = (bf16[4,384,128]{2,1,0:T(8,128)(2,1)S(1)}, bf16[4,384,128]{2,1,0:T(8,128)(2,1)S(1)}, u32[]{:S(2)}, u32[]{:S(2)}) collective-permute-start(bf16[4,384,128]{2,1,0:T(8,128)(2,1)S(1)} %stack_maps.1.refs_2_), channel_id=1, source_target_pairs={{0,8},{8,0},{16,24},{24,16},{32,40},{40,32},{48,56},{56,48},{64,72... | collective-permute-start | bytes 1179656 | tf_op jit(solution)/shard_map/ppermute | solution.py:267
  98.9 11.9 %copy-start.15 = (bf16[4,384,128]{2,1,0:T(8,128)(2,1)}, bf16[4,384,128]{2,1,0:T(8,128)(2,1)S(1)}, u32[]{:S(2)}) copy-start(bf16[4,384,128]{2,1,0:T(8,128)(2,1)S(1)} %collective-permute-done.18.refs_3_) | copy-start | bytes 1179652
  98.9 11.9 %collective-permute-start.19 = (bf16[4,384,128]{2,1,0:T(8,128)(2,1)S(1)}, bf16[4,384,128]{2,1,0:T(8,128)(2,1)S(1)}, u32[]{:S(2)}, u32[]{:S(2)}) collective-permute-start(bf16[4,384,128]{2,1,0:T(8,128)(2,1)S(1)} %collective-permute-done.18.refs_3_), channel_id=1, source_target_pairs={{0,8},{8,0},{16,24},{24,16},{32,40},{40,32},{48,56},{56,48},{64,72... | collective-permute-start | bytes 1179656 | tf_op jit(solution)/shard_map/ppermute | solution.py:267
  106.8 4.0 %copy-start.16 = (bf16[4,384,128]{2,1,0:T(8,128)(2,1)}, bf16[4,384,128]{2,1,0:T(8,128)(2,1)S(1)}, u32[]{:S(2)}) copy-start(bf16[4,384,128]{2,1,0:T(8,128)(2,1)S(1)} %collective-permute-done.20.refs_4_) | copy-start | bytes 1179652
  106.8 4.0 %collective-permute-start.21 = (bf16[4,384,128]{2,1,0:T(8,128)(2,1)S(1)}, bf16[4,384,128]{2,1,0:T(8,128)(2,1)S(1)}, u32[]{:S(2)}, u32[]{:S(2)}) collective-permute-start(bf16[4,384,128]{2,1,0:T(8,128)(2,1)S(1)} %collective-permute-done.20.refs_4_), channel_id=1, source_target_pairs={{0,8},{8,0},{16,24},{24,16},{32,40},{40,32},{48,56},{56,48},{64,72... | collective-permute-start | bytes 1179656 | tf_op jit(solution)/shard_map/ppermute | solution.py:267
  106.9 3.9 %copy-start.17 = (bf16[4,384,128]{2,1,0:T(8,128)(2,1)}, bf16[4,384,128]{2,1,0:T(8,128)(2,1)S(1)}, u32[]{:S(2)}) copy-start(bf16[4,384,128]{2,1,0:T(8,128)(2,1)S(1)} %collective-permute-done.22.refs_5_) | copy-start | bytes 1179652
  106.9 5.2 %collective-permute-start.23 = (bf16[4,384,128]{2,1,0:T(8,128)(2,1)S(1)}, bf16[4,384,128]{2,1,0:T(8,128)(2,1)S(1)}, u32[]{:S(2)}, u32[]{:S(2)}) collective-permute-start(bf16[4,384,128]{2,1,0:T(8,128)(2,1)S(1)} %collective-permute-done.22.refs_5_), channel_id=1, source_target_pairs={{0,8},{8,0},{16,24},{24,16},{32,40},{40,32},{48,56},{56,48},{64,72... | collective-permute-start | bytes 1179656 | tf_op jit(solution)/shard_map/ppermute | solution.py:267
  110.8 4.1 %copy-start.2 = (bf16[4,384,128]{2,1,0:T(8,128)(2,1)}, bf16[4,384,128]{2,1,0:T(8,128)(2,1)S(1)}, u32[]{:S(2)}) copy-start(bf16[4,384,128]{2,1,0:T(8,128)(2,1)S(1)} %collective-permute-done.17.refs_0_.refs_6_) | copy-start | bytes 1179652
  110.8 4.1 %copy-start.3 = (bf16[4,384,128]{2,1,0:T(8,128)(2,1)}, bf16[4,384,128]{2,1,0:T(8,128)(2,1)S(1)}, u32[]{:S(2)}) copy-start(bf16[4,384,128]{2,1,0:T(8,128)(2,1)S(1)} %collective-permute-done.19.refs_1_.refs_7_) | copy-start | bytes 1179652
  110.8 4.0 %copy-start.4 = (bf16[4,384,128]{2,1,0:T(8,128)(2,1)}, bf16[4,384,128]{2,1,0:T(8,128)(2,1)S(1)}, u32[]{:S(2)}) copy-start(bf16[4,384,128]{2,1,0:T(8,128)(2,1)S(1)} %collective-permute-done.21.refs_2_.refs_8_) | copy-start | bytes 1179652
  112.1 0.7 copy-start.5
  112.9 1.0 copy-start.6
  113.9 0.8 copy-start.10
  128.9 25.2 %copy-start.7 = (bf16[4,2,128,128]{3,2,1,0:T(8,128)(2,1)S(1)}, bf16[4,2,128,128]{3,2,1,0:T(8,128)(2,1)}, u32[]{:S(2)}) copy-start(bf16[4,2,128,128]{3,2,1,0:T(8,128)(2,1)} %cpl.3) | copy-start | bytes 786436
  128.9 25.2 %copy-start.12 = (bf16[512,256]{1,0:T(8,128)(2,1)S(1)}, bf16[512,256]{1,0:T(8,128)(2,1)}, u32[]{:S(2)}) copy-start(bf16[512,256]{1,0:T(8,128)(2,1)} %get-tuple-element.32.fl) | copy-start | bytes 786436
  128.9 25.2 %copy-start.13 = (s32[1,8]{1,0:T(1,128)S(1)}, s32[1,8]{1,0:T(1,128)}, u32[]{:S(2)}) copy-start(s32[1,8]{1,0:T(1,128)} %owners.5) | copy-start | bytes 100
  128.9 25.2 %copy-start.14 = (s32[4,2]{0,1:T(2,128)S(1)}, s32[4,2]{0,1:T(2,128)}, u32[]{:S(2)}) copy-start(s32[4,2]{0,1:T(2,128)} %param.11) | copy-start | bytes 100
  128.9 3.6 %collective-permute-start.24 = (f32[16,32,256]{2,1,0:T(8,128)S(1)}, f32[16,32,256]{2,1,0:T(8,128)S(1)}, u32[]{:S(2)}, u32[]{:S(2)}) collective-permute-start(f32[16,32,256]{2,1,0:T(8,128)S(1)} %all_to_all.15.refs_0_), channel_id=1, source_target_pairs={{0,8},{8,0},{16,24},{24,16},{32,40},{40,32},{48,56},{56,48},{64,72... | collective-permute-start | bytes 1572872 | tf_op jit(solution)/shard_map/ppermute | solution.py:267
  147.3 15.2 %all-to-all-start.2 = ((bf16[8,32,256]{2,1,0:T(8,128)(2,1)}), bf16[8,32,256]{2,1,0:T(8,128)(2,1)S(1)}, u32[]{:S(2)}, u32[]{:S(2)}) async-start(bf16[8,32,256]{2,1,0:T(8,128)(2,1)} %chain.1), calls=%async_computation.3 | async-start | bytes 262144 | tf_op jit(solution)/shard_map/all_to_all | solution.py:397
  154.2 1.6 copy-start
  155.8 6.7 %copy-start.8 = (bf16[4,128,128]{2,1,0:T(8,128)(2,1)S(1)}, bf16[4,128,128]{2,1,0:T(8,128)(2,1)}, u32[]{:S(2)}) copy-start(bf16[4,128,128]{2,1,0:T(8,128)(2,1)} %inv.5) | copy-start | bytes 393220
  155.8 6.7 %copy-start.11 = (f32[256,256]{1,0:T(8,128)S(1)}, f32[256,256]{1,0:T(8,128)}, u32[]{:S(2)}) copy-start(f32[256,256]{1,0:T(8,128)} %get-tuple-element.30.kept) | copy-start | bytes 786436
Sparse Core Ops, SparseCore 0:
  11.4 39.8 reduce-scatter.1
  115.9 34.4 all-gather.2

commit v5 on v4

--- a/solution.py
+++ b/solution.py
@@ -136,43 +136,48 @@
         corner[at, :] = block[rows : rows + step, b:].astype(F32) + block[
             rows + step :, :b
         ].astype(F32)
-    applied = mm(inv[...], whole[...], NN)
-    app = applied.astype(BF)
     first_hi, first_lo = halves(mm(tail[...], link[...], NN))
     maps[:b, :] = first_hi
     maps[b : 2 * b, :] = first_lo
     inner = mm2(corner[...], link[...], NN)
     maps[2 * b :, :] = mm2(inner, link[...], TN).astype(BF)
+    applied = mm(inv[...], whole[...], NN)
+    app = applied.astype(BF)
     for g in range(n):
         block = mm(inv[:, g * rows : (g + 1) * rows], app, TN).astype(BF)
         terms[owners[0, g], :rows, :] = block
     state_hi, state_lo = halves(jnp.where(owners[0, n - 1] == me, applied[rows - b :, :], 0.0).T)
-    head_hi, head_lo = halves(mm(app, inv[:, :b], TN))
-    cols = (terms.shape[1] - rows) // 2
+    head = mm2(mm(app, inv[:, :b], TN), link[...], NN).astype(BF)
+    half = terms.shape[1] - rows
+    half = half // 3
     for j in range(n):
-        at = slice(j * cols, (j + 1) * cols)
-        terms[j, rows : rows + cols, :b] = state_hi[at]
-        terms[j, rows : rows + cols, b:] = head_hi[at]
-        terms[j, rows + cols :, :b] = state_lo[at]
-        terms[j, rows + cols :, b:] = head_lo[at]
-
-
-def sum_ends_kernel(parts, link, *refs):
-    spread = refs[-1]
-    b = link.shape[0]
-    cols = spread.shape[1]
-    rows = parts.shape[1] - 2 * cols
+        at = 2 * half * j
+        terms[j, rows : rows + 2 * half, :b] = state_hi[at : at + 2 * half]
+        terms[j, rows : rows + 2 * half, b:] = head[at : at + 2 * half]
+        terms[j, rows + 2 * half :, :b] = state_lo[at : at + half]
+        terms[j, rows + 2 * half :, b:] = state_lo[at + half : at + 2 * half]
+
+
+def sum_ends_kernel(parts, spread):
+    b = spread.shape[2] // 2
+    rows = parts.shape[1] - spread.shape[1]
+    half = spread.shape[1] // 3
+    cols = 2 * half
     total = parts[0, rows:, :].astype(F32)
     for j in range(1, parts.shape[0]):
         total += parts[j, rows:, :].astype(F32)
-    ends = total[:cols] + total[cols:]
-    head = mm2(ends[:, b:], link[...], NN)
+    low = jnp.concatenate([total[cols:, :b], total[cols:, b:]], axis=0)
+    state_hi, state_lo = halves(total[:cols, :b] + low)
+    head = total[:cols, b:].astype(BF)
     for j in range(spread.shape[0]):
-        spread[j, :, :b] = ends[:, :b]
-        spread[j, :, b:] = head
-
-
-def sum_terms_kernel(parts, shared, _, kept, packed):
+        spread[j, :cols, :b] = state_hi
+        spread[j, :cols, b:] = head
+        spread[j, cols:, :b] = state_lo[:half]
+        spread[j, cols:, b:] = state_lo[half:]
+
+
+def sum_terms_kernel(parts, shared, *refs):
+    kept, packed = refs[-2:]
     rows = kept.shape[0]
     total = parts[0, :rows, :].astype(F32)
     for j in range(1, parts.shape[0]):
@@ -188,9 +193,14 @@
         out[j] = refs[j][...]
 
 
-def times_map(value, hi, lo, dims):
+def times_map(value, both, dims):
+    b = both.shape[1]
     vh, vl = halves(value)
-    return mm(vh, hi, dims) + (mm(vl, hi, dims) + mm(vh, lo, dims))
+    if dims is NN:
+        wide = mm(vh, jnp.concatenate([both[:b], both[b:]], axis=1), NN)
+    else:
+        wide = mm(vh, both, NT)
+    return (wide[:, :b] + wide[:, b:]) + mm(vl, both[:b], dims)
 
 
 def chain_kernel(*refs):
@@ -209,24 +219,30 @@
                 at = lax.rem(y + j, 4) * 4 + lax.rem(x + k, 4)
                 where = maps.at[side, at]
                 pltpu.make_async_copy(map_parts[j].at[k], where, sems.at[side, at]).start()
-        ag[side] = ag_part[...]
+        cols = out.shape[1]
+        for q in range(ag_part.shape[0]):
+            low = ag_part[q, cols:, :].astype(F32)
+            low = jnp.concatenate([low[:, :b], low[:, b:]], axis=0)
+            ag[side, q, :, :b] = ag_part[q, :cols, :b].astype(F32) + low
+            ag[side, q, :, b:] = ag_part[q, :cols, b:].astype(F32)
     state = jnp.zeros((out.shape[1], b), F32)
     for w in range(length):
         states[w] = state
         at = (w % 2, w // 2)
         pltpu.make_async_copy(mapss[0][0].at[0], maps.at[at], sems.at[at]).wait()
         if w + 1 < length:
-            moved = times_map(state, maps[(*at, slice(0, b))], maps[(*at, slice(b, 2 * b))], NT)
+            moved = times_map(state, maps[(*at, slice(0, 2 * b))], NT)
             state = ag[(*at, slice(None), slice(0, b))] - moved
     back = jnp.zeros_like(state)
     for w in range(length - 1, -1, -1):
         incoming[w] = back
         if w > 0:
             at = (w % 2, w // 2)
-            vh, vl = halves(states[w])
+            pair = jnp.concatenate(halves(states[w]), axis=1)
             corner = maps[(*at, slice(2 * b, 3 * b))]
-            local = ag[(*at, slice(None), slice(b, 2 * b))] - (mm(vh, corner, NN) + mm(vl, corner, NN))
-            moved = times_map(back, maps[(*at, slice(0, b))], maps[(*at, slice(b, 2 * b))], NN)
+            corner = mm(pair, jnp.concatenate([corner, corner], axis=0), NN)
+            local = ag[(*at, slice(None), slice(b, 2 * b))] - corner
+            moved = times_map(back, maps[(*at, slice(0, 2 * b))], NN)
             back = local - moved
     mine = mm2(states[wide], link[...], NT).astype(BF)
     last = incoming[wide].astype(BF)
@@ -343,7 +359,7 @@
     terms, maps = call(
         middle_kernel,
         "middle",
-        (held((n, rows + 2 * cols, sketch), BF), held((3 * b, b), BF)),
+        (held((n, rows + cols + cols // 2, sketch), BF), held((3 * b, b), BF)),
         [SMEM] + [VMEM] * (2 + n) + [ANY],
         [pltpu.VMEM((all_rows, sketch), BF), pltpu.VMEM((b, b), F32), pltpu.VMEM((b, b), BF)],
         flops=4 * rows * all_rows * sketch,
@@ -361,17 +377,17 @@
     ag = call(
         sum_ends_kernel,
         "sum_ends",
-        held((chips, cols, 2 * b), F32),
-        [VMEM] * 6,
+        held((chips, cols + cols // 2, 2 * b), BF),
+        [VMEM],
         moved=1 << 19,
-    )(terms, sep_link, *[near(part) for part in maps_other])
+    )(terms)
     kept, packed = call(
         sum_terms_kernel,
         "sum_terms",
         (pltpu.HBM((rows, sketch), F32), pltpu.HBM((2 * rows, sketch), BF)),
-        [VMEM] * 2 + [ANY],
+        [VMEM] * 7,
         moved=2 << 20,
-    )(terms, shared, near(ag))
+    )(terms, shared, near(ag), *[near(part) for part in maps_other[:3]], near(maps[3]))
     gathered = lax.all_gather(packed, "narrow", axis=0, tiled=False)
 
     same_core = [[2 * q + c for q in range(chips)] for c in range(2)]
@@ -382,7 +398,7 @@
         chain_kernel,
         "chain",
         held((n, cols, 2 * b), BF),
-        [VMEM] * 2 + [ANY] * 8 + [VMEM],
+        [VMEM] * 2 + [ANY] * 7 + [VMEM] * 2,
         [
             pltpu.VMEM((2, chips, cols, 2 * b), F32),
             pltpu.VMEM((2, chips, 3 * b, b), BF),
@@ -393,7 +409,7 @@
         flops=2 * 9 * chain_len * cols * b * b,
         moved=8 << 20,
         limit=56,
-    )(ag, ag_other, *maps, *maps_other, sep_link)
+    )(ag, ag_other, *maps, *maps_other[:3], near(maps_other[3]), sep_link)
     z = lax.all_to_all(z, "narrow", 0, 0, tiled=True).reshape(sketch, 2 * b)
 
     base, fix, own = call(

time: 171 us -> 165 us (0.965)
  blocking collectives: 13.1 us -> 0 us
  starting transfers between devices: 66.1 us -> 73.1 us
  waiting for transfers between devices: 46.6 us -> 50.2 us
  local copies, waits for them, and re-layouts: 4.14 us -> 1.64 us
    all_to_all x1 -> x0, blocking collectives: 13.1 us -> none  [per_device(): lax.all_to_all(ag, 'wide', 0, 0, tiled=True, axis_index_groups=same_core)]
    all_to_all x0 -> x1, waiting for transfers between devices: none -> 6.68 us  [per_device(): lax.all_to_all(ag, 'wide', 0, 0, tiled=True, axis_index_groups=same_core)]
    all_to_all x0 -> x1, starting transfers between devices: none -> 5.92 us  [per_device(): lax.all_to_all(ag, 'wide', 0, 0, tiled=True, axis_index_groups=same_core)]
    pallas_call x1, Pallas kernels: 14.7 us -> 12.1 us  [per_device(): call(chain_kernel, 'chain', held((n, cols, 2 * b), BF), [VMEM] * 2 + [ANY...]
    unnamed x36 -> x26, local copies, waits for them, and re-layouts: 4.14 us -> 1.64 us
    ppermute x6, waiting for transfers between devices: 3.98 us -> 1.65 us  [turned_wide(): return lax.ppermute(value, 'wide', [(source(i), i) for i in range(32)])]
  transfers between devices with their start and end apart: 29 -> 30, of which waited for: 13 -> 15; matrix products, arithmetic and copies ran while one was open for 0% -> 0% of each run, Pallas kernels for 9% -> 8%
where the time goes in v5:
time: 165 us
  starting transfers between devices  73.1 us (44%)
  waiting for transfers between devices  50.2 us (30%)
  Pallas kernels  25.5 us (15%)
  between operations  14.3 us (9%)
    ppermute x14, waiting for transfers between devices, turned(): return lax.ppermute(value, 'narrow', [(i, (i + by) % n) for i in range(n)])  34.1 us
    ppermute x5, starting transfers between devices, swap(): return lax.ppermute(value, axis, [(i, i ^ by) for i in range(n)])  25.7 us
    ppermute x14, starting transfers between devices, turned(): return lax.ppermute(value, 'narrow', [(i, (i + by) % n) for i in range(n)])  20.4 us
    pallas_call x1, Pallas kernels, per_device(): call(chain_kernel, 'chain', held((n, cols, 2 * b), BF), [VMEM] * 2 + [ANY...  12.1 us
    ppermute x6, starting transfers between devices, turned_wide(): return lax.ppermute(value, 'wide', [(source(i), i) for i in range(32)])  9.45 us
    all_to_all x1, starting transfers between devices, per_device(): z = lax.all_to_all(z, 'narrow', 0, 0, tiled=True).reshape(sketch, 2 * b)  6.88 us
    all_to_all x1, waiting for transfers between devices, per_device(): lax.all_to_all(ag, 'wide', 0, 0, tiled=True, axis_index_groups=same_core)  6.68 us
    all_to_all x1, starting transfers between devices, per_device(): lax.all_to_all(ag, 'wide', 0, 0, tiled=True, axis_index_groups=same_core)  5.92 us
  transfers between devices with their start and end apart: 30, of which 15 were waited for; matrix products, arithmetic and copies ran while one was open for 0% of the time, Pallas kernels for 8%

profile of v5, /device:TPU:1, one launch (start us, length us, event | category | flops | bytes accessed | tf_op | source)
XLA Modules:
  0.0 164.9 jit_solution(322044868772069606)
XLA Ops:
  7.2 4.1 %leaf_forward.1 = (bf16[512,256]{1,0:T(8,128)(2,1)}, bf16[2048,256]{1,0:T(8,128)(2,1)}, bf16[288,256]{1,0:T(8,128)(2,1)S(1)}, bf16[288,256]{1,0:T(8,128)(2,1)S(1...) custom-call(s32[2,4]{1,0:T(2,128)} %bitcast.5, ...), custom_call_target="tpu_custom_call" | custom-call | flops 100663296 | bytes 4194304 | tf_op jit(solution)/shard_map/leaf_forward/pallas_call | solution.py:341
  11.3 2.5 %collective-permute-start = (bf16[288,256]{1,0:T(8,128)(2,1)S(1)}, bf16[288,256]{1,0:T(8,128)(2,1)S(1)}, u32[]{:S(2)}, u32[]{:S(2)}) collective-permute-start(bf16[288,256]{1,0:T(8,128)(2,1)S(1)} %get-tuple-element.19), channel_id=1, source_target_pairs={{0,1},{1,2},{2,3},{3,4},{4,5},{5,6},{6,7},{7,0},{8,9},{9,10},{10,1... | collective-permute-start | bytes 442376 | tf_op jit(solution)/shard_map/ppermute | solution.py:288
  13.8 4.0 %collective-permute-start.4 = (bf16[288,256]{1,0:T(8,128)(2,1)S(1)}, bf16[288,256]{1,0:T(8,128)(2,1)S(1)}, u32[]{:S(2)}, u32[]{:S(2)}) collective-permute-start(bf16[288,256]{1,0:T(8,128)(2,1)S(1)} %get-tuple-element.23), channel_id=1, source_target_pairs={{0,7},{1,0},{2,1},{3,2},{4,3},{5,4},{6,5},{7,6},{8,15},{9,8},{10,9... | collective-permute-start | bytes 442376 | tf_op jit(solution)/shard_map/ppermute | solution.py:288
  17.9 3.5 %collective-permute-done = bf16[288,256]{1,0:T(8,128)(2,1)S(1)} collective-permute-done((bf16[288,256]{1,0:T(8,128)(2,1)S(1)}, bf16[288,256]{1,0:T(8,128)(2,1)S(1)}, u32[]{:S(2)}, u32[]{:S(2)}) %collective-permute-start) | collective-permute-done | bytes 147488 | tf_op jit(solution)/shard_map/ppermute | solution.py:288
  21.4 0.1 collective-permute-start.1
  21.5 2.7 %collective-permute-start.5 = (bf16[288,256]{1,0:T(8,128)(2,1)S(1)}, bf16[288,256]{1,0:T(8,128)(2,1)S(1)}, u32[]{:S(2)}, u32[]{:S(2)}) collective-permute-start(bf16[288,256]{1,0:T(8,128)(2,1)S(1)} %add_convert_fusion.1), channel_id=1, source_target_pairs={{0,7},{1,0},{2,1},{3,2},{4,3},{5,4},{6,5},{7,6},{8,15},{9,8},{10,9... | collective-permute-start | bytes 442376 | tf_op jit(solution)/shard_map/ppermute | solution.py:288
  24.3 2.4 %collective-permute-done.1 = bf16[288,256]{1,0:T(8,128)(2,1)S(1)} collective-permute-done((bf16[288,256]{1,0:T(8,128)(2,1)S(1)}, bf16[288,256]{1,0:T(8,128)(2,1)S(1)}, u32[]{:S(2)}, u32[]{:S(2)}) %collective-permute-start.1) | collective-permute-done | bytes 147488 | tf_op jit(solution)/shard_map/ppermute | solution.py:288
  26.7 0.1 collective-permute-start.2
  26.9 2.7 %collective-permute-start.6 = (bf16[288,256]{1,0:T(8,128)(2,1)S(1)}, bf16[288,256]{1,0:T(8,128)(2,1)S(1)}, u32[]{:S(2)}, u32[]{:S(2)}) collective-permute-start(bf16[288,256]{1,0:T(8,128)(2,1)S(1)} %add_convert_fusion), channel_id=1, source_target_pairs={{0,7},{1,0},{2,1},{3,2},{4,3},{5,4},{6,5},{7,6},{8,15},{9,8},{10,9... | collective-permute-start | bytes 442376 | tf_op jit(solution)/shard_map/ppermute | solution.py:288
  29.6 4.2 %collective-permute-done.2 = bf16[288,256]{1,0:T(8,128)(2,1)S(1)} collective-permute-done((bf16[288,256]{1,0:T(8,128)(2,1)S(1)}, bf16[288,256]{1,0:T(8,128)(2,1)S(1)}, u32[]{:S(2)}, u32[]{:S(2)}) %collective-permute-start.2) | collective-permute-done | bytes 147488 | tf_op jit(solution)/shard_map/ppermute | solution.py:288
  33.8 0.1 collective-permute-start.3
  33.9 6.6 %collective-permute-done.3.right = bf16[288,256]{1,0:T(8,128)(2,1)S(1)} collective-permute-done((bf16[288,256]{1,0:T(8,128)(2,1)S(1)}, bf16[288,256]{1,0:T(8,128)(2,1)S(1)}, u32[]{:S(2)}, u32[]{:S(2)}) %collective-permute-start.3) | collective-permute-done | bytes 147488 | tf_op jit(solution)/shard_map/ppermute | solution.py:288
  40.5 0.1 collective-permute-start.10
  40.6 2.7 %collective-permute-start.7 = (bf16[288,256]{1,0:T(8,128)(2,1)S(1)}, bf16[288,256]{1,0:T(8,128)(2,1)S(1)}, u32[]{:S(2)}, u32[]{:S(2)}) collective-permute-start(bf16[288,256]{1,0:T(8,128)(2,1)S(1)} %sum_own.1.refs_0_), channel_id=1, source_target_pairs={{0,7},{1,0},{2,1},{3,2},{4,3},{5,4},{6,5},{7,6},{8,15},{9,8},{10,9... | collective-permute-start | bytes 442376 | tf_op jit(solution)/shard_map/ppermute | solution.py:288
  43.3 4.4 %collective-permute-done.10.refs_7_ = bf16[288,256]{1,0:T(8,128)(2,1)S(1)} collective-permute-done((bf16[288,256]{1,0:T(8,128)(2,1)S(1)}, bf16[288,256]{1,0:T(8,128)(2,1)S(1)}, u32[]{:S(2)}, u32[]{:S(2)}) %collective-permute-start.10) | collective-permute-done | bytes 147488 | tf_op jit(solution)/shard_map/ppermute | solution.py:288
  47.7 2.7 %collective-permute-start.8 = (bf16[288,256]{1,0:T(8,128)(2,1)S(1)}, bf16[288,256]{1,0:T(8,128)(2,1)S(1)}, u32[]{:S(2)}, u32[]{:S(2)}) collective-permute-start(bf16[288,256]{1,0:T(8,128)(2,1)S(1)} %collective-permute-done.7.refs_1_), channel_id=1, source_target_pairs={{0,7},{1,0},{2,1},{3,2},{4,3},{5,4},{6,5},{7,6},{8,15},{9,8},{10,9... | collective-permute-start | bytes 442376 | tf_op jit(solution)/shard_map/ppermute | solution.py:288
  50.4 3.3 %collective-permute-done.11.refs_6_ = bf16[288,256]{1,0:T(8,128)(2,1)S(1)} collective-permute-done((bf16[288,256]{1,0:T(8,128)(2,1)S(1)}, bf16[288,256]{1,0:T(8,128)(2,1)S(1)}, u32[]{:S(2)}, u32[]{:S(2)}) %collective-permute-start.11) | collective-permute-done | bytes 147488 | tf_op jit(solution)/shard_map/ppermute | solution.py:288
  53.7 2.7 %collective-permute-start.9 = (bf16[288,256]{1,0:T(8,128)(2,1)S(1)}, bf16[288,256]{1,0:T(8,128)(2,1)S(1)}, u32[]{:S(2)}, u32[]{:S(2)}) collective-permute-start(bf16[288,256]{1,0:T(8,128)(2,1)S(1)} %collective-permute-done.8.refs_2_), channel_id=1, source_target_pairs={{0,7},{1,0},{2,1},{3,2},{4,3},{5,4},{6,5},{7,6},{8,15},{9,8},{10,9... | collective-permute-start | bytes 442376 | tf_op jit(solution)/shard_map/ppermute | solution.py:288
  56.4 2.9 %collective-permute-done.12.refs_5_ = bf16[288,256]{1,0:T(8,128)(2,1)S(1)} collective-permute-done((bf16[288,256]{1,0:T(8,128)(2,1)S(1)}, bf16[288,256]{1,0:T(8,128)(2,1)S(1)}, u32[]{:S(2)}, u32[]{:S(2)}) %collective-permute-start.12) | collective-permute-done | bytes 147488 | tf_op jit(solution)/shard_map/ppermute | solution.py:288
  59.2 6.9 %collective-permute-done.13.refs_4_ = bf16[288,256]{1,0:T(8,128)(2,1)S(1)} collective-permute-done((bf16[288,256]{1,0:T(8,128)(2,1)S(1)}, bf16[288,256]{1,0:T(8,128)(2,1)S(1)}, u32[]{:S(2)}, u32[]{:S(2)}) %collective-permute-start.13) | collective-permute-done | bytes 147488 | tf_op jit(solution)/shard_map/ppermute | solution.py:288
  66.1 3.9 %middle.1 = (bf16[8,304,256]{2,1,0:T(8,128)(2,1)}, bf16[384,128]{1,0:T(8,128)(2,1)S(1)}) custom-call(s32[1,8]{1,0:T(1,128)} %owners.5, bf16[256,2048]{1,0:T(8,128)(2,1)} %inv.4, bf16[288,256]{1,0:T(8,128)(2,1)S(1)} %sum_own.1.refs_0_, bf16[288,256]{1,0:T(8,128)(2,1)S(1)} %collective-permute-done.7.refs_1_, ...), custom_call_target="tpu_custom_call" | custom-call | flops 536870912 | bytes 4194304 | tf_op jit(solution)/shard_map/middle/pallas_call | solution.py:359
  70.0 4.7 %all-to-all-start = ((bf16[8,304,256]{2,1,0:T(8,128)(2,1)}), bf16[8,304,256]{2,1,0:T(8,128)(2,1)S(1)}, u32[]{:S(2)}, u32[]{:S(2)}) async-start(bf16[8,304,256]{2,1,0:T(8,128)(2,1)} %get-tuple-element.28), calls=%async_computation.1 | async-start | bytes 2490368 | tf_op jit(solution)/shard_map/all_to_all | solution.py:375
  74.7 0.7 collective-permute-start.16
  75.5 2.3 %collective-permute-start.15 = (bf16[384,128]{1,0:T(8,128)(2,1)S(1)}, bf16[384,128]{1,0:T(8,128)(2,1)S(1)}, u32[]{:S(2)}, u32[]{:S(2)}) collective-permute-start(bf16[384,128]{1,0:T(8,128)(2,1)S(1)} %get-tuple-element.29.refs_0_), channel_id=1, source_target_pairs={{32,0},{40,8},{48,16},{56,24},{0,32},{8,40},{16,48},{24,56},{96,64... | collective-permute-start | bytes 294920 | tf_op jit(solution)/shard_map/ppermute | solution.py:321
  77.8 2.0 %collective-permute-start.14 = (bf16[384,128]{1,0:T(8,128)(2,1)S(1)}, bf16[384,128]{1,0:T(8,128)(2,1)S(1)}, u32[]{:S(2)}, u32[]{:S(2)}) collective-permute-start(bf16[384,128]{1,0:T(8,128)(2,1)S(1)} %get-tuple-element.29.refs_0_), channel_id=1, source_target_pairs={{16,0},{24,8},{32,16},{40,24},{48,32},{56,40},{0,48},{8,56},{80,64... | collective-permute-start | bytes 294920 | tf_op jit(solution)/shard_map/ppermute | solution.py:321
  79.7 1.0 collective-permute-done.15.refs_2_
  80.7 0.7 collective-permute-done.14.refs_1_
  81.4 3.0 %collective-permute-start.20 = (bf16[4,384,128]{2,1,0:T(8,128)(2,1)S(1)}, bf16[4,384,128]{2,1,0:T(8,128)(2,1)}, u32[]{:S(2)}, u32[]{:S(2)}) collective-permute-start(bf16[4,384,128]{2,1,0:T(8,128)(2,1)S(1)} %stack_maps.1.refs_2_), channel_id=1, source_target_pairs={{128,0},{136,8},{144,16},{152,24},{160,32},{168,40},{176,48},{184,... | collective-permute-start | bytes 1179656 | tf_op jit(solution)/shard_map/ppermute | solution.py:321
  84.4 1.2 collective-permute-start.18
  85.6 0.3 collective-permute-start.22
  85.9 12.7 %collective-permute-start.17 = (bf16[4,384,128]{2,1,0:T(8,128)(2,1)S(1)}, bf16[4,384,128]{2,1,0:T(8,128)(2,1)S(1)}, u32[]{:S(2)}, u32[]{:S(2)}) collective-permute-start(bf16[4,384,128]{2,1,0:T(8,128)(2,1)S(1)} %stack_maps.1.refs_2_), channel_id=1, source_target_pairs={{0,8},{8,0},{16,24},{24,16},{32,40},{40,32},{48,56},{56,48},{64,72... | collective-permute-start | bytes 1179656 | tf_op jit(solution)/shard_map/ppermute | solution.py:283
  98.5 4.1 %collective-permute-start.21 = (bf16[4,384,128]{2,1,0:T(8,128)(2,1)}, bf16[4,384,128]{2,1,0:T(8,128)(2,1)S(1)}, u32[]{:S(2)}, u32[]{:S(2)}) collective-permute-start(bf16[4,384,128]{2,1,0:T(8,128)(2,1)} %collective-permute-done.20.refs_4_), channel_id=1, source_target_pairs={{0,8},{8,0},{16,24},{24,16},{32,40},{40,32},{48,56},{56,48},{64,72... | collective-permute-start | bytes 1179656 | tf_op jit(solution)/shard_map/ppermute | solution.py:283
  102.6 4.6 %collective-permute-start.19 = (bf16[4,384,128]{2,1,0:T(8,128)(2,1)}, bf16[4,384,128]{2,1,0:T(8,128)(2,1)S(1)}, u32[]{:S(2)}, u32[]{:S(2)}) collective-permute-start(bf16[4,384,128]{2,1,0:T(8,128)(2,1)} %collective-permute-done.18.refs_3_), channel_id=1, source_target_pairs={{0,8},{8,0},{16,24},{24,16},{32,40},{40,32},{48,56},{56,48},{64,72... | collective-permute-start | bytes 1179656 | tf_op jit(solution)/shard_map/ppermute | solution.py:283
  107.3 0.8 sum_ends.1.refs_0_
  108.1 0.7 collective-permute-done.19.refs_2_.refs_7_
  108.8 2.1 %sum_terms.1 = (f32[256,256]{1,0:T(8,128)}, bf16[512,256]{1,0:T(8,128)(2,1)}) custom-call(bf16[8,304,256]{2,1,0:T(8,128)(2,1)S(1)} %all-to-all-done.parts, bf16[256,256]{1,0:T(8,128)(2,1)S(1)} %copy-done.8, bf16[16,48,256]{2,1,0:T(8,128)(2,1)} %sum_ends.1.refs_0_, bf16[4,384,128]{2,1,0:T(8,128)(2,1)S(1)} %collective-permute-done.17.refs_1_.refs_6_, ...), custom_call_target="tpu_custom_call" | custom-call | bytes 2097152 | tf_op jit(solution)/shard_map/sum_terms/pallas_call | solution.py:384
  110.9 5.9 %all-to-all-start.1 = ((bf16[16,48,256]{2,1,0:T(8,128)(2,1)}), bf16[16,48,256]{2,1,0:T(8,128)(2,1)S(1)}, u32[]{:S(2)}, u32[]{:S(2)}) async-start(bf16[16,48,256]{2,1,0:T(8,128)(2,1)} %sum_ends.1.refs_0_), calls=%async_computation.2 | async-start | bytes 786432 | tf_op jit(solution)/shard_map/all_to_all | solution.py:394
  116.9 1.7 %collective-permute-start.24 = (bf16[4,384,128]{2,1,0:T(8,128)(2,1)S(1)}, bf16[4,384,128]{2,1,0:T(8,128)(2,1)S(1)}, u32[]{:S(2)}, u32[]{:S(2)}) collective-permute-start(bf16[4,384,128]{2,1,0:T(8,128)(2,1)S(1)} %collective-permute-done.22.refs_4_.refs_5_), channel_id=1, source_target_pairs={{0,8},{8,0},{16,24},{24,16},{32,40},{40,32},{48,56},{56,48},{64,72... | collective-permute-start | bytes 1179656 | tf_op jit(solution)/shard_map/ppermute | solution.py:283
  118.6 6.7 %all-to-all-done.1.refs_0_ = bf16[16,48,256]{2,1,0:T(8,128)(2,1)S(1)} async-done(((bf16[16,48,256]{2,1,0:T(8,128)(2,1)}), bf16[16,48,256]{2,1,0:T(8,128)(2,1)S(1)}, u32[]{:S(2)}, u32[]{:S(2)}) %all-to-all-start.1) | async-done | bytes 393248 | tf_op jit(solution)/shard_map/all_to_all | solution.py:394
  125.3 2.6 %collective-permute-start.23 = (bf16[16,48,256]{2,1,0:T(8,128)(2,1)S(1)}, bf16[16,48,256]{2,1,0:T(8,128)(2,1)S(1)}, u32[]{:S(2)}, u32[]{:S(2)}) collective-permute-start(bf16[16,48,256]{2,1,0:T(8,128)(2,1)S(1)} %all-to-all-done.1.refs_0_), channel_id=1, source_target_pairs={{0,8},{8,0},{16,24},{24,16},{32,40},{40,32},{48,56},{56,48},{64,72... | collective-permute-start | bytes 1179656 | tf_op jit(solution)/shard_map/ppermute | solution.py:283
  127.9 1.3 collective-permute-done.23.refs_1_
  129.3 12.1 %chain.1 = bf16[8,32,256]{2,1,0:T(8,128)(2,1)} custom-call(bf16[16,48,256]{2,1,0:T(8,128)(2,1)S(1)} %all-to-all-done.1.refs_0_, bf16[16,48,256]{2,1,0:T(8,128)(2,1)S(1)} %collective-permute-done.23.refs_1_, bf16[4,384,128]{2,1,0:T(8,128)(2,1)} %copy-done.5, bf16[4,384,128]{2,1,0:T(8,128)(2,1)} %collective-permute-done.18.refs_3_, ...), custom_call_target="tpu_custom_call" | custom-call | flops 301989888 | bytes 8388608 | tf_op jit(solution)/shard_map/chain/pallas_call | solution.py:397
  141.4 6.9 %all-to-all-start.2 = ((bf16[8,32,256]{2,1,0:T(8,128)(2,1)}), bf16[8,32,256]{2,1,0:T(8,128)(2,1)S(1)}, u32[]{:S(2)}, u32[]{:S(2)}) async-start(bf16[8,32,256]{2,1,0:T(8,128)(2,1)} %chain.1), calls=%async_computation.3 | async-start | bytes 262144 | tf_op jit(solution)/shard_map/all_to_all | solution.py:413
  148.2 0.9 all-gather.3.cloned.1.call-done
  149.2 1.6 copy-done
  150.8 1.0 before.1
  151.8 4.7 %all-to-all-done.2 = bf16[8,32,256]{2,1,0:T(8,128)(2,1)S(1)} async-done(((bf16[8,32,256]{2,1,0:T(8,128)(2,1)}), bf16[8,32,256]{2,1,0:T(8,128)(2,1)S(1)}, u32[]{:S(2)}, u32[]{:S(2)}) %all-to-all-start.2) | async-done | bytes 131104 | tf_op jit(solution)/shard_map/all_to_all | solution.py:413
  156.5 1.5 final.1
  (54 shorter events, 0.5 us)
Async XLA Ops:
  7.2 58.9 %reduce-scatter.2.cloned.1.call-start = ((), (), s32[]{:S(2)}) async-start(), calls=%async_computation.4 | async-start | bytes 1179648 | tf_op jit(solution)/shard_map/reduce_scatter | solution.py:358
  11.3 10.1 %collective-permute-start = (bf16[288,256]{1,0:T(8,128)(2,1)S(1)}, bf16[288,256]{1,0:T(8,128)(2,1)S(1)}, u32[]{:S(2)}, u32[]{:S(2)}) collective-permute-start(bf16[288,256]{1,0:T(8,128)(2,1)S(1)} %get-tuple-element.19), channel_id=1, source_target_pairs={{0,1},{1,2},{2,3},{3,4},{4,5},{5,6},{6,7},{7,0},{8,9},{9,10},{10,1... | collective-permute-start | bytes 442376 | tf_op jit(solution)/shard_map/ppermute | solution.py:288
  13.8 7.6 %collective-permute-start.4 = (bf16[288,256]{1,0:T(8,128)(2,1)S(1)}, bf16[288,256]{1,0:T(8,128)(2,1)S(1)}, u32[]{:S(2)}, u32[]{:S(2)}) collective-permute-start(bf16[288,256]{1,0:T(8,128)(2,1)S(1)} %get-tuple-element.23), channel_id=1, source_target_pairs={{0,7},{1,0},{2,1},{3,2},{4,3},{5,4},{6,5},{7,6},{8,15},{9,8},{10,9... | collective-permute-start | bytes 442376 | tf_op jit(solution)/shard_map/ppermute | solution.py:288
  21.4 5.3 %collective-permute-start.1 = (bf16[288,256]{1,0:T(8,128)(2,1)S(1)}, bf16[288,256]{1,0:T(8,128)(2,1)S(1)}, u32[]{:S(2)}, u32[]{:S(2)}) collective-permute-start(bf16[288,256]{1,0:T(8,128)(2,1)S(1)} %add_convert_fusion.4), channel_id=1, source_target_pairs={{0,1},{1,2},{2,3},{3,4},{4,5},{5,6},{6,7},{7,0},{8,9},{9,10},{10,1... | collective-permute-start | bytes 442376 | tf_op jit(solution)/shard_map/ppermute | solution.py:288
  21.5 5.3 %collective-permute-start.5 = (bf16[288,256]{1,0:T(8,128)(2,1)S(1)}, bf16[288,256]{1,0:T(8,128)(2,1)S(1)}, u32[]{:S(2)}, u32[]{:S(2)}) collective-permute-start(bf16[288,256]{1,0:T(8,128)(2,1)S(1)} %add_convert_fusion.1), channel_id=1, source_target_pairs={{0,7},{1,0},{2,1},{3,2},{4,3},{5,4},{6,5},{7,6},{8,15},{9,8},{10,9... | collective-permute-start | bytes 442376 | tf_op jit(solution)/shard_map/ppermute | solution.py:288
  26.7 7.0 %collective-permute-start.2 = (bf16[288,256]{1,0:T(8,128)(2,1)S(1)}, bf16[288,256]{1,0:T(8,128)(2,1)S(1)}, u32[]{:S(2)}, u32[]{:S(2)}) collective-permute-start(bf16[288,256]{1,0:T(8,128)(2,1)S(1)} %add_convert_fusion.3), channel_id=1, source_target_pairs={{0,1},{1,2},{2,3},{3,4},{4,5},{5,6},{6,7},{7,0},{8,9},{9,10},{10,1... | collective-permute-start | bytes 442376 | tf_op jit(solution)/shard_map/ppermute | solution.py:288
  26.9 7.0 %collective-permute-start.6 = (bf16[288,256]{1,0:T(8,128)(2,1)S(1)}, bf16[288,256]{1,0:T(8,128)(2,1)S(1)}, u32[]{:S(2)}, u32[]{:S(2)}) collective-permute-start(bf16[288,256]{1,0:T(8,128)(2,1)S(1)} %add_convert_fusion), channel_id=1, source_target_pairs={{0,7},{1,0},{2,1},{3,2},{4,3},{5,4},{6,5},{7,6},{8,15},{9,8},{10,9... | collective-permute-start | bytes 442376 | tf_op jit(solution)/shard_map/ppermute | solution.py:288
  33.8 6.7 %collective-permute-start.3 = (bf16[288,256]{1,0:T(8,128)(2,1)S(1)}, bf16[288,256]{1,0:T(8,128)(2,1)S(1)}, u32[]{:S(2)}, u32[]{:S(2)}) collective-permute-start(bf16[288,256]{1,0:T(8,128)(2,1)S(1)} %add_convert_fusion.2), channel_id=1, source_target_pairs={{0,1},{1,2},{2,3},{3,4},{4,5},{5,6},{6,7},{7,0},{8,9},{9,10},{10,1... | collective-permute-start | bytes 442376 | tf_op jit(solution)/shard_map/ppermute | solution.py:288
  40.5 7.2 %collective-permute-start.10 = (bf16[288,256]{1,0:T(8,128)(2,1)S(1)}, bf16[288,256]{1,0:T(8,128)(2,1)S(1)}, u32[]{:S(2)}, u32[]{:S(2)}) collective-permute-start(bf16[288,256]{1,0:T(8,128)(2,1)S(1)} %sum_own.1.refs_0_), channel_id=1, source_target_pairs={{0,1},{1,2},{2,3},{3,4},{4,5},{5,6},{6,7},{7,0},{8,9},{9,10},{10,1... | collective-permute-start | bytes 442376 | tf_op jit(solution)/shard_map/ppermute | solution.py:288
  40.6 7.1 %collective-permute-start.7 = (bf16[288,256]{1,0:T(8,128)(2,1)S(1)}, bf16[288,256]{1,0:T(8,128)(2,1)S(1)}, u32[]{:S(2)}, u32[]{:S(2)}) collective-permute-start(bf16[288,256]{1,0:T(8,128)(2,1)S(1)} %sum_own.1.refs_0_), channel_id=1, source_target_pairs={{0,7},{1,0},{2,1},{3,2},{4,3},{5,4},{6,5},{7,6},{8,15},{9,8},{10,9... | collective-permute-start | bytes 442376 | tf_op jit(solution)/shard_map/ppermute | solution.py:288
  47.7 6.0 %collective-permute-start.11 = (bf16[288,256]{1,0:T(8,128)(2,1)S(1)}, bf16[288,256]{1,0:T(8,128)(2,1)S(1)}, u32[]{:S(2)}, u32[]{:S(2)}) collective-permute-start(bf16[288,256]{1,0:T(8,128)(2,1)S(1)} %collective-permute-done.10.refs_7_), channel_id=1, source_target_pairs={{0,1},{1,2},{2,3},{3,4},{4,5},{5,6},{6,7},{7,0},{8,9},{9,10},{10,1... | collective-permute-start | bytes 442376 | tf_op jit(solution)/shard_map/ppermute | solution.py:288
  47.7 6.0 %collective-permute-start.8 = (bf16[288,256]{1,0:T(8,128)(2,1)S(1)}, bf16[288,256]{1,0:T(8,128)(2,1)S(1)}, u32[]{:S(2)}, u32[]{:S(2)}) collective-permute-start(bf16[288,256]{1,0:T(8,128)(2,1)S(1)} %collective-permute-done.7.refs_1_), channel_id=1, source_target_pairs={{0,7},{1,0},{2,1},{3,2},{4,3},{5,4},{6,5},{7,6},{8,15},{9,8},{10,9... | collective-permute-start | bytes 442376 | tf_op jit(solution)/shard_map/ppermute | solution.py:288
  53.7 5.6 %collective-permute-start.12 = (bf16[288,256]{1,0:T(8,128)(2,1)S(1)}, bf16[288,256]{1,0:T(8,128)(2,1)S(1)}, u32[]{:S(2)}, u32[]{:S(2)}) collective-permute-start(bf16[288,256]{1,0:T(8,128)(2,1)S(1)} %collective-permute-done.11.refs_6_), channel_id=1, source_target_pairs={{0,1},{1,2},{2,3},{3,4},{4,5},{5,6},{6,7},{7,0},{8,9},{9,10},{10,1... | collective-permute-start | bytes 442376 | tf_op jit(solution)/shard_map/ppermute | solution.py:288
  53.7 5.6 %collective-permute-start.9 = (bf16[288,256]{1,0:T(8,128)(2,1)S(1)}, bf16[288,256]{1,0:T(8,128)(2,1)S(1)}, u32[]{:S(2)}, u32[]{:S(2)}) collective-permute-start(bf16[288,256]{1,0:T(8,128)(2,1)S(1)} %collective-permute-done.8.refs_2_), channel_id=1, source_target_pairs={{0,7},{1,0},{2,1},{3,2},{4,3},{5,4},{6,5},{7,6},{8,15},{9,8},{10,9... | collective-permute-start | bytes 442376 | tf_op jit(solution)/shard_map/ppermute | solution.py:288
  59.2 6.9 %collective-permute-start.13 = (bf16[288,256]{1,0:T(8,128)(2,1)S(1)}, bf16[288,256]{1,0:T(8,128)(2,1)S(1)}, u32[]{:S(2)}, u32[]{:S(2)}) collective-permute-start(bf16[288,256]{1,0:T(8,128)(2,1)S(1)} %collective-permute-done.12.refs_5_), channel_id=1, source_target_pairs={{0,1},{1,2},{2,3},{3,4},{4,5},{5,6},{6,7},{7,0},{8,9},{9,10},{10,1... | collective-permute-start | bytes 442376 | tf_op jit(solution)/shard_map/ppermute | solution.py:288
  70.0 37.3 %all-to-all-start = ((bf16[8,304,256]{2,1,0:T(8,128)(2,1)}), bf16[8,304,256]{2,1,0:T(8,128)(2,1)S(1)}, u32[]{:S(2)}, u32[]{:S(2)}) async-start(bf16[8,304,256]{2,1,0:T(8,128)(2,1)} %get-tuple-element.28), calls=%async_computation.1 | async-start | bytes 2490368 | tf_op jit(solution)/shard_map/all_to_all | solution.py:375
  74.7 34.1 %copy-start.8 = (bf16[256,256]{1,0:T(8,128)(2,1)S(1)}, bf16[256,256]{1,0:T(8,128)(2,1)}, u32[]{:S(2)}) copy-start(bf16[256,256]{1,0:T(8,128)(2,1)} %reduce-scatter.2.cloned.1.call-done.refs_9_.shared) | copy-start | bytes 393220
  74.7 74.5 %all-gather.3.cloned.1.call-start = ((), (), s32[]{:S(2)}) async-start(), calls=%async_computation.5 | async-start | bytes 2359296 | tf_op jit(solution)/shard_map/all_gather | solution.py:391
  74.7 5.0 %collective-permute-start.16 = (bf16[384,128]{1,0:T(8,128)(2,1)S(1)}, bf16[384,128]{1,0:T(8,128)(2,1)S(1)}, u32[]{:S(2)}, u32[]{:S(2)}) collective-permute-start(bf16[384,128]{1,0:T(8,128)(2,1)S(1)} %get-tuple-element.29.refs_0_), channel_id=1, source_target_pairs={{48,0},{56,8},{0,16},{8,24},{16,32},{24,40},{32,48},{40,56},{112,6... | collective-permute-start | bytes 294920 | tf_op jit(solution)/shard_map/ppermute | solution.py:321
  75.5 5.3 %collective-permute-start.15 = (bf16[384,128]{1,0:T(8,128)(2,1)S(1)}, bf16[384,128]{1,0:T(8,128)(2,1)S(1)}, u32[]{:S(2)}, u32[]{:S(2)}) collective-permute-start(bf16[384,128]{1,0:T(8,128)(2,1)S(1)} %get-tuple-element.29.refs_0_), channel_id=1, source_target_pairs={{32,0},{40,8},{48,16},{56,24},{0,32},{8,40},{16,48},{24,56},{96,64... | collective-permute-start | bytes 294920 | tf_op jit(solution)/shard_map/ppermute | solution.py:321
  77.8 3.6 %collective-permute-start.14 = (bf16[384,128]{1,0:T(8,128)(2,1)S(1)}, bf16[384,128]{1,0:T(8,128)(2,1)S(1)}, u32[]{:S(2)}, u32[]{:S(2)}) collective-permute-start(bf16[384,128]{1,0:T(8,128)(2,1)S(1)} %get-tuple-element.29.refs_0_), channel_id=1, source_target_pairs={{16,0},{24,8},{32,16},{40,24},{48,32},{56,40},{0,48},{8,56},{80,64... | collective-permute-start | bytes 294920 | tf_op jit(solution)/shard_map/ppermute | solution.py:321
  81.4 29.5 %copy-start.5 = (bf16[4,384,128]{2,1,0:T(8,128)(2,1)}, bf16[4,384,128]{2,1,0:T(8,128)(2,1)S(1)}, u32[]{:S(2)}) copy-start(bf16[4,384,128]{2,1,0:T(8,128)(2,1)S(1)} %stack_maps.1.refs_2_) | copy-start | bytes 1179652
  81.4 17.1 %collective-permute-start.20 = (bf16[4,384,128]{2,1,0:T(8,128)(2,1)S(1)}, bf16[4,384,128]{2,1,0:T(8,128)(2,1)}, u32[]{:S(2)}, u32[]{:S(2)}) collective-permute-start(bf16[4,384,128]{2,1,0:T(8,128)(2,1)S(1)} %stack_maps.1.refs_2_), channel_id=1, source_target_pairs={{128,0},{136,8},{144,16},{152,24},{160,32},{168,40},{176,48},{184,... | collective-permute-start | bytes 1179656 | tf_op jit(solution)/shard_map/ppermute | solution.py:321
  84.4 18.3 %collective-permute-start.18 = (bf16[4,384,128]{2,1,0:T(8,128)(2,1)S(1)}, bf16[4,384,128]{2,1,0:T(8,128)(2,1)}, u32[]{:S(2)}, u32[]{:S(2)}) collective-permute-start(bf16[4,384,128]{2,1,0:T(8,128)(2,1)S(1)} %stack_maps.1.refs_2_), channel_id=1, source_target_pairs={{64,0},{72,8},{80,16},{88,24},{96,32},{104,40},{112,48},{120,56},{... | collective-permute-start | bytes 1179656 | tf_op jit(solution)/shard_map/ppermute | solution.py:321
  85.6 22.5 %collective-permute-start.22 = (bf16[4,384,128]{2,1,0:T(8,128)(2,1)S(1)}, bf16[4,384,128]{2,1,0:T(8,128)(2,1)S(1)}, u32[]{:S(2)}, u32[]{:S(2)}) collective-permute-start(bf16[4,384,128]{2,1,0:T(8,128)(2,1)S(1)} %stack_maps.1.refs_2_), channel_id=1, source_target_pairs={{192,0},{200,8},{208,16},{216,24},{224,32},{232,40},{240,48},{248,... | collective-permute-start | bytes 1179656 | tf_op jit(solution)/shard_map/ppermute | solution.py:321
  85.9 22.2 %collective-permute-start.17 = (bf16[4,384,128]{2,1,0:T(8,128)(2,1)S(1)}, bf16[4,384,128]{2,1,0:T(8,128)(2,1)S(1)}, u32[]{:S(2)}, u32[]{:S(2)}) collective-permute-start(bf16[4,384,128]{2,1,0:T(8,128)(2,1)S(1)} %stack_maps.1.refs_2_), channel_id=1, source_target_pairs={{0,8},{8,0},{16,24},{24,16},{32,40},{40,32},{48,56},{56,48},{64,72... | collective-permute-start | bytes 1179656 | tf_op jit(solution)/shard_map/ppermute | solution.py:283
  98.5 9.5 %collective-permute-start.21 = (bf16[4,384,128]{2,1,0:T(8,128)(2,1)}, bf16[4,384,128]{2,1,0:T(8,128)(2,1)S(1)}, u32[]{:S(2)}, u32[]{:S(2)}) collective-permute-start(bf16[4,384,128]{2,1,0:T(8,128)(2,1)} %collective-permute-done.20.refs_4_), channel_id=1, source_target_pairs={{0,8},{8,0},{16,24},{24,16},{32,40},{40,32},{48,56},{56,48},{64,72... | collective-permute-start | bytes 1179656 | tf_op jit(solution)/shard_map/ppermute | solution.py:283
  102.6 6.2 %collective-permute-start.19 = (bf16[4,384,128]{2,1,0:T(8,128)(2,1)}, bf16[4,384,128]{2,1,0:T(8,128)(2,1)S(1)}, u32[]{:S(2)}, u32[]{:S(2)}) collective-permute-start(bf16[4,384,128]{2,1,0:T(8,128)(2,1)} %collective-permute-done.18.refs_3_), channel_id=1, source_target_pairs={{0,8},{8,0},{16,24},{24,16},{32,40},{40,32},{48,56},{56,48},{64,72... | collective-permute-start | bytes 1179656 | tf_op jit(solution)/shard_map/ppermute | solution.py:283
  108.1 8.8 %copy-start.1 = (bf16[4,384,128]{2,1,0:T(8,128)(2,1)}, bf16[4,384,128]{2,1,0:T(8,128)(2,1)S(1)}, u32[]{:S(2)}) copy-start(bf16[4,384,128]{2,1,0:T(8,128)(2,1)S(1)} %collective-permute-done.22.refs_4_.refs_5_) | copy-start | bytes 1179652
  108.1 2.8 %copy-start.2 = (bf16[4,384,128]{2,1,0:T(8,128)(2,1)}, bf16[4,384,128]{2,1,0:T(8,128)(2,1)S(1)}, u32[]{:S(2)}) copy-start(bf16[4,384,128]{2,1,0:T(8,128)(2,1)S(1)} %collective-permute-done.17.refs_1_.refs_6_) | copy-start | bytes 1179652
  108.1 2.8 %copy-start.3 = (bf16[4,384,128]{2,1,0:T(8,128)(2,1)}, bf16[4,384,128]{2,1,0:T(8,128)(2,1)S(1)}, u32[]{:S(2)}) copy-start(bf16[4,384,128]{2,1,0:T(8,128)(2,1)S(1)} %collective-permute-done.21.refs_3_.refs_8_) | copy-start | bytes 1179652
  108.8 2.1 %copy-start.4 = (bf16[4,384,128]{2,1,0:T(8,128)(2,1)}, bf16[4,384,128]{2,1,0:T(8,128)(2,1)S(1)}, u32[]{:S(2)}) copy-start(bf16[4,384,128]{2,1,0:T(8,128)(2,1)S(1)} %collective-permute-done.19.refs_2_.refs_7_) | copy-start | bytes 1179652
  110.9 14.3 %all-to-all-start.1 = ((bf16[16,48,256]{2,1,0:T(8,128)(2,1)}), bf16[16,48,256]{2,1,0:T(8,128)(2,1)S(1)}, u32[]{:S(2)}, u32[]{:S(2)}) async-start(bf16[16,48,256]{2,1,0:T(8,128)(2,1)} %sum_ends.1.refs_0_), calls=%async_computation.2 | async-start | bytes 786432 | tf_op jit(solution)/shard_map/all_to_all | solution.py:394
  116.9 32.3 %copy-start.6 = (bf16[4,2,128,128]{3,2,1,0:T(8,128)(2,1)S(1)}, bf16[4,2,128,128]{3,2,1,0:T(8,128)(2,1)}, u32[]{:S(2)}) copy-start(bf16[4,2,128,128]{3,2,1,0:T(8,128)(2,1)} %cpl.3) | copy-start | bytes 786436
  116.9 32.3 %copy-start.10 = (bf16[512,256]{1,0:T(8,128)(2,1)S(1)}, bf16[512,256]{1,0:T(8,128)(2,1)}, u32[]{:S(2)}) copy-start(bf16[512,256]{1,0:T(8,128)(2,1)} %get-tuple-element.32.fl) | copy-start | bytes 786436
  116.9 32.3 %copy-start.11 = (s32[1,8]{1,0:T(1,128)S(1)}, s32[1,8]{1,0:T(1,128)}, u32[]{:S(2)}) copy-start(s32[1,8]{1,0:T(1,128)} %owners.5) | copy-start | bytes 100
  116.9 32.3 %copy-start.12 = (s32[4,2]{0,1:T(2,128)S(1)}, s32[4,2]{0,1:T(2,128)}, u32[]{:S(2)}) copy-start(s32[4,2]{0,1:T(2,128)} %param.11) | copy-start | bytes 100
  116.9 11.0 %collective-permute-start.24 = (bf16[4,384,128]{2,1,0:T(8,128)(2,1)S(1)}, bf16[4,384,128]{2,1,0:T(8,128)(2,1)S(1)}, u32[]{:S(2)}, u32[]{:S(2)}) collective-permute-start(bf16[4,384,128]{2,1,0:T(8,128)(2,1)S(1)} %collective-permute-done.22.refs_4_.refs_5_), channel_id=1, source_target_pairs={{0,8},{8,0},{16,24},{24,16},{32,40},{40,32},{48,56},{56,48},{64,72... | collective-permute-start | bytes 1179656 | tf_op jit(solution)/shard_map/ppermute | solution.py:283
  125.3 4.0 %collective-permute-start.23 = (bf16[16,48,256]{2,1,0:T(8,128)(2,1)S(1)}, bf16[16,48,256]{2,1,0:T(8,128)(2,1)S(1)}, u32[]{:S(2)}, u32[]{:S(2)}) collective-permute-start(bf16[16,48,256]{2,1,0:T(8,128)(2,1)S(1)} %all-to-all-done.1.refs_0_), channel_id=1, source_target_pairs={{0,8},{8,0},{16,24},{24,16},{32,40},{40,32},{48,56},{56,48},{64,72... | collective-permute-start | bytes 1179656 | tf_op jit(solution)/shard_map/ppermute | solution.py:283
  141.4 15.1 %all-to-all-start.2 = ((bf16[8,32,256]{2,1,0:T(8,128)(2,1)}), bf16[8,32,256]{2,1,0:T(8,128)(2,1)S(1)}, u32[]{:S(2)}, u32[]{:S(2)}) async-start(bf16[8,32,256]{2,1,0:T(8,128)(2,1)} %chain.1), calls=%async_computation.3 | async-start | bytes 262144 | tf_op jit(solution)/shard_map/all_to_all | solution.py:413
  149.2 1.6 copy-start
  150.8 5.7 %copy-start.7 = (bf16[4,128,128]{2,1,0:T(8,128)(2,1)S(1)}, bf16[4,128,128]{2,1,0:T(8,128)(2,1)}, u32[]{:S(2)}) copy-start(bf16[4,128,128]{2,1,0:T(8,128)(2,1)} %inv.5) | copy-start | bytes 393220
  150.8 5.7 %copy-start.9 = (f32[256,256]{1,0:T(8,128)S(1)}, f32[256,256]{1,0:T(8,128)}, u32[]{:S(2)}) copy-start(f32[256,256]{1,0:T(8,128)} %get-tuple-element.30.kept) | copy-start | bytes 786436
Sparse Core Ops, SparseCore 0:
  11.4 39.8 reduce-scatter.1
  111.1 38.0 all-gather.2

commit v6 on v5

--- a/solution.py
+++ b/solution.py
@@ -369,7 +369,8 @@
     maps = call(stack_kernel, "stack_maps", held((4, 3 * b, b), BF), [VMEM] * 4, moved=1 << 18)(
         near(maps), *[near(turned_wide(maps, "x", k)) for k in (1, 2, 3)]
     )
-    maps = [maps] + [turned_wide(maps, "y", k) for k in (1, 2, 3)]
+    far, after, ahead = [turned_wide(maps, "y", k) for k in (2, 1, 3)]
+    maps = [maps, after, far, ahead]
     maps_other = [swap(part, "wide", 1) for part in maps]
 
     terms = lax.all_to_all(terms, "narrow", 0, 0, tiled=True)
@@ -387,7 +388,7 @@
         (pltpu.HBM((rows, sketch), F32), pltpu.HBM((2 * rows, sketch), BF)),
         [VMEM] * 7,
         moved=2 << 20,
-    )(terms, shared, near(ag), *[near(part) for part in maps_other[:3]], near(maps[3]))
+    )(terms, shared, near(ag), *[near(maps_other[j]) for j in (2, 0, 1)], near(maps[3]))
     gathered = lax.all_gather(packed, "narrow", axis=0, tiled=False)
 
     same_core = [[2 * q + c for q in range(chips)] for c in range(2)]
@@ -423,6 +424,7 @@
         [SMEM] * 2 + [VMEM] * 3,
         flops=2 * 16 * b * b * sketch,
         moved=4 << 20,
+        limit=56,
     )(parent, row_owner, gathered, leaf_coupling, fl)
     leaf_out, sep_out = call(
         final_kernel,

time: 165 us -> 166 us (level)
  waiting for transfers between devices: 50.2 us -> 51.9 us
  transfers between devices with their start and end apart: 30 -> 30, of which waited for: 15 -> 16; matrix products, arithmetic and copies ran while one was open for 0% -> 0% of each run, Pallas kernels for 8% -> 9%
where the time goes in v6:
time: 166 us; the launch traced here: 165 us
  starting transfers between devices  72.1 us (43%)
  waiting for transfers between devices  51.9 us (31%)
  Pallas kernels  26.7 us (16%)
  between operations  14.2 us (9%)
    ppermute x14, waiting for transfers between devices, turned(): return lax.ppermute(value, 'narrow', [(i, (i + by) % n) for i in range(n)])  34.1 us
    ppermute x5, starting transfers between devices, swap(): return lax.ppermute(value, axis, [(i, i ^ by) for i in range(n)])  24.2 us
    ppermute x14, starting transfers between devices, turned(): return lax.ppermute(value, 'narrow', [(i, (i + by) % n) for i in range(n)])  20.4 us
    pallas_call x1, Pallas kernels, per_device(): call(chain_kernel, 'chain', held((n, cols, 2 * b), BF), [VMEM] * 2 + [ANY...  12.1 us
    ppermute x6, starting transfers between devices, turned_wide(): return lax.ppermute(value, 'wide', [(source(i), i) for i in range(32)])  8.83 us
    all_to_all x1, waiting for transfers between devices, per_device(): lax.all_to_all(ag, 'wide', 0, 0, tiled=True, axis_index_groups=same_core)  7.41 us
    all_to_all x1, starting transfers between devices, per_device(): lax.all_to_all(ag, 'wide', 0, 0, tiled=True, axis_index_groups=same_core)  7.09 us
    all_to_all x1, starting transfers between devices, per_device(): z = lax.all_to_all(z, 'narrow', 0, 0, tiled=True).reshape(sketch, 2 * b)  6.88 us
  transfers between devices with their start and end apart: 30, of which 16 were waited for; matrix products, arithmetic and copies ran while one was open for 0% of the time, Pallas kernels for 9%

profile of v6, /device:TPU:1, one launch (start us, length us, event | category | flops | bytes accessed | tf_op | source)
XLA Modules:
  0.0 165.2 jit_solution(14530199143711342482)
XLA Ops:
  7.2 4.1 %leaf_forward.1 = (bf16[512,256]{1,0:T(8,128)(2,1)}, bf16[2048,256]{1,0:T(8,128)(2,1)}, bf16[288,256]{1,0:T(8,128)(2,1)S(1)}, bf16[288,256]{1,0:T(8,128)(2,1)S(1...) custom-call(s32[2,4]{1,0:T(2,128)} %bitcast.5, ...), custom_call_target="tpu_custom_call" | custom-call | flops 100663296 | bytes 4194304 | tf_op jit(solution)/shard_map/leaf_forward/pallas_call | solution.py:341
  11.3 2.5 %collective-permute-start = (bf16[288,256]{1,0:T(8,128)(2,1)S(1)}, bf16[288,256]{1,0:T(8,128)(2,1)S(1)}, u32[]{:S(2)}, u32[]{:S(2)}) collective-permute-start(bf16[288,256]{1,0:T(8,128)(2,1)S(1)} %get-tuple-element.19), channel_id=1, source_target_pairs={{0,1},{1,2},{2,3},{3,4},{4,5},{5,6},{6,7},{7,0},{8,9},{9,10},{10,1... | collective-permute-start | bytes 442376 | tf_op jit(solution)/shard_map/ppermute | solution.py:288
  13.9 4.0 %collective-permute-start.4 = (bf16[288,256]{1,0:T(8,128)(2,1)S(1)}, bf16[288,256]{1,0:T(8,128)(2,1)S(1)}, u32[]{:S(2)}, u32[]{:S(2)}) collective-permute-start(bf16[288,256]{1,0:T(8,128)(2,1)S(1)} %get-tuple-element.23), channel_id=1, source_target_pairs={{0,7},{1,0},{2,1},{3,2},{4,3},{5,4},{6,5},{7,6},{8,15},{9,8},{10,9... | collective-permute-start | bytes 442376 | tf_op jit(solution)/shard_map/ppermute | solution.py:288
  17.9 3.5 %collective-permute-done = bf16[288,256]{1,0:T(8,128)(2,1)S(1)} collective-permute-done((bf16[288,256]{1,0:T(8,128)(2,1)S(1)}, bf16[288,256]{1,0:T(8,128)(2,1)S(1)}, u32[]{:S(2)}, u32[]{:S(2)}) %collective-permute-start) | collective-permute-done | bytes 147488 | tf_op jit(solution)/shard_map/ppermute | solution.py:288
  21.4 0.1 collective-permute-start.1
  21.6 2.7 %collective-permute-start.5 = (bf16[288,256]{1,0:T(8,128)(2,1)S(1)}, bf16[288,256]{1,0:T(8,128)(2,1)S(1)}, u32[]{:S(2)}, u32[]{:S(2)}) collective-permute-start(bf16[288,256]{1,0:T(8,128)(2,1)S(1)} %add_convert_fusion.1), channel_id=1, source_target_pairs={{0,7},{1,0},{2,1},{3,2},{4,3},{5,4},{6,5},{7,6},{8,15},{9,8},{10,9... | collective-permute-start | bytes 442376 | tf_op jit(solution)/shard_map/ppermute | solution.py:288
  24.3 2.4 %collective-permute-done.1 = bf16[288,256]{1,0:T(8,128)(2,1)S(1)} collective-permute-done((bf16[288,256]{1,0:T(8,128)(2,1)S(1)}, bf16[288,256]{1,0:T(8,128)(2,1)S(1)}, u32[]{:S(2)}, u32[]{:S(2)}) %collective-permute-start.1) | collective-permute-done | bytes 147488 | tf_op jit(solution)/shard_map/ppermute | solution.py:288
  26.7 0.1 collective-permute-start.2
  26.9 2.7 %collective-permute-start.6 = (bf16[288,256]{1,0:T(8,128)(2,1)S(1)}, bf16[288,256]{1,0:T(8,128)(2,1)S(1)}, u32[]{:S(2)}, u32[]{:S(2)}) collective-permute-start(bf16[288,256]{1,0:T(8,128)(2,1)S(1)} %add_convert_fusion), channel_id=1, source_target_pairs={{0,7},{1,0},{2,1},{3,2},{4,3},{5,4},{6,5},{7,6},{8,15},{9,8},{10,9... | collective-permute-start | bytes 442376 | tf_op jit(solution)/shard_map/ppermute | solution.py:288
  29.6 4.2 %collective-permute-done.2 = bf16[288,256]{1,0:T(8,128)(2,1)S(1)} collective-permute-done((bf16[288,256]{1,0:T(8,128)(2,1)S(1)}, bf16[288,256]{1,0:T(8,128)(2,1)S(1)}, u32[]{:S(2)}, u32[]{:S(2)}) %collective-permute-start.2) | collective-permute-done | bytes 147488 | tf_op jit(solution)/shard_map/ppermute | solution.py:288
  33.8 0.1 collective-permute-start.3
  33.9 6.6 %collective-permute-done.3.right = bf16[288,256]{1,0:T(8,128)(2,1)S(1)} collective-permute-done((bf16[288,256]{1,0:T(8,128)(2,1)S(1)}, bf16[288,256]{1,0:T(8,128)(2,1)S(1)}, u32[]{:S(2)}, u32[]{:S(2)}) %collective-permute-start.3) | collective-permute-done | bytes 147488 | tf_op jit(solution)/shard_map/ppermute | solution.py:288
  40.5 0.1 sum_own.1.refs_0_
  40.6 0.1 collective-permute-start.10
  40.7 2.7 %collective-permute-start.7 = (bf16[288,256]{1,0:T(8,128)(2,1)S(1)}, bf16[288,256]{1,0:T(8,128)(2,1)S(1)}, u32[]{:S(2)}, u32[]{:S(2)}) collective-permute-start(bf16[288,256]{1,0:T(8,128)(2,1)S(1)} %sum_own.1.refs_0_), channel_id=1, source_target_pairs={{0,7},{1,0},{2,1},{3,2},{4,3},{5,4},{6,5},{7,6},{8,15},{9,8},{10,9... | collective-permute-start | bytes 442376 | tf_op jit(solution)/shard_map/ppermute | solution.py:288
  43.3 4.4 %collective-permute-done.10.refs_7_ = bf16[288,256]{1,0:T(8,128)(2,1)S(1)} collective-permute-done((bf16[288,256]{1,0:T(8,128)(2,1)S(1)}, bf16[288,256]{1,0:T(8,128)(2,1)S(1)}, u32[]{:S(2)}, u32[]{:S(2)}) %collective-permute-start.10) | collective-permute-done | bytes 147488 | tf_op jit(solution)/shard_map/ppermute | solution.py:288
  47.7 2.7 %collective-permute-start.8 = (bf16[288,256]{1,0:T(8,128)(2,1)S(1)}, bf16[288,256]{1,0:T(8,128)(2,1)S(1)}, u32[]{:S(2)}, u32[]{:S(2)}) collective-permute-start(bf16[288,256]{1,0:T(8,128)(2,1)S(1)} %collective-permute-done.7.refs_1_), channel_id=1, source_target_pairs={{0,7},{1,0},{2,1},{3,2},{4,3},{5,4},{6,5},{7,6},{8,15},{9,8},{10,9... | collective-permute-start | bytes 442376 | tf_op jit(solution)/shard_map/ppermute | solution.py:288
  50.4 3.3 %collective-permute-done.11.refs_6_ = bf16[288,256]{1,0:T(8,128)(2,1)S(1)} collective-permute-done((bf16[288,256]{1,0:T(8,128)(2,1)S(1)}, bf16[288,256]{1,0:T(8,128)(2,1)S(1)}, u32[]{:S(2)}, u32[]{:S(2)}) %collective-permute-start.11) | collective-permute-done | bytes 147488 | tf_op jit(solution)/shard_map/ppermute | solution.py:288
  53.7 2.7 %collective-permute-start.9 = (bf16[288,256]{1,0:T(8,128)(2,1)S(1)}, bf16[288,256]{1,0:T(8,128)(2,1)S(1)}, u32[]{:S(2)}, u32[]{:S(2)}) collective-permute-start(bf16[288,256]{1,0:T(8,128)(2,1)S(1)} %collective-permute-done.8.refs_2_), channel_id=1, source_target_pairs={{0,7},{1,0},{2,1},{3,2},{4,3},{5,4},{6,5},{7,6},{8,15},{9,8},{10,9... | collective-permute-start | bytes 442376 | tf_op jit(solution)/shard_map/ppermute | solution.py:288
  56.4 2.9 %collective-permute-done.12.refs_5_ = bf16[288,256]{1,0:T(8,128)(2,1)S(1)} collective-permute-done((bf16[288,256]{1,0:T(8,128)(2,1)S(1)}, bf16[288,256]{1,0:T(8,128)(2,1)S(1)}, u32[]{:S(2)}, u32[]{:S(2)}) %collective-permute-start.12) | collective-permute-done | bytes 147488 | tf_op jit(solution)/shard_map/ppermute | solution.py:288
  59.3 6.9 %collective-permute-done.13.refs_4_ = bf16[288,256]{1,0:T(8,128)(2,1)S(1)} collective-permute-done((bf16[288,256]{1,0:T(8,128)(2,1)S(1)}, bf16[288,256]{1,0:T(8,128)(2,1)S(1)}, u32[]{:S(2)}, u32[]{:S(2)}) %collective-permute-start.13) | collective-permute-done | bytes 147488 | tf_op jit(solution)/shard_map/ppermute | solution.py:288
  66.1 3.9 %middle.1 = (bf16[8,304,256]{2,1,0:T(8,128)(2,1)}, bf16[384,128]{1,0:T(8,128)(2,1)S(1)}) custom-call(s32[1,8]{1,0:T(1,128)} %owners.5, bf16[256,2048]{1,0:T(8,128)(2,1)} %inv.4, bf16[288,256]{1,0:T(8,128)(2,1)S(1)} %sum_own.1.refs_0_, bf16[288,256]{1,0:T(8,128)(2,1)S(1)} %collective-permute-done.7.refs_1_, ...), custom_call_target="tpu_custom_call" | custom-call | flops 536870912 | bytes 4194304 | tf_op jit(solution)/shard_map/middle/pallas_call | solution.py:359
  70.0 4.7 %all-to-all-start = ((bf16[8,304,256]{2,1,0:T(8,128)(2,1)}), bf16[8,304,256]{2,1,0:T(8,128)(2,1)S(1)}, u32[]{:S(2)}, u32[]{:S(2)}) async-start(bf16[8,304,256]{2,1,0:T(8,128)(2,1)} %get-tuple-element.28), calls=%async_computation.1 | async-start | bytes 2490368 | tf_op jit(solution)/shard_map/all_to_all | solution.py:376
  74.7 0.7 collective-permute-start.16
  75.5 2.3 %collective-permute-start.15 = (bf16[384,128]{1,0:T(8,128)(2,1)S(1)}, bf16[384,128]{1,0:T(8,128)(2,1)S(1)}, u32[]{:S(2)}, u32[]{:S(2)}) collective-permute-start(bf16[384,128]{1,0:T(8,128)(2,1)S(1)} %get-tuple-element.29.refs_0_), channel_id=1, source_target_pairs={{32,0},{40,8},{48,16},{56,24},{0,32},{8,40},{16,48},{24,56},{96,64... | collective-permute-start | bytes 294920 | tf_op jit(solution)/shard_map/ppermute | solution.py:321
  77.8 2.0 %collective-permute-start.14 = (bf16[384,128]{1,0:T(8,128)(2,1)S(1)}, bf16[384,128]{1,0:T(8,128)(2,1)S(1)}, u32[]{:S(2)}, u32[]{:S(2)}) collective-permute-start(bf16[384,128]{1,0:T(8,128)(2,1)S(1)} %get-tuple-element.29.refs_0_), channel_id=1, source_target_pairs={{16,0},{24,8},{32,16},{40,24},{48,32},{56,40},{0,48},{8,56},{80,64... | collective-permute-start | bytes 294920 | tf_op jit(solution)/shard_map/ppermute | solution.py:321
  79.7 1.0 collective-permute-done.15.refs_2_
  80.7 0.7 collective-permute-done.14.refs_1_
  81.4 2.6 %collective-permute-start.20 = (bf16[4,384,128]{2,1,0:T(8,128)(2,1)S(1)}, bf16[4,384,128]{2,1,0:T(8,128)(2,1)}, u32[]{:S(2)}, u32[]{:S(2)}) collective-permute-start(bf16[4,384,128]{2,1,0:T(8,128)(2,1)S(1)} %stack_maps.1.refs_2_), channel_id=1, source_target_pairs={{64,0},{72,8},{80,16},{88,24},{96,32},{104,40},{112,48},{120,56},{... | collective-permute-start | bytes 1179656 | tf_op jit(solution)/shard_map/ppermute | solution.py:321
  84.0 1.0 collective-permute-start.17
  85.0 0.3 collective-permute-start.22
  85.3 12.7 %collective-permute-start.19 = (bf16[4,384,128]{2,1,0:T(8,128)(2,1)S(1)}, bf16[4,384,128]{2,1,0:T(8,128)(2,1)S(1)}, u32[]{:S(2)}, u32[]{:S(2)}) collective-permute-start(bf16[4,384,128]{2,1,0:T(8,128)(2,1)S(1)} %stack_maps.1.refs_2_), channel_id=1, source_target_pairs={{0,8},{8,0},{16,24},{24,16},{32,40},{40,32},{48,56},{56,48},{64,72... | collective-permute-start | bytes 1179656 | tf_op jit(solution)/shard_map/ppermute | solution.py:283
  97.9 7.9 %collective-permute-start.21 = (bf16[4,384,128]{2,1,0:T(8,128)(2,1)}, bf16[4,384,128]{2,1,0:T(8,128)(2,1)S(1)}, u32[]{:S(2)}, u32[]{:S(2)}) collective-permute-start(bf16[4,384,128]{2,1,0:T(8,128)(2,1)} %collective-permute-done.20.refs_3_), channel_id=1, source_target_pairs={{0,8},{8,0},{16,24},{24,16},{32,40},{40,32},{48,56},{56,48},{64,72... | collective-permute-start | bytes 1179656 | tf_op jit(solution)/shard_map/ppermute | solution.py:283
  105.8 0.8 sum_ends.1.refs_0_
  106.6 0.7 collective-permute-done.21.refs_3_.refs_7_
  107.4 0.6 collective-permute-done.18.refs_1_.refs_8_
  107.9 2.1 %sum_terms.1 = (f32[256,256]{1,0:T(8,128)}, bf16[512,256]{1,0:T(8,128)(2,1)}) custom-call(bf16[8,304,256]{2,1,0:T(8,128)(2,1)S(1)} %all-to-all-done.parts, bf16[256,256]{1,0:T(8,128)(2,1)S(1)} %copy-done.6, bf16[16,48,256]{2,1,0:T(8,128)(2,1)} %sum_ends.1.refs_0_, bf16[4,384,128]{2,1,0:T(8,128)(2,1)S(1)} %collective-permute-done.18.refs_1_.refs_8_, ...), custom_call_target="tpu_custom_call" | custom-call | bytes 2097152 | tf_op jit(solution)/shard_map/sum_terms/pallas_call | solution.py:385
  110.0 7.1 %all-to-all-start.1 = ((bf16[16,48,256]{2,1,0:T(8,128)(2,1)}), bf16[16,48,256]{2,1,0:T(8,128)(2,1)S(1)}, u32[]{:S(2)}, u32[]{:S(2)}) async-start(bf16[16,48,256]{2,1,0:T(8,128)(2,1)} %sum_ends.1.refs_0_), calls=%async_computation.2 | async-start | bytes 786432 | tf_op jit(solution)/shard_map/all_to_all | solution.py:395
  117.2 1.4 collective-permute-start.24
  118.5 7.4 %all-to-all-done.1.refs_0_ = bf16[16,48,256]{2,1,0:T(8,128)(2,1)S(1)} async-done(((bf16[16,48,256]{2,1,0:T(8,128)(2,1)}), bf16[16,48,256]{2,1,0:T(8,128)(2,1)S(1)}, u32[]{:S(2)}, u32[]{:S(2)}) %all-to-all-start.1) | async-done | bytes 393248 | tf_op jit(solution)/shard_map/all_to_all | solution.py:395
  126.0 2.2 %collective-permute-start.23 = (bf16[16,48,256]{2,1,0:T(8,128)(2,1)S(1)}, bf16[16,48,256]{2,1,0:T(8,128)(2,1)S(1)}, u32[]{:S(2)}, u32[]{:S(2)}) collective-permute-start(bf16[16,48,256]{2,1,0:T(8,128)(2,1)S(1)} %all-to-all-done.1.refs_0_), channel_id=1, source_target_pairs={{0,8},{8,0},{16,24},{24,16},{32,40},{40,32},{48,56},{56,48},{64,72... | collective-permute-start | bytes 1179656 | tf_op jit(solution)/shard_map/ppermute | solution.py:283
  128.2 1.3 collective-permute-done.23.refs_1_
  129.5 12.1 %chain.1 = bf16[8,32,256]{2,1,0:T(8,128)(2,1)} custom-call(bf16[16,48,256]{2,1,0:T(8,128)(2,1)S(1)} %all-to-all-done.1.refs_0_, bf16[16,48,256]{2,1,0:T(8,128)(2,1)S(1)} %collective-permute-done.23.refs_1_, bf16[4,384,128]{2,1,0:T(8,128)(2,1)} %copy-done.4, bf16[4,384,128]{2,1,0:T(8,128)(2,1)} %collective-permute-done.20.refs_3_, ...), custom_call_target="tpu_custom_call" | custom-call | flops 301989888 | bytes 8388608 | tf_op jit(solution)/shard_map/chain/pallas_call | solution.py:398
  141.6 6.9 %all-to-all-start.2 = ((bf16[8,32,256]{2,1,0:T(8,128)(2,1)}), bf16[8,32,256]{2,1,0:T(8,128)(2,1)S(1)}, u32[]{:S(2)}, u32[]{:S(2)}) async-start(bf16[8,32,256]{2,1,0:T(8,128)(2,1)} %chain.1), calls=%async_computation.3 | async-start | bytes 262144 | tf_op jit(solution)/shard_map/all_to_all | solution.py:414
  148.5 0.9 all-gather.3.cloned.1.call-done
  149.4 2.2 %before.1 = (f32[512,256]{1,0:T(8,128)S(1)}, bf16[512,256]{1,0:T(8,128)(2,1)S(1)}, bf16[256,256]{1,0:T(8,128)(2,1)S(1)}) custom-call(s32[2,4]{1,0:T(2,128)} %bitcast.6, s32[1,8]{1,0:T(1,128)} %owners.5, bf16[8,512,256]{2,1,0:T(8,128)(2,1)} %bitcast.4, bf16[4,2,128,128]{3,2,1,0:T(8,128)(2,1)} %cpl.3, bf16[512,256]{1,0:T(8,128)(2,1)} %get-tuple-element.32.fl), custom_call_target="tpu_custom_call" | custom-call | flops 134217728 | bytes 4194304 | tf_op jit(solution)/shard_map/before/pallas_call | solution.py:416
  151.6 5.1 %all-to-all-done.2 = bf16[8,32,256]{2,1,0:T(8,128)(2,1)S(1)} async-done(((bf16[8,32,256]{2,1,0:T(8,128)(2,1)}), bf16[8,32,256]{2,1,0:T(8,128)(2,1)S(1)}, u32[]{:S(2)}, u32[]{:S(2)}) %all-to-all-start.2) | async-done | bytes 131104 | tf_op jit(solution)/shard_map/all_to_all | solution.py:414
  156.8 1.5 final.1
  (44 shorter events, 0.4 us)
Async XLA Ops:
  7.2 59.0 %reduce-scatter.2.cloned.1.call-start = ((), (), s32[]{:S(2)}) async-start(), calls=%async_computation.4 | async-start | bytes 1179648 | tf_op jit(solution)/shard_map/reduce_scatter | solution.py:358
  11.3 10.1 %collective-permute-start = (bf16[288,256]{1,0:T(8,128)(2,1)S(1)}, bf16[288,256]{1,0:T(8,128)(2,1)S(1)}, u32[]{:S(2)}, u32[]{:S(2)}) collective-permute-start(bf16[288,256]{1,0:T(8,128)(2,1)S(1)} %get-tuple-element.19), channel_id=1, source_target_pairs={{0,1},{1,2},{2,3},{3,4},{4,5},{5,6},{6,7},{7,0},{8,9},{9,10},{10,1... | collective-permute-start | bytes 442376 | tf_op jit(solution)/shard_map/ppermute | solution.py:288
  13.9 7.6 %collective-permute-start.4 = (bf16[288,256]{1,0:T(8,128)(2,1)S(1)}, bf16[288,256]{1,0:T(8,128)(2,1)S(1)}, u32[]{:S(2)}, u32[]{:S(2)}) collective-permute-start(bf16[288,256]{1,0:T(8,128)(2,1)S(1)} %get-tuple-element.23), channel_id=1, source_target_pairs={{0,7},{1,0},{2,1},{3,2},{4,3},{5,4},{6,5},{7,6},{8,15},{9,8},{10,9... | collective-permute-start | bytes 442376 | tf_op jit(solution)/shard_map/ppermute | solution.py:288
  21.4 5.3 %collective-permute-start.1 = (bf16[288,256]{1,0:T(8,128)(2,1)S(1)}, bf16[288,256]{1,0:T(8,128)(2,1)S(1)}, u32[]{:S(2)}, u32[]{:S(2)}) collective-permute-start(bf16[288,256]{1,0:T(8,128)(2,1)S(1)} %add_convert_fusion.4), channel_id=1, source_target_pairs={{0,1},{1,2},{2,3},{3,4},{4,5},{5,6},{6,7},{7,0},{8,9},{9,10},{10,1... | collective-permute-start | bytes 442376 | tf_op jit(solution)/shard_map/ppermute | solution.py:288
  21.6 5.3 %collective-permute-start.5 = (bf16[288,256]{1,0:T(8,128)(2,1)S(1)}, bf16[288,256]{1,0:T(8,128)(2,1)S(1)}, u32[]{:S(2)}, u32[]{:S(2)}) collective-permute-start(bf16[288,256]{1,0:T(8,128)(2,1)S(1)} %add_convert_fusion.1), channel_id=1, source_target_pairs={{0,7},{1,0},{2,1},{3,2},{4,3},{5,4},{6,5},{7,6},{8,15},{9,8},{10,9... | collective-permute-start | bytes 442376 | tf_op jit(solution)/shard_map/ppermute | solution.py:288
  26.7 7.0 %collective-permute-start.2 = (bf16[288,256]{1,0:T(8,128)(2,1)S(1)}, bf16[288,256]{1,0:T(8,128)(2,1)S(1)}, u32[]{:S(2)}, u32[]{:S(2)}) collective-permute-start(bf16[288,256]{1,0:T(8,128)(2,1)S(1)} %add_convert_fusion.3), channel_id=1, source_target_pairs={{0,1},{1,2},{2,3},{3,4},{4,5},{5,6},{6,7},{7,0},{8,9},{9,10},{10,1... | collective-permute-start | bytes 442376 | tf_op jit(solution)/shard_map/ppermute | solution.py:288
  26.9 7.0 %collective-permute-start.6 = (bf16[288,256]{1,0:T(8,128)(2,1)S(1)}, bf16[288,256]{1,0:T(8,128)(2,1)S(1)}, u32[]{:S(2)}, u32[]{:S(2)}) collective-permute-start(bf16[288,256]{1,0:T(8,128)(2,1)S(1)} %add_convert_fusion), channel_id=1, source_target_pairs={{0,7},{1,0},{2,1},{3,2},{4,3},{5,4},{6,5},{7,6},{8,15},{9,8},{10,9... | collective-permute-start | bytes 442376 | tf_op jit(solution)/shard_map/ppermute | solution.py:288
  33.8 6.7 %collective-permute-start.3 = (bf16[288,256]{1,0:T(8,128)(2,1)S(1)}, bf16[288,256]{1,0:T(8,128)(2,1)S(1)}, u32[]{:S(2)}, u32[]{:S(2)}) collective-permute-start(bf16[288,256]{1,0:T(8,128)(2,1)S(1)} %add_convert_fusion.2), channel_id=1, source_target_pairs={{0,1},{1,2},{2,3},{3,4},{4,5},{5,6},{6,7},{7,0},{8,9},{9,10},{10,1... | collective-permute-start | bytes 442376 | tf_op jit(solution)/shard_map/ppermute | solution.py:288
  40.6 7.2 %collective-permute-start.10 = (bf16[288,256]{1,0:T(8,128)(2,1)S(1)}, bf16[288,256]{1,0:T(8,128)(2,1)S(1)}, u32[]{:S(2)}, u32[]{:S(2)}) collective-permute-start(bf16[288,256]{1,0:T(8,128)(2,1)S(1)} %sum_own.1.refs_0_), channel_id=1, source_target_pairs={{0,1},{1,2},{2,3},{3,4},{4,5},{5,6},{6,7},{7,0},{8,9},{9,10},{10,1... | collective-permute-start | bytes 442376 | tf_op jit(solution)/shard_map/ppermute | solution.py:288
  40.7 7.1 %collective-permute-start.7 = (bf16[288,256]{1,0:T(8,128)(2,1)S(1)}, bf16[288,256]{1,0:T(8,128)(2,1)S(1)}, u32[]{:S(2)}, u32[]{:S(2)}) collective-permute-start(bf16[288,256]{1,0:T(8,128)(2,1)S(1)} %sum_own.1.refs_0_), channel_id=1, source_target_pairs={{0,7},{1,0},{2,1},{3,2},{4,3},{5,4},{6,5},{7,6},{8,15},{9,8},{10,9... | collective-permute-start | bytes 442376 | tf_op jit(solution)/shard_map/ppermute | solution.py:288
  47.7 6.0 %collective-permute-start.11 = (bf16[288,256]{1,0:T(8,128)(2,1)S(1)}, bf16[288,256]{1,0:T(8,128)(2,1)S(1)}, u32[]{:S(2)}, u32[]{:S(2)}) collective-permute-start(bf16[288,256]{1,0:T(8,128)(2,1)S(1)} %collective-permute-done.10.refs_7_), channel_id=1, source_target_pairs={{0,1},{1,2},{2,3},{3,4},{4,5},{5,6},{6,7},{7,0},{8,9},{9,10},{10,1... | collective-permute-start | bytes 442376 | tf_op jit(solution)/shard_map/ppermute | solution.py:288
  47.7 6.0 %collective-permute-start.8 = (bf16[288,256]{1,0:T(8,128)(2,1)S(1)}, bf16[288,256]{1,0:T(8,128)(2,1)S(1)}, u32[]{:S(2)}, u32[]{:S(2)}) collective-permute-start(bf16[288,256]{1,0:T(8,128)(2,1)S(1)} %collective-permute-done.7.refs_1_), channel_id=1, source_target_pairs={{0,7},{1,0},{2,1},{3,2},{4,3},{5,4},{6,5},{7,6},{8,15},{9,8},{10,9... | collective-permute-start | bytes 442376 | tf_op jit(solution)/shard_map/ppermute | solution.py:288
  53.7 5.6 %collective-permute-start.12 = (bf16[288,256]{1,0:T(8,128)(2,1)S(1)}, bf16[288,256]{1,0:T(8,128)(2,1)S(1)}, u32[]{:S(2)}, u32[]{:S(2)}) collective-permute-start(bf16[288,256]{1,0:T(8,128)(2,1)S(1)} %collective-permute-done.11.refs_6_), channel_id=1, source_target_pairs={{0,1},{1,2},{2,3},{3,4},{4,5},{5,6},{6,7},{7,0},{8,9},{9,10},{10,1... | collective-permute-start | bytes 442376 | tf_op jit(solution)/shard_map/ppermute | solution.py:288
  53.7 5.6 %collective-permute-start.9 = (bf16[288,256]{1,0:T(8,128)(2,1)S(1)}, bf16[288,256]{1,0:T(8,128)(2,1)S(1)}, u32[]{:S(2)}, u32[]{:S(2)}) collective-permute-start(bf16[288,256]{1,0:T(8,128)(2,1)S(1)} %collective-permute-done.8.refs_2_), channel_id=1, source_target_pairs={{0,7},{1,0},{2,1},{3,2},{4,3},{5,4},{6,5},{7,6},{8,15},{9,8},{10,9... | collective-permute-start | bytes 442376 | tf_op jit(solution)/shard_map/ppermute | solution.py:288
  59.3 6.9 %collective-permute-start.13 = (bf16[288,256]{1,0:T(8,128)(2,1)S(1)}, bf16[288,256]{1,0:T(8,128)(2,1)S(1)}, u32[]{:S(2)}, u32[]{:S(2)}) collective-permute-start(bf16[288,256]{1,0:T(8,128)(2,1)S(1)} %collective-permute-done.12.refs_5_), channel_id=1, source_target_pairs={{0,1},{1,2},{2,3},{3,4},{4,5},{5,6},{6,7},{7,0},{8,9},{9,10},{10,1... | collective-permute-start | bytes 442376 | tf_op jit(solution)/shard_map/ppermute | solution.py:288
  70.0 35.8 %all-to-all-start = ((bf16[8,304,256]{2,1,0:T(8,128)(2,1)}), bf16[8,304,256]{2,1,0:T(8,128)(2,1)S(1)}, u32[]{:S(2)}, u32[]{:S(2)}) async-start(bf16[8,304,256]{2,1,0:T(8,128)(2,1)} %get-tuple-element.28), calls=%async_computation.1 | async-start | bytes 2490368 | tf_op jit(solution)/shard_map/all_to_all | solution.py:376
  74.7 33.2 %copy-start.6 = (bf16[256,256]{1,0:T(8,128)(2,1)S(1)}, bf16[256,256]{1,0:T(8,128)(2,1)}, u32[]{:S(2)}) copy-start(bf16[256,256]{1,0:T(8,128)(2,1)} %reduce-scatter.2.cloned.1.call-done.refs_9_.shared) | copy-start | bytes 393220
  74.7 74.7 %all-gather.3.cloned.1.call-start = ((), (), s32[]{:S(2)}) async-start(), calls=%async_computation.5 | async-start | bytes 2359296 | tf_op jit(solution)/shard_map/all_gather | solution.py:392
  74.7 5.0 %collective-permute-start.16 = (bf16[384,128]{1,0:T(8,128)(2,1)S(1)}, bf16[384,128]{1,0:T(8,128)(2,1)S(1)}, u32[]{:S(2)}, u32[]{:S(2)}) collective-permute-start(bf16[384,128]{1,0:T(8,128)(2,1)S(1)} %get-tuple-element.29.refs_0_), channel_id=1, source_target_pairs={{48,0},{56,8},{0,16},{8,24},{16,32},{24,40},{32,48},{40,56},{112,6... | collective-permute-start | bytes 294920 | tf_op jit(solution)/shard_map/ppermute | solution.py:321
  75.5 5.3 %collective-permute-start.15 = (bf16[384,128]{1,0:T(8,128)(2,1)S(1)}, bf16[384,128]{1,0:T(8,128)(2,1)S(1)}, u32[]{:S(2)}, u32[]{:S(2)}) collective-permute-start(bf16[384,128]{1,0:T(8,128)(2,1)S(1)} %get-tuple-element.29.refs_0_), channel_id=1, source_target_pairs={{32,0},{40,8},{48,16},{56,24},{0,32},{8,40},{16,48},{24,56},{96,64... | collective-permute-start | bytes 294920 | tf_op jit(solution)/shard_map/ppermute | solution.py:321
  77.8 3.6 %collective-permute-start.14 = (bf16[384,128]{1,0:T(8,128)(2,1)S(1)}, bf16[384,128]{1,0:T(8,128)(2,1)S(1)}, u32[]{:S(2)}, u32[]{:S(2)}) collective-permute-start(bf16[384,128]{1,0:T(8,128)(2,1)S(1)} %get-tuple-element.29.refs_0_), channel_id=1, source_target_pairs={{16,0},{24,8},{32,16},{40,24},{48,32},{56,40},{0,48},{8,56},{80,64... | collective-permute-start | bytes 294920 | tf_op jit(solution)/shard_map/ppermute | solution.py:321
  81.4 28.6 %copy-start.4 = (bf16[4,384,128]{2,1,0:T(8,128)(2,1)}, bf16[4,384,128]{2,1,0:T(8,128)(2,1)S(1)}, u32[]{:S(2)}) copy-start(bf16[4,384,128]{2,1,0:T(8,128)(2,1)S(1)} %stack_maps.1.refs_2_) | copy-start | bytes 1179652
  81.4 16.5 %collective-permute-start.20 = (bf16[4,384,128]{2,1,0:T(8,128)(2,1)S(1)}, bf16[4,384,128]{2,1,0:T(8,128)(2,1)}, u32[]{:S(2)}, u32[]{:S(2)}) collective-permute-start(bf16[4,384,128]{2,1,0:T(8,128)(2,1)S(1)} %stack_maps.1.refs_2_), channel_id=1, source_target_pairs={{64,0},{72,8},{80,16},{88,24},{96,32},{104,40},{112,48},{120,56},{... | collective-permute-start | bytes 1179656 | tf_op jit(solution)/shard_map/ppermute | solution.py:321
  84.0 21.8 %collective-permute-start.17 = (bf16[4,384,128]{2,1,0:T(8,128)(2,1)S(1)}, bf16[4,384,128]{2,1,0:T(8,128)(2,1)}, u32[]{:S(2)}, u32[]{:S(2)}) collective-permute-start(bf16[4,384,128]{2,1,0:T(8,128)(2,1)S(1)} %stack_maps.1.refs_2_), channel_id=1, source_target_pairs={{128,0},{136,8},{144,16},{152,24},{160,32},{168,40},{176,48},{184,... | collective-permute-start | bytes 1179656 | tf_op jit(solution)/shard_map/ppermute | solution.py:321
  85.0 21.6 %collective-permute-start.22 = (bf16[4,384,128]{2,1,0:T(8,128)(2,1)S(1)}, bf16[4,384,128]{2,1,0:T(8,128)(2,1)S(1)}, u32[]{:S(2)}, u32[]{:S(2)}) collective-permute-start(bf16[4,384,128]{2,1,0:T(8,128)(2,1)S(1)} %stack_maps.1.refs_2_), channel_id=1, source_target_pairs={{192,0},{200,8},{208,16},{216,24},{224,32},{232,40},{240,48},{248,... | collective-permute-start | bytes 1179656 | tf_op jit(solution)/shard_map/ppermute | solution.py:321
  85.3 21.4 %collective-permute-start.19 = (bf16[4,384,128]{2,1,0:T(8,128)(2,1)S(1)}, bf16[4,384,128]{2,1,0:T(8,128)(2,1)S(1)}, u32[]{:S(2)}, u32[]{:S(2)}) collective-permute-start(bf16[4,384,128]{2,1,0:T(8,128)(2,1)S(1)} %stack_maps.1.refs_2_), channel_id=1, source_target_pairs={{0,8},{8,0},{16,24},{24,16},{32,40},{40,32},{48,56},{56,48},{64,72... | collective-permute-start | bytes 1179656 | tf_op jit(solution)/shard_map/ppermute | solution.py:283
  97.9 9.4 %collective-permute-start.21 = (bf16[4,384,128]{2,1,0:T(8,128)(2,1)}, bf16[4,384,128]{2,1,0:T(8,128)(2,1)S(1)}, u32[]{:S(2)}, u32[]{:S(2)}) collective-permute-start(bf16[4,384,128]{2,1,0:T(8,128)(2,1)} %collective-permute-done.20.refs_3_), channel_id=1, source_target_pairs={{0,8},{8,0},{16,24},{24,16},{32,40},{40,32},{48,56},{56,48},{64,72... | collective-permute-start | bytes 1179656 | tf_op jit(solution)/shard_map/ppermute | solution.py:283
  105.8 2.1 %collective-permute-start.18 = (bf16[4,384,128]{2,1,0:T(8,128)(2,1)}, bf16[4,384,128]{2,1,0:T(8,128)(2,1)S(1)}, u32[]{:S(2)}, u32[]{:S(2)}) collective-permute-start(bf16[4,384,128]{2,1,0:T(8,128)(2,1)} %collective-permute-done.17.refs_4_), channel_id=1, source_target_pairs={{0,8},{8,0},{16,24},{24,16},{32,40},{40,32},{48,56},{56,48},{64,72... | collective-permute-start | bytes 1179656 | tf_op jit(solution)/shard_map/ppermute | solution.py:283
  106.6 10.5 %copy-start = (bf16[4,384,128]{2,1,0:T(8,128)(2,1)}, bf16[4,384,128]{2,1,0:T(8,128)(2,1)S(1)}, u32[]{:S(2)}) copy-start(bf16[4,384,128]{2,1,0:T(8,128)(2,1)S(1)} %collective-permute-done.22.refs_4_.refs_5_) | copy-start | bytes 1179652
  106.6 3.4 %copy-start.1 = (bf16[4,384,128]{2,1,0:T(8,128)(2,1)}, bf16[4,384,128]{2,1,0:T(8,128)(2,1)S(1)}, u32[]{:S(2)}) copy-start(bf16[4,384,128]{2,1,0:T(8,128)(2,1)S(1)} %collective-permute-done.19.refs_2_.refs_6_) | copy-start | bytes 1179652
  107.4 2.6 %copy-start.2 = (bf16[4,384,128]{2,1,0:T(8,128)(2,1)}, bf16[4,384,128]{2,1,0:T(8,128)(2,1)S(1)}, u32[]{:S(2)}) copy-start(bf16[4,384,128]{2,1,0:T(8,128)(2,1)S(1)} %collective-permute-done.21.refs_3_.refs_7_) | copy-start | bytes 1179652
  107.9 2.1 %copy-start.3 = (bf16[4,384,128]{2,1,0:T(8,128)(2,1)}, bf16[4,384,128]{2,1,0:T(8,128)(2,1)S(1)}, u32[]{:S(2)}) copy-start(bf16[4,384,128]{2,1,0:T(8,128)(2,1)S(1)} %collective-permute-done.18.refs_1_.refs_8_) | copy-start | bytes 1179652
  110.0 15.9 %all-to-all-start.1 = ((bf16[16,48,256]{2,1,0:T(8,128)(2,1)}), bf16[16,48,256]{2,1,0:T(8,128)(2,1)S(1)}, u32[]{:S(2)}, u32[]{:S(2)}) async-start(bf16[16,48,256]{2,1,0:T(8,128)(2,1)} %sum_ends.1.refs_0_), calls=%async_computation.2 | async-start | bytes 786432 | tf_op jit(solution)/shard_map/all_to_all | solution.py:395
  117.2 11.0 %collective-permute-start.24 = (bf16[4,384,128]{2,1,0:T(8,128)(2,1)S(1)}, bf16[4,384,128]{2,1,0:T(8,128)(2,1)S(1)}, u32[]{:S(2)}, u32[]{:S(2)}) collective-permute-start(bf16[4,384,128]{2,1,0:T(8,128)(2,1)S(1)} %collective-permute-done.22.refs_4_.refs_5_), channel_id=1, source_target_pairs={{0,8},{8,0},{16,24},{24,16},{32,40},{40,32},{48,56},{56,48},{64,72... | collective-permute-start | bytes 1179656 | tf_op jit(solution)/shard_map/ppermute | solution.py:283
  126.0 3.6 %collective-permute-start.23 = (bf16[16,48,256]{2,1,0:T(8,128)(2,1)S(1)}, bf16[16,48,256]{2,1,0:T(8,128)(2,1)S(1)}, u32[]{:S(2)}, u32[]{:S(2)}) collective-permute-start(bf16[16,48,256]{2,1,0:T(8,128)(2,1)S(1)} %all-to-all-done.1.refs_0_), channel_id=1, source_target_pairs={{0,8},{8,0},{16,24},{24,16},{32,40},{40,32},{48,56},{56,48},{64,72... | collective-permute-start | bytes 1179656 | tf_op jit(solution)/shard_map/ppermute | solution.py:283
  141.6 15.2 %all-to-all-start.2 = ((bf16[8,32,256]{2,1,0:T(8,128)(2,1)}), bf16[8,32,256]{2,1,0:T(8,128)(2,1)S(1)}, u32[]{:S(2)}, u32[]{:S(2)}) async-start(bf16[8,32,256]{2,1,0:T(8,128)(2,1)} %chain.1), calls=%async_computation.3 | async-start | bytes 262144 | tf_op jit(solution)/shard_map/all_to_all | solution.py:414
  149.4 7.3 %copy-start.5 = (bf16[4,128,128]{2,1,0:T(8,128)(2,1)S(1)}, bf16[4,128,128]{2,1,0:T(8,128)(2,1)}, u32[]{:S(2)}) copy-start(bf16[4,128,128]{2,1,0:T(8,128)(2,1)} %inv.5) | copy-start | bytes 393220
  149.4 7.3 %copy-start.7 = (f32[256,256]{1,0:T(8,128)S(1)}, f32[256,256]{1,0:T(8,128)}, u32[]{:S(2)}) copy-start(f32[256,256]{1,0:T(8,128)} %get-tuple-element.30.kept) | copy-start | bytes 786436
Sparse Core Ops, SparseCore 0:
  11.4 39.8 reduce-scatter.1
  110.2 39.2 all-gather.2
